TPU v7x, 32 devices: a whole 2x2x4 slice. The times are simulated.
32 devices in a mesh: groups: 2 (over y), rowblk: 4 (over x, core), colblk: 4 (over z).
Axes of the slice: x: 2, y: 2, z: 4, core: 2. Of those that a mesh axis runs over, the one named last changes fastest.
Arguments:
- tiles: bfloat16 [3072, 128, 128], P(('groups', 'rowblk', 'colblk')), parts along dimension 0, may hold values from -0.1875 to 0.1875
- tile_row: int32 [3072], P(('groups', 'rowblk', 'colblk')), parts along dimension 0, may hold values from 0 to 31, as said below
- tile_col: int32 [3072], P(('groups', 'rowblk', 'colblk')), parts along dimension 0, may hold values from 0 to 63
- tile_count: int32 [32], P(('groups', 'rowblk', 'colblk')), parts along dimension 0, may hold values from 12 to 96, as said below
- cost: float32 [65536], P(('groups', 'colblk')), parts along dimension 0, may hold values from -12 to 12
- demand: float32 [8, 32768], P(None, ('groups', 'rowblk')), parts along dimension 1, may hold values from -12 to 12
- upper: float32 [65536], P(('groups', 'colblk')), parts along dimension 0, may hold values from 0.5 to 2
- col_flag: int32 [65536], P(('groups', 'colblk')), parts along dimension 0, may hold values 0 or 1
- row_flag: int32 [32768], P(('groups', 'rowblk')), parts along dimension 0, may hold values 0 or 1
- primal_start: float32 [8, 65536], P(None, ('groups', 'colblk')), parts along dimension 1, may hold values from 0 to 1
- dual_start: float32 [8, 32768], P(None, ('groups', 'rowblk')), parts along dimension 1, may hold values from -3 to 3
Outputs:
- primal_point: float32 [8, 65536], P(None, ('groups', 'colblk')), parts along dimension 1
- dual_point: float32 [8, 32768], P(None, ('groups', 'rowblk')), parts along dimension 1
- primal_weight: float32 [16], P('groups'), parts along dimension 0
There are 2 independent parts, one for each index of `groups`. A program takes and returns all parts, laid end to end along the dimension named above; each array names one. Nothing has to cross between parts.
Inputs may be any that keep to these rules, and one draw needn't show every extreme that they name: On one device the pairs (tile_row, tile_col) of its 96 slots are all different. `tile_count`: in every draw one device has all 96 slots live.
All inputs are finite; a program needn't handle non-finite values. No bound on the sum of `col_flag` or of `row_flag` on one device may be relied on, other than what follows from the above.
Results may differ from a plain program's by a relative error of at most 0.0012.
Values may be sent and summed in bfloat16 or wider, within the bound.
No kernel may reach another device: no remote copies, remote signals or barrier semaphores. Data moves between devices by JAX's collectives and lax.ppermute only.
A program may use at most 64 MiB of HBM per device.

v0:
```python
import jax
import jax.numpy as jnp
from jax import lax
from jax.sharding import PartitionSpec as P

ITERS = 2


ETA = 0.3
EPS = 1e-06
GROUP = 8


def tile_pass(tiles, rows, cols, first, stop, source, width, backward):
    total = tiles.shape[0]
    tile = tiles.shape[1]
    lanes = jnp.arange(GROUP, dtype=jnp.int32)
    targets = jnp.arange(width, dtype=jnp.int32)
    turns = (stop - first + GROUP - 1) // GROUP

    def advance(turn, acc):
        begin = first + turn * GROUP
        shifted = jnp.minimum(begin, total - GROUP)
        index = shifted + lanes
        alive = (index >= begin) & (index < stop)
        block = lax.dynamic_slice_in_dim(tiles, shifted, GROUP, 0).astype(jnp.float32)
        row_ids = lax.dynamic_slice_in_dim(rows, shifted, GROUP, 0)
        col_ids = lax.dynamic_slice_in_dim(cols, shifted, GROUP, 0)
        if backward:
            picked = jnp.take(source, row_ids, axis=1)
            contrib = jnp.einsum("gij,sgi->sgj", block, picked, precision=lax.Precision.HIGHEST)
            landing = col_ids
        else:
            picked = jnp.take(source, col_ids, axis=1)
            contrib = jnp.einsum("gij,sgj->sgi", block, picked, precision=lax.Precision.HIGHEST)
            landing = row_ids
        onehot = ((landing[:, None] == targets[None, :]) & alive[:, None]).astype(jnp.float32)
        return acc + jnp.einsum("gk,sgi->ski", onehot, contrib, precision=lax.Precision.HIGHEST)

    init = jnp.zeros((source.shape[0], width, tile), jnp.float32)
    return lax.fori_loop(0, turns, advance, init)


def project_primal(point, partial_value, cost, upper, bounded, tau):
    moved = point - tau * (cost[None, :] - partial_value)
    moved = jnp.where(bounded[None, :], jnp.minimum(moved, upper[None, :]), moved)
    return jnp.maximum(moved, 0.0)


def on_device(
    tiles,
    tile_row,
    tile_col,
    tile_count,
    cost,
    demand,
    upper,
    col_flag,
    row_flag,
    primal_start,
    dual_start,
):
    tile = tiles.shape[1]
    scenarios = primal_start.shape[0]
    col_blocks = primal_start.shape[1] // tile
    row_blocks = dual_start.shape[1] // tile
    own_count = tile_count[0]
    bounded = col_flag > 0
    inequal = row_flag > 0
    point, dual = (primal_start, dual_start)
    weight = jnp.ones((scenarios,), jnp.float32)
    for step in range(ITERS):
        tau = (ETA / weight)[:, None]
        sigma = (ETA * weight)[:, None]
        backward_source = dual.reshape(scenarios, row_blocks, tile)
        backward_mine = tile_pass(
            tiles, tile_row, tile_col, 0, own_count, backward_source, col_blocks, True
        )
        partial_value = backward_mine.reshape(scenarios, col_blocks * tile)
        share = lax.psum_scatter(
            partial_value.astype(jnp.bfloat16), "rowblk", scatter_dimension=1, tiled=True
        ).astype(jnp.float32)
        width = share.shape[1]
        begin = lax.axis_index("rowblk") * width

        def portion(values):
            return lax.dynamic_slice_in_dim(values, begin, width, values.ndim - 1)

        point_part = portion(point)
        x_hat = project_primal(
            point_part, share, portion(cost), portion(upper), portion(bounded), tau
        )
        primal_diff = x_hat - point_part
        primal_term = jnp.sum(primal_diff * primal_diff, axis=1)
        x_bar = lax.all_gather(2.0 * x_hat - point_part, "rowblk", axis=1, tiled=True)
        source = x_bar.reshape(scenarios, col_blocks, tile)
        mine = tile_pass(tiles, tile_row, tile_col, 0, own_count, source, row_blocks, False)
        summed = lax.psum(mine.reshape(scenarios, row_blocks * tile), "colblk")
        moved = dual + sigma * (demand - summed)
        y_hat = jnp.where(inequal[None, :], jnp.maximum(moved, 0.0), moved)
        dual_diff = y_hat - dual
        dual_term = jnp.sum(dual_diff * dual_diff, axis=1) / lax.axis_size("colblk")
        primal_norm, dual_norm = lax.psum((primal_term, dual_term), ("rowblk", "colblk"))
        weight = jnp.sqrt(weight * jnp.sqrt((dual_norm + EPS) / (primal_norm + EPS)))
        mix = (step + 1.0) / (step + 2.0)
        point = mix * x_bar + (1.0 - mix) * primal_start
        dual = mix * (2.0 * y_hat - dual) + (1.0 - mix) * dual_start
    return (point, dual, weight)


def solution(mesh):
    return jax.shard_map(
        on_device,
        mesh=mesh,
        in_specs=(
            P(("groups", "rowblk", "colblk"), None, None),
            P(("groups", "rowblk", "colblk")),
            P(("groups", "rowblk", "colblk")),
            P(("groups", "rowblk", "colblk")),
            P(("groups", "colblk")),
            P(None, ("groups", "rowblk")),
            P(("groups", "colblk")),
            P(("groups", "colblk")),
            P(("groups", "rowblk")),
            P(None, ("groups", "colblk")),
            P(None, ("groups", "rowblk")),
        ),
        out_specs=(P(None, ("groups", "colblk")), P(None, ("groups", "rowblk")), P("groups")),
        check_vma=False,
    )
```

profile of v0, /device:TPU:0, one launch (start us, length us, event | category | flops | bytes accessed | tf_op | source)
XLA Modules:
  0.0 408.9 jit_solution(16620750190762773866)
XLA Ops:
  7.9 10.8 %while.44 = (s32[]{:T(128)}, f32[8,64,128]{2,1,0:T(8,128)S(1)}, s32[]{:T(128)}, s32[96]{0:T(128)}, f32[8,32,128]{2,0,1:T(8,128)}, /*index=5*/bf16[96,128,128]{2,...) while((s32[]{:T(128)}, f32[8,64,128]{2,1,0:T(8,128)S(1)}, ...), condition=%wide.region_1.3_spmd.clone, body=%wide.region_0.2_spmd.clone.sunk | while | flops 18950232 | bytes 954839 | solution.py:41
  7.9 1.4 compare_and_fusion.12
  9.3 1.5 gather_fusion
  10.8 1.3 fusion.113
  12.1 0.7 dynamic_slice.114
  13.3 1.4 compare_and_fusion.12
  14.7 1.5 gather_fusion
  16.2 1.3 fusion.113
  17.5 0.7 dynamic_slice.114
  18.7 0.7 copy.48
  19.6 0.7 dynamic_slice.57
  21.0 0.7 dynamic-slice_compare_fusion
  21.7 73.0 %reduce-scatter.3.cloned.1.call-done = bf16[8,2048]{1,0:T(8,128)(2,1)} async-done(((bf16[8,8192]{1,0:T(8,128)(2,1)}), bf16[8,2048]{1,0:T(8,128)(2,1)}) %reduce-scatter.3.cloned.1.call-update) | async-done | bytes 32784 | tf_op jit(solution)/shard_map/reduce_scatter | solution.py:80
  94.7 0.9 multiply_reduce_fusion.3
  95.6 5.8 %all_gather.6 = f32[8,8192]{1,0:T(8,128)S(1)} all-gather(f32[8,2048]{1,0:T(8,128)S(1)} %get-tuple-element.414), channel_id=1, replica_groups=mesh['groups'=2,'rowblk'=4,'colblk'=4] {'rowblk'}, dimensions={1}, use_global_device_ids=true | all-gather | bytes 327680 | tf_op jit(solution)/shard_map/all_gather | solution.py:95
  101.4 9.1 %while.45 = (s32[]{:T(128)}, f32[8,32,128]{2,1,0:T(8,128)S(1)}, s32[]{:T(128)}, s32[96]{0:T(128)}, f32[8,64,128]{2,0,1:T(8,128)S(1)}, /*index=5*/bf16[96,128,128...) while((s32[]{:T(128)}, f32[8,32,128]{2,1,0:T(8,128)S(1)}, ...), condition=%wide.region_4.7_spmd.clone, body=%wide.region_3.6_spmd.clone.sunk | while | flops 15771223 | bytes 692695 | solution.py:41
  101.4 1.4 compare_and_fusion.13
  103.3 1.5 fusion.119
  104.9 0.7 dynamic_slice.116
  106.0 1.4 compare_and_fusion.13
  107.9 1.5 fusion.119
  109.4 0.7 dynamic_slice.116
  110.5 0.7 copy.47
  111.4 79.3 %all-reduce.5.cloned.1.call-done = f32[8,4096]{1,0:T(8,128)} async-done(((f32[8,4096]{1,0:T(8,128)}), f32[8,4096]{1,0:T(8,128)}) %all-reduce.5.cloned.1.call-update) | async-done | bytes 131088 | tf_op jit(solution)/shard_map/psum | solution.py:98
  190.7 1.1 multiply_reduce_fusion.1
  191.8 9.0 %while.46 = (s32[]{:T(128)}, f32[8,64,128]{2,1,0:T(8,128)S(1)}, s32[]{:T(128)}, s32[96]{0:T(128)}, f32[8,32,128]{2,0,1:T(8,128)S(1)}, /*index=5*/bf16[96,128,128...) while((s32[]{:T(128)}, f32[8,64,128]{2,1,0:T(8,128)S(1)}, ...), condition=%wide.region_11.14_spmd.clone, body=%wide.region_10.13_spmd.clone.sunk | while | flops 18950232 | bytes 954839 | solution.py:41
  191.8 1.4 compare_and_fusion.14
  193.7 1.3 fusion.125
  195.1 0.7 dynamic_slice.118
  196.3 1.4 compare_and_fusion.14
  198.2 1.3 fusion.125
  199.5 0.7 dynamic_slice.118
  200.8 0.7 copy.46
  201.6 66.1 %all-reduce.1 = (f32[8]{0:T(128)S(1)}, f32[8]{0:T(128)S(1)}) all-reduce(f32[8]{0:T(128)S(1)} %get-tuple-element.413, f32[8]{0:T(128)S(1)} %broadcast_multiply_fusion.1), channel_id=1, replica_groups=mesh['groups'=2,'rowblk'=4,'colblk'=4] {'rowblk','colblk'}, use_global_device_ids=true, to_apply=%region_9.12 | all-reduce | flops 16 | bytes 128 | tf_op jit(solution)/shard_map/psum | solution.py:103
  267.8 1.0 multiply_reduce_fusion.2
  268.8 10.2 %all_gather.7 = f32[8,8192]{1,0:T(8,128)S(1)} all-gather(f32[8,2048]{1,0:T(8,128)S(1)} %get-tuple-element.408), channel_id=1, replica_groups=mesh['groups'=2,'rowblk'=4,'colblk'=4] {'rowblk'}, dimensions={1}, use_global_device_ids=true | all-gather | bytes 327680 | tf_op jit(solution)/shard_map/all_gather | solution.py:95
  279.0 9.1 %while.47 = (s32[]{:T(128)}, f32[8,32,128]{2,1,0:T(8,128)S(1)}, s32[]{:T(128)}, s32[96]{0:T(128)}, f32[8,64,128]{2,0,1:T(8,128)S(1)}, /*index=5*/bf16[96,128,128...) while((s32[]{:T(128)}, f32[8,32,128]{2,1,0:T(8,128)S(1)}, ...), condition=%wide.region_14.17_spmd.clone, body=%wide.region_13.16_spmd.clone.sunk | while | flops 15771223 | bytes 692695 | solution.py:41
  279.0 1.4 compare_and_fusion.15
  281.0 1.5 fusion.131
  282.5 0.7 dynamic_slice.120
  283.6 1.4 compare_and_fusion.15
  285.5 1.5 fusion.131
  287.0 0.7 dynamic_slice.120
  288.1 0.7 copy.45
  288.9 0.7 multiply_add_fusion
  289.6 79.3 %all-reduce.7.cloned.1.call-done = f32[8,4096]{1,0:T(8,128)} async-done(((f32[8,4096]{1,0:T(8,128)}), f32[8,4096]{1,0:T(8,128)}) %all-reduce.7.cloned.1.call-update) | async-done | bytes 131088 | tf_op jit(solution)/shard_map/psum | solution.py:98
  369.0 1.8 multiply_reduce_fusion
  370.8 31.0 %all-reduce = (f32[8]{0:T(128)S(1)}, f32[8]{0:T(128)S(1)}) all-reduce(f32[8]{0:T(128)S(1)} %get-tuple-element.407, f32[8]{0:T(128)S(1)} %broadcast_multiply_fusion), channel_id=1, replica_groups=mesh['groups'=2,'rowblk'=4,'colblk'=4] {'rowblk','colblk'}, use_global_device_ids=true, to_apply=%region_19.22 | all-reduce | flops 16 | bytes 128 | tf_op jit(solution)/shard_map/psum | solution.py:103
  (54 shorter events, 8.1 us)
Async XLA Ops:
  7.2 87.5 %reduce-scatter.3.cloned.1.call-start = ((), (), s32[]{:S(2)}) async-start(), calls=%async_computation.2 | async-start | bytes 163840 | tf_op jit(solution)/shard_map/reduce_scatter | solution.py:80
  7.9 86.8 %copy-start.1 = (f32[8,8192]{1,0:T(8,128)S(1)}, f32[8,8192]{1,0:T(8,128)}, u32[]{:S(2)}) copy-start(f32[8,8192]{1,0:T(8,128)} %param.32) | copy-start | bytes 786436
  18.7 92.7 %copy-start.4 = (s32[4096]{0:T(1024)S(1)}, s32[4096]{0:T(1024)}, u32[]{:S(2)}) copy-start(s32[4096]{0:T(1024)} %param.31) | copy-start | bytes 49156
  18.7 172.0 %copy-start = (f32[8,32,128]{2,0,1:T(8,128)S(1)}, f32[8,32,128]{2,0,1:T(8,128)}, u32[]{:S(2)}) copy-start(f32[8,32,128]{2,0,1:T(8,128)} %get-tuple-element.803) | copy-start | bytes 393220
  18.7 172.0 %copy-start.2 = (f32[8,4096]{1,0:T(8,128)S(1)}, f32[8,4096]{1,0:T(8,128)}, u32[]{:S(2)}) copy-start(f32[8,4096]{1,0:T(8,128)} %param.28) | copy-start | bytes 393220
  19.5 171.1 %all-reduce.5.cloned.1.call-start = ((), (), s32[]{:S(2)}) async-start(), calls=%async_computation.3 | async-start | bytes 262144 | tf_op jit(solution)/shard_map/psum | solution.py:98
  111.3 156.5 %reduce-scatter.5.cloned.1.call-start = ((), (), s32[]{:S(2)}) async-start(), calls=%async_computation.4 | async-start | bytes 163840 | tf_op jit(solution)/shard_map/reduce_scatter | solution.py:80
  200.8 168.2 %copy-start.3 = (f32[8,4096]{1,0:T(8,128)S(1)}, f32[8,4096]{1,0:T(8,128)}, u32[]{:S(2)}) copy-start(f32[8,4096]{1,0:T(8,128)} %all-reduce.5.cloned.1.call-done) | copy-start | bytes 393220
  201.5 167.4 %all-reduce.7.cloned.1.call-start = ((), (), s32[]{:S(2)}) async-start(), calls=%async_computation.5 | async-start | bytes 262144 | tf_op jit(solution)/shard_map/psum | solution.py:98
Sparse Core Ops, SparseCore 0:
  19.6 74.9 reduce-scatter.2
  111.4 79.2 all-reduce.4
  201.7 63.9 reduce-scatter.4
  289.0 79.9 all-reduce.6
where the time goes:
time: 410 us; the launch traced here: 409 us
  waiting for transfers between devices  232 us (57%)
  blocking collectives  113 us (28%)
  other arithmetic  18 us (4%)
  local copies, waits for them, and re-layouts  16.6 us (4%)
  between operations  14.6 us (4%)
  matrix products  14.3 us (3%)
    psum x2, waiting for transfers between devices, on_device(): summed = lax.psum(mine.reshape(scenarios, row_blocks * tile), 'colblk')  159 us
    psum x2, blocking collectives, on_device(): lax.psum((primal_term, dual_term), ('rowblk', 'colblk'))  97.1 us
    reduce_scatter x2, waiting for transfers between devices, on_device(): lax.psum_scatter(partial_value.astype(jnp.bfloat16), 'rowblk', scatter_di...  73 us
    all_gather x2, blocking collectives, on_device(): lax.all_gather(2.0 * x_hat - point_part, 'rowblk', axis=1, tiled=True)  16 us
  transfers between devices with their start and end apart: 4, of which 3 were waited for; matrix products, arithmetic and copies ran while one was open for 1% of the time, Pallas kernels for 0%

commit v1 on v0

v1 whole, which is shorter than its diff:
```python
import functools

import jax
import jax.numpy as jnp
from jax import lax
from jax.experimental import pallas as pl
from jax.experimental.pallas import tpu as pltpu
from jax.sharding import PartitionSpec as P

ITERS = 2
ETA = 0.3
EPS = 1e-06
PART = 32
VMEM_LIMIT = 40 * 1024 * 1024

SMEM_SPEC = pl.BlockSpec(memory_space=pltpu.SMEM)
VMEM_SPEC = pl.BlockSpec(memory_space=pltpu.VMEM)


def split_rows(value):
    high = value.astype(jnp.bfloat16)
    low = (value - high.astype(jnp.float32)).astype(jnp.bfloat16)
    return jnp.concatenate([high, low], axis=0)


def join_rows(value):
    half = value.shape[0] // 2
    return value[:half].astype(jnp.float32) + value[half:].astype(jnp.float32)


def tile_products(count, rows, cols, tiles, source, acc, backward):
    total, tile = tiles.shape[0], tiles.shape[1]
    spare = acc.shape[0] - 1
    scen = acc.shape[1]
    live = count[0]
    depth = 0 if backward else 1
    dims = (((1,), (depth,)), ((), ()))
    acc[...] = jnp.zeros_like(acc)

    def part(first, size):
        landing, results = [], []
        for g in range(first, first + size):
            goes = cols[g] if backward else rows[g]
            landing.append(jnp.where(g < live, goes, spare))
        pair = 2 if size % 2 == 0 else 1
        for g in range(first, first + size, pair):
            picked = [source[rows[g + k] if backward else cols[g + k]] for k in range(pair)]
            if pair == 2:
                blank = jnp.zeros_like(picked[0])
                left = jnp.concatenate(
                    [
                        jnp.concatenate([picked[0], blank], axis=1),
                        jnp.concatenate([blank, picked[1]], axis=1),
                    ],
                    axis=0,
                )
                right = jnp.concatenate([tiles[g], tiles[g + 1]], axis=depth)
            else:
                left, right = picked[0], tiles[g]
            product = lax.dot_general(left, right, dims, preferred_element_type=jnp.float32)
            for k in range(pair):
                own = product[2 * scen * k : 2 * scen * (k + 1)]
                results.append(own[:scen] + own[scen:])
        for where, value in zip(landing, results):
            acc[where] += value

    for first in range(0, total, PART):
        size = min(PART, total - first)
        if first == 0:
            part(first, size)
        else:
            pl.when(first < live)(functools.partial(part, first, size))


def pack(acc, out, norm, slot):
    half = (acc.shape[0] - 1) // 2
    for b in range(half):
        out[b] = jnp.concatenate([acc[b], acc[b + half]], axis=0).astype(jnp.bfloat16)
    lanes = lax.broadcasted_iota(jnp.int32, (acc.shape[1], acc.shape[2]), 1)
    out[half] = split_rows(jnp.where(lanes == slot, norm, 0.0))


def unpack(parts, b, half):
    scen = parts[0].shape[1] // 2
    rows = slice(0, scen) if b < half else slice(scen, 2 * scen)
    k = b if b < half else b - half
    terms = [p[k, rows, :].astype(jnp.float32) for p in parts]
    while len(terms) > 1:
        terms = [terms[i] + terms[i + 1] for i in range(0, len(terms), 2)]
    return terms[0]


def unpack_norm(parts, half):
    terms = [join_rows(p[half]) for p in parts]
    while len(terms) > 1:
        terms = [terms[i] + terms[i + 1] for i in range(0, len(terms), 2)]
    return jnp.sum(terms[0], axis=1, keepdims=True)


def first_kernel(count, rows, cols, tiles, dual, out, source, acc):
    tile = tiles.shape[1]
    for b in range(source.shape[0]):
        source[b] = split_rows(dual[:, b * tile : (b + 1) * tile])
    tile_products(count, rows, cols, tiles, source, acc, True)
    pack(acc, out, 0.0, 0)


def primal_kernel(mix, n_parts, *refs):
    count, rows, cols, slot, tiles = refs[:5]
    parts = refs[5 : 5 + n_parts]
    refs = refs[5 + n_parts :]
    weight_in, primal_norm, cost, upper, flag, point, start = refs[:7]
    point_out, weight_out, out, source, acc = refs[7:]
    tile = tiles.shape[1]
    blocks = source.shape[0]
    half = blocks // 2
    if mix > 0.5:
        dual_norm = unpack_norm(parts, half)
        weight = weight_in[:, :1]
        ratio = (dual_norm + EPS) / (primal_norm[:, :1] + EPS)
        weight = jnp.sqrt(weight * jnp.sqrt(ratio))
        weight_out[...] = jnp.broadcast_to(weight, weight_out.shape)
        tau = ETA / weight
    else:
        weight_out[...] = weight_in[...]
        tau = ETA / weight_in[:, :1]
    tau = jnp.broadcast_to(tau, (tau.shape[0], tile))
    moved_norm = jnp.zeros_like(tau)
    for b in range(blocks):
        lanes = slice(b * tile, (b + 1) * tile)
        value = unpack(parts, b, half)
        old = point[:, lanes]
        moved = old - tau * (cost[b : b + 1, :] - value)
        limit = jnp.where(flag[b : b + 1, :] > 0, upper[b : b + 1, :], jnp.inf)
        x_hat = jnp.maximum(jnp.minimum(moved, limit), 0.0)
        step = x_hat - old
        moved_norm += step * step
        x_bar = 2.0 * x_hat - old
        point_out[:, lanes] = mix * x_bar + (1.0 - mix) * start[:, lanes]
        source[b] = split_rows(x_bar)
    tile_products(count, rows, cols, tiles, source, acc, False)
    pack(acc, out, jnp.sum(moved_norm, axis=1, keepdims=True), slot[0])


def dual_kernel(mix, last, n_parts, *refs):
    count, rows, cols, slot, tiles = refs[:5]
    parts = refs[5 : 5 + n_parts]
    refs = refs[5 + n_parts :]
    weight, demand, flag, dual, start = refs[:5]
    if last:
        dual_out, primal_norm, out = refs[5:]
    else:
        dual_out, primal_norm, out, source, acc = refs[5:]
    tile = flag.shape[1]
    blocks = flag.shape[0]
    half = blocks // 2
    primal_norm[...] = jnp.broadcast_to(unpack_norm(parts, half), primal_norm.shape)
    sigma = ETA * weight[...]
    moved_norm = jnp.zeros_like(sigma)
    for b in range(blocks):
        lanes = slice(b * tile, (b + 1) * tile)
        value = unpack(parts, b, half)
        old = dual[:, lanes]
        moved = old + sigma * (demand[:, lanes] - value)
        floor = jnp.where(flag[b : b + 1, :] > 0, 0.0, -jnp.inf)
        y_hat = jnp.maximum(moved, floor)
        step = y_hat - old
        moved_norm += step * step
        new = mix * (2.0 * y_hat - old) + (1.0 - mix) * start[:, lanes]
        dual_out[:, lanes] = new
        if not last:
            source[b] = split_rows(new)
    dual_norm = jnp.sum(moved_norm, axis=1, keepdims=True)
    if last:
        lanes = lax.broadcasted_iota(jnp.int32, out.shape, 1)
        out[...] = jnp.where(lanes == slot[0], dual_norm, 0.0)
    else:
        tile_products(count, rows, cols, tiles, source, acc, True)
        pack(acc, out, dual_norm, slot[0])


def call(kernel, inputs, outputs, scratch, scalars):
    specs = [SMEM_SPEC] * scalars + [VMEM_SPEC] * (len(inputs) - scalars)
    return pl.pallas_call(
        kernel,
        out_shape=outputs,
        in_specs=specs,
        out_specs=[VMEM_SPEC] * len(outputs),
        scratch_shapes=scratch,
        compiler_params=pltpu.CompilerParams(vmem_limit_bytes=VMEM_LIMIT),
    )(*inputs)


def swap(value, axis, mask):
    size = lax.axis_size(axis)
    return lax.ppermute(value, axis, [(i, i ^ mask) for i in range(size)])


def plus(a, b):
    return (a.astype(jnp.float32) + b.astype(jnp.float32)).astype(a.dtype)


def butterfly(value, axis, radix):
    size = lax.axis_size(axis)
    if size & (size - 1):
        return [lax.psum(value.astype(jnp.float32), axis)]
    mask, parts = 1, [value]
    while mask < size:
        terms = [p.astype(jnp.float32) for p in parts]
        while len(terms) > 1:
            terms = [terms[i] + terms[i + 1] for i in range(0, len(terms), 2)]
        total = terms[0].astype(value.dtype)
        span = min(radix, size // mask)
        parts = [total] + [swap(total, axis, mask * k) for k in range(1, span)]
        mask *= span
    return parts


def on_device(
    tiles,
    tile_row,
    tile_col,
    tile_count,
    cost,
    demand,
    upper,
    col_flag,
    row_flag,
    primal_start,
    dual_start,
):
    tile = tiles.shape[1]
    scen = primal_start.shape[0]
    col_blocks = primal_start.shape[1] // tile
    row_blocks = dual_start.shape[1] // tile
    bf16, f32 = jnp.bfloat16, jnp.float32
    cost, upper, col_flag = (v.reshape(col_blocks, tile) for v in (cost, upper, col_flag))
    row_flag = row_flag.reshape(row_blocks, tile)
    row_slot = lax.axis_index("rowblk").astype(jnp.int32).reshape(1)
    col_slot = lax.axis_index("colblk").astype(jnp.int32).reshape(1)
    grid = [tile_count, tile_row, tile_col]

    small = jax.ShapeDtypeStruct((scen, tile), f32)
    col_parts = jax.ShapeDtypeStruct((col_blocks // 2 + 1, 2 * scen, tile), bf16)
    row_parts = jax.ShapeDtypeStruct((row_blocks // 2 + 1, 2 * scen, tile), bf16)
    primal = jax.ShapeDtypeStruct(primal_start.shape, f32)
    dual_like = jax.ShapeDtypeStruct(dual_start.shape, f32)
    to_cols = [
        pltpu.VMEM((row_blocks, 2 * scen, tile), bf16),
        pltpu.VMEM((col_blocks + 1, scen, tile), f32),
    ]
    to_rows = [
        pltpu.VMEM((col_blocks, 2 * scen, tile), bf16),
        pltpu.VMEM((row_blocks + 1, scen, tile), f32),
    ]

    point, dual = primal_start, dual_start
    weight = jnp.ones((scen, tile), f32)
    primal_norm = weight
    (terms,) = call(first_kernel, [*grid, tiles, dual], [col_parts], to_cols, 3)
    for step in range(ITERS):
        mix = (step + 1.0) / (step + 2.0)
        last = step == ITERS - 1
        parts = butterfly(terms, "rowblk", 2)
        point, weight, terms = call(
            functools.partial(primal_kernel, mix, len(parts)),
            [*grid, col_slot, tiles, *parts, weight, primal_norm, cost, upper, col_flag, point, primal_start],
            [primal, small, row_parts],
            to_rows,
            4,
        )
        parts = butterfly(terms, "colblk", 4)
        dual, primal_norm, terms = call(
            functools.partial(dual_kernel, mix, last, len(parts)),
            [*grid, row_slot, tiles, *parts, weight, demand, row_flag, dual, dual_start],
            [dual_like, small, small if last else col_parts],
            [] if last else to_cols,
            4,
        )
    parts = butterfly(terms, "rowblk", 4)
    dual_norm = jnp.sum(functools.reduce(jnp.add, parts), axis=1)
    ratio = (dual_norm + EPS) / (primal_norm[:, 0] + EPS)
    weight = jnp.sqrt(weight[:, 0] * jnp.sqrt(ratio))
    return point, dual, weight


def solution(mesh):
    return jax.shard_map(
        on_device,
        mesh=mesh,
        in_specs=(
            P(("groups", "rowblk", "colblk"), None, None),
            P(("groups", "rowblk", "colblk")),
            P(("groups", "rowblk", "colblk")),
            P(("groups", "rowblk", "colblk")),
            P(("groups", "colblk")),
            P(None, ("groups", "rowblk")),
            P(("groups", "colblk")),
            P(("groups", "colblk")),
            P(("groups", "rowblk")),
            P(None, ("groups", "colblk")),
            P(None, ("groups", "rowblk")),
        ),
        out_specs=(P(None, ("groups", "colblk")), P(None, ("groups", "rowblk")), P("groups")),
        check_vma=False,
    )
```

time: 410 us -> 62.9 us (0.15)
  waiting for transfers between devices: 232 us -> 22.9 us
  blocking collectives: 113 us -> 0 us
  other arithmetic: 18 us -> 1.51 us
  starting transfers between devices: 0.16 us -> 16.4 us
  matrix products: 14.3 us -> 0 us
  between operations: 14.6 us -> 1.41 us
  Pallas kernels: 0 us -> 8.2 us
  local copies, waits for them, and re-layouts: 16.6 us -> 12 us
    psum x2 -> x0, waiting for transfers between devices: 159 us -> none  [on_device(): summed = lax.psum(mine.reshape(scenarios, row_blocks * tile), 'colblk')]
    psum x2 -> x0, blocking collectives: 97.1 us -> none  [on_device(): lax.psum((primal_term, dual_term), ('rowblk', 'colblk'))]
    reduce_scatter x2 -> x0, waiting for transfers between devices: 73 us -> none  [on_device(): lax.psum_scatter(partial_value.astype(jnp.bfloat16), 'rowblk', scatter_di...]
    ppermute x0 -> x13, waiting for transfers between devices: none -> 22.9 us  [swap(): return lax.ppermute(value, axis, [(i, i ^ mask) for i in range(size)])]
    ppermute x0 -> x13, starting transfers between devices: none -> 16.4 us  [swap(): return lax.ppermute(value, axis, [(i, i ^ mask) for i in range(size)])]
    all_gather x2 -> x0, blocking collectives: 16 us -> none  [on_device(): lax.all_gather(2.0 * x_hat - point_part, 'rowblk', axis=1, tiled=True)]
    dot_general x16 -> x0, matrix products: 14.3 us -> none  [the longest x4 6.01 us: advance(): jnp.einsum('gij,sgj->sgi', block, picked, precision=lax.Precision.HIGHEST)]
    and x8 -> x0, other arithmetic: 11.1 us -> none  [the longest x4 5.53 us: advance(): picked = jnp.take(source, row_ids, axis=1)]
  transfers between devices with their start and end apart: 4 -> 13, of which waited for: 3 -> 10; matrix products, arithmetic and copies ran while one was open for 1% -> 0% of each run, Pallas kernels for 0% -> 0%
where the time goes in v1:
time: 62.9 us; the launch traced here: 62.5 us
  waiting for transfers between devices  22.9 us (36%)
  starting transfers between devices  16.4 us (26%)
  local copies, waits for them, and re-layouts  12 us (19%)
  Pallas kernels  8.2 us (13%)
  other arithmetic  1.51 us (2%)
  between operations  1.41 us (2%)
    ppermute x13, waiting for transfers between devices, swap(): return lax.ppermute(value, axis, [(i, i ^ mask) for i in range(size)])  22.9 us
    ppermute x13, starting transfers between devices, swap(): return lax.ppermute(value, axis, [(i, i ^ mask) for i in range(size)])  16.4 us
    unnamed x52, local copies, waits for them, and re-layouts  11.9 us
    pallas_call x5, Pallas kernels, call(): pl.pallas_call(kernel, out_shape=outputs, in_specs=specs, out_specs=[VMEM...  8.2 us
  transfers between devices with their start and end apart: 13, of which 10 were waited for; matrix products, arithmetic and copies ran while one was open for 0% of the time, Pallas kernels for 0%

profile of v1, /device:TPU:0, one launch (start us, length us, event | category | flops | bytes accessed | tf_op | source)
XLA Modules:
  0.0 62.5 jit_solution(2406223354518169327)
XLA Ops:
  1.3 1.9 %copy-done = bf16[96,128,128]{2,1,0:T(8,128)(2,1)S(1)} copy-done((bf16[96,128,128]{2,1,0:T(8,128)(2,1)S(1)}, bf16[96,128,128]{2,1,0:T(8,128)(2,1)}, u32[]{:S(2)}) %copy-start) | copy-done | bytes 3145752
  3.2 0.9 %copy-done.3 = f32[8,4096]{1,0:T(8,128)S(1)} copy-done((f32[8,4096]{1,0:T(8,128)S(1)}, f32[8,4096]{1,0:T(8,128)}, u32[]{:S(2)}) %copy-start.3) | copy-done | bytes 131096
  4.1 0.7 %copy-done.19 = s32[96]{0:T(128)S(1)} copy-done((s32[96]{0:T(128)S(1)}, s32[96]{0:T(128)}, u32[]{:S(2)}) %copy-start.19) | copy-done | bytes 408
  4.7 0.7 %copy-done.22 = s32[96]{0:T(128)S(1)} copy-done((s32[96]{0:T(128)S(1)}, s32[96]{0:T(128)}, u32[]{:S(2)}) %copy-start.22) | copy-done | bytes 408
  5.4 0.9 %shard_map.130 = bf16[33,16,128]{2,1,0:T(8,128)(2,1)S(1)} custom-call(s32[1]{0:T(128)S(6)} %copy.14.count.refs_0_, s32[96]{0:T(128)S(1)} %copy-done.19, s32[96]{0:T(128)S(1)} %copy-done.22, bf16[96,128,128]{2,1,0:T(8,128)(2,1)S(1)} %copy-done, f32[8,4096]{1,0:T(8,128)S(1)} %copy-done.3), custom_call_target="tpu_custom_call" | custom-call | tf_op jit(solution)/shard_map/pallas_call | solution.py:184
  6.3 0.8 %collective-permute-start = (bf16[33,16,128]{2,1,0:T(8,128)(2,1)S(1)}, bf16[33,16,128]{2,1,0:T(8,128)(2,1)S(1)}, u32[]{:S(2)}, u32[]{:S(2)}) collective-permute-start(bf16[33,16,128]{2,1,0:T(8,128)(2,1)S(1)} %shard_map.130), channel_id=1, source_target_pairs={{0,4},{4,0},{8,12},{12,8},{1,5},{5,1},{9,13},{13,9},{2,6},{6,2},{1... | collective-permute-start | bytes 405512 | tf_op jit(solution)/shard_map/ppermute | solution.py:196
  7.1 1.0 %collective-permute-done = bf16[33,16,128]{2,1,0:T(8,128)(2,1)S(1)} collective-permute-done((bf16[33,16,128]{2,1,0:T(8,128)(2,1)S(1)}, bf16[33,16,128]{2,1,0:T(8,128)(2,1)S(1)}, u32[]{:S(2)}, u32[]{:S(2)}) %collective-permute-start) | collective-permute-done | bytes 135200 | tf_op jit(solution)/shard_map/ppermute | solution.py:196
  8.1 0.7 %add_convert_fusion.1.refs_5_ = bf16[33,16,128]{2,1,0:T(8,128)(2,1)} fusion(bf16[33,16,128]{2,1,0:T(8,128)(2,1)S(1)} %collective-permute-done, bf16[33,16,128]{2,1,0:T(8,128)(2,1)S(1)} %shard_map.130), kind=kLoop, calls=%fused_computation.1 | loop fusion | flops 270336 | bytes 405504 | tf_op jit(solution)/shard_map/convert_element_type | solution.py:212
  8.8 2.9 %collective-permute-start.1 = (bf16[33,16,128]{2,1,0:T(8,128)(2,1)}, bf16[33,16,128]{2,1,0:T(8,128)(2,1)}, u32[]{:S(2)}, u32[]{:S(2)}) collective-permute-start(bf16[33,16,128]{2,1,0:T(8,128)(2,1)} %add_convert_fusion.1.refs_5_), channel_id=1, source_target_pairs={{0,8},{4,12},{8,0},{12,4},{1,9},{5,13},{9,1},{13,5},{2,10},{6,14},... | collective-permute-start | bytes 405512 | tf_op jit(solution)/shard_map/ppermute | solution.py:196
  11.7 4.2 %collective-permute-done.1.refs_6_ = bf16[33,16,128]{2,1,0:T(8,128)(2,1)} collective-permute-done((bf16[33,16,128]{2,1,0:T(8,128)(2,1)}, bf16[33,16,128]{2,1,0:T(8,128)(2,1)}, u32[]{:S(2)}, u32[]{:S(2)}) %collective-permute-start.1) | collective-permute-done | bytes 135200 | tf_op jit(solution)/shard_map/ppermute | solution.py:196
  15.9 0.8 %copy-done.9 = f32[8192]{0:T(1024)S(1)} copy-done((f32[8192]{0:T(1024)S(1)}, f32[8192]{0:T(1024)}, u32[]{:S(2)}) %copy-start.9) | copy-done | bytes 32792
  16.6 0.8 %copy-done.11 = f32[8192]{0:T(1024)S(1)} copy-done((f32[8192]{0:T(1024)S(1)}, f32[8192]{0:T(1024)}, u32[]{:S(2)}) %copy-start.11) | copy-done | bytes 32792
  17.4 0.8 %copy-done.13 = s32[8192]{0:T(1024)S(1)} copy-done((s32[8192]{0:T(1024)S(1)}, s32[8192]{0:T(1024)}, u32[]{:S(2)}) %copy-start.13) | copy-done | bytes 32792
  18.2 0.7 %copy-done.20 = s32[96]{0:T(128)S(1)} copy-done((s32[96]{0:T(128)S(1)}, s32[96]{0:T(128)}, u32[]{:S(2)}) %copy-start.20) | copy-done | bytes 408
  18.8 0.7 %copy-done.23 = s32[96]{0:T(128)S(1)} copy-done((s32[96]{0:T(128)S(1)}, s32[96]{0:T(128)}, u32[]{:S(2)}) %copy-start.23) | copy-done | bytes 408
  19.5 2.4 %shard_map.131 = (f32[8,8192]{1,0:T(8,128)S(1)}, f32[8,128]{1,0:T(8,128)S(1)}, bf16[17,16,128]{2,1,0:T(8,128)(2,1)}) custom-call(s32[1]{0:T(128)S(6)} %copy.14.count.refs_0_, s32[96]{0:T(128)S(1)} %copy-done.20, s32[96]{0:T(128)S(1)} %copy-done.23, s32[1]{0:T(128)} %bitcast.refs_3_, bf16[96,128,128]{2,1,0:T(8,128)(2,1)S(1)} %copy-done.1, ...), custom_call_target="tpu_custom_call" | custom-call | tf_op jit(solution)/shard_map/pallas_call | solution.py:184
  21.9 0.7 %copy-done.7 = f32[8,8192]{1,0:T(8,128)} copy-done((f32[8,8192]{1,0:T(8,128)}, f32[8,8192]{1,0:T(8,128)S(1)}, u32[]{:S(2)}) %copy-start.7) | copy-done | bytes 262168
  22.6 0.6 copy-done.16
  23.2 4.3 %collective-permute-start.4 = (bf16[17,16,128]{2,1,0:T(8,128)(2,1)}, bf16[17,16,128]{2,1,0:T(8,128)(2,1)}, u32[]{:S(2)}, u32[]{:S(2)}) collective-permute-start(bf16[17,16,128]{2,1,0:T(8,128)(2,1)} %get-tuple-element.15.refs_5_), channel_id=1, source_target_pairs={{0,3},{1,2},{2,1},{3,0},{4,7},{5,6},{6,5},{7,4},{8,11},{9,10},{10,... | collective-permute-start | bytes 208904 | tf_op jit(solution)/shard_map/ppermute | solution.py:196
  27.5 0.6 collective-permute-start.2
  28.1 2.7 %collective-permute-done.4.refs_8_ = bf16[17,16,128]{2,1,0:T(8,128)(2,1)} collective-permute-done((bf16[17,16,128]{2,1,0:T(8,128)(2,1)}, bf16[17,16,128]{2,1,0:T(8,128)(2,1)}, u32[]{:S(2)}, u32[]{:S(2)}) %collective-permute-start.4) | collective-permute-done | bytes 69664 | tf_op jit(solution)/shard_map/ppermute | solution.py:196
  30.8 2.8 %collective-permute-done.3.refs_7_ = bf16[17,16,128]{2,1,0:T(8,128)(2,1)} collective-permute-done((bf16[17,16,128]{2,1,0:T(8,128)(2,1)}, bf16[17,16,128]{2,1,0:T(8,128)(2,1)}, u32[]{:S(2)}, u32[]{:S(2)}) %collective-permute-start.3) | collective-permute-done | bytes 69664 | tf_op jit(solution)/shard_map/ppermute | solution.py:196
  33.5 0.0 copy-start.5
  33.5 0.9 %copy-done.5 = f32[8,4096]{1,0:T(8,128)S(1)} copy-done((f32[8,4096]{1,0:T(8,128)S(1)}, f32[8,4096]{1,0:T(8,128)}, u32[]{:S(2)}) %copy-start.5) | copy-done | bytes 131096
  34.4 0.7 %copy-done.17 = f32[8,128]{1,0:T(8,128)S(1)} copy-done((f32[8,128]{1,0:T(8,128)S(1)}, f32[8,128]{1,0:T(8,128)}, u32[]{:S(2)}) %copy-start.17) | copy-done | bytes 4120
  35.1 0.7 %copy-done.21 = s32[96]{0:T(128)S(1)} copy-done((s32[96]{0:T(128)S(1)}, s32[96]{0:T(128)}, u32[]{:S(2)}) %copy-start.21) | copy-done | bytes 408
  35.8 0.7 %copy-done.24 = s32[96]{0:T(128)S(1)} copy-done((s32[96]{0:T(128)S(1)}, s32[96]{0:T(128)}, u32[]{:S(2)}) %copy-start.24) | copy-done | bytes 408
  36.4 1.5 %shard_map.132 = (f32[8,4096]{1,0:T(8,128)S(1)}, f32[8,128]{1,0:T(8,128)S(1)}, bf16[33,16,128]{2,1,0:T(8,128)(2,1)S(1)}) custom-call(s32[1]{0:T(128)S(6)} %copy.14.count.refs_0_, s32[96]{0:T(128)S(1)} %copy-done.21, s32[96]{0:T(128)S(1)} %copy-done.24, s32[1]{0:T(128)} %bitcast.1.refs_3_, bf16[96,128,128]{2,1,0:T(8,128)(2,1)S(1)} %copy-done.1, ...), custom_call_target="tpu_custom_call" | custom-call | tf_op jit(solution)/shard_map/pallas_call | solution.py:184
  37.9 0.0 copy-start.6
  37.9 0.1 collective-permute-start.5
  38.0 1.3 %collective-permute-done.5 = bf16[33,16,128]{2,1,0:T(8,128)(2,1)S(1)} collective-permute-done((bf16[33,16,128]{2,1,0:T(8,128)(2,1)S(1)}, bf16[33,16,128]{2,1,0:T(8,128)(2,1)S(1)}, u32[]{:S(2)}, u32[]{:S(2)}) %collective-permute-start.5) | collective-permute-done | bytes 135200 | tf_op jit(solution)/shard_map/ppermute | solution.py:196
  39.4 1.5 %collective-permute-start.6 = (bf16[33,16,128]{2,1,0:T(8,128)(2,1)S(1)}, bf16[33,16,128]{2,1,0:T(8,128)(2,1)S(1)}, u32[]{:S(2)}, u32[]{:S(2)}) collective-permute-start(bf16[33,16,128]{2,1,0:T(8,128)(2,1)S(1)} %add_convert_fusion.refs_5_), channel_id=1, source_target_pairs={{0,8},{4,12},{8,0},{12,4},{1,9},{5,13},{9,1},{13,5},{2,10},{6,14},... | collective-permute-start | bytes 405512 | tf_op jit(solution)/shard_map/ppermute | solution.py:196
  40.9 4.2 %collective-permute-done.6.refs_6_ = bf16[33,16,128]{2,1,0:T(8,128)(2,1)S(1)} collective-permute-done((bf16[33,16,128]{2,1,0:T(8,128)(2,1)S(1)}, bf16[33,16,128]{2,1,0:T(8,128)(2,1)S(1)}, u32[]{:S(2)}, u32[]{:S(2)}) %collective-permute-start.6) | collective-permute-done | bytes 135200 | tf_op jit(solution)/shard_map/ppermute | solution.py:196
  45.1 2.1 %shard_map.133 = (f32[8,8192]{1,0:T(8,128)}, f32[8,128]{1,0:T(8,128)S(1)}, bf16[17,16,128]{2,1,0:T(8,128)(2,1)S(1)}) custom-call(s32[1]{0:T(128)S(6)} %copy.14.count.refs_0_, s32[96]{0:T(128)S(1)} %copy-done.21, s32[96]{0:T(128)S(1)} %copy-done.25, s32[1]{0:T(128)} %bitcast.refs_3_, bf16[96,128,128]{2,1,0:T(8,128)(2,1)S(1)} %copy-done.1, ...), custom_call_target="tpu_custom_call" | custom-call | tf_op jit(solution)/shard_map/pallas_call | solution.py:184
  47.2 3.1 %collective-permute-start.9 = (bf16[17,16,128]{2,1,0:T(8,128)(2,1)S(1)}, bf16[17,16,128]{2,1,0:T(8,128)(2,1)S(1)}, u32[]{:S(2)}, u32[]{:S(2)}) collective-permute-start(bf16[17,16,128]{2,1,0:T(8,128)(2,1)S(1)} %get-tuple-element.21.refs_5_), channel_id=1, source_target_pairs={{0,3},{1,2},{2,1},{3,0},{4,7},{5,6},{6,5},{7,4},{8,11},{9,10},{10,... | collective-permute-start | bytes 208904 | tf_op jit(solution)/shard_map/ppermute | solution.py:196
  50.3 1.3 %collective-permute-start.7 = (bf16[17,16,128]{2,1,0:T(8,128)(2,1)S(1)}, bf16[17,16,128]{2,1,0:T(8,128)(2,1)S(1)}, u32[]{:S(2)}, u32[]{:S(2)}) collective-permute-start(bf16[17,16,128]{2,1,0:T(8,128)(2,1)S(1)} %get-tuple-element.21.refs_5_), channel_id=1, source_target_pairs={{0,1},{1,0},{2,3},{3,2},{4,5},{5,4},{6,7},{7,6},{8,9},{9,8},{10,11... | collective-permute-start | bytes 208904 | tf_op jit(solution)/shard_map/ppermute | solution.py:196
  51.6 0.1 slice_reduce_fusion
  51.7 2.0 %collective-permute-done.9.refs_8_ = bf16[17,16,128]{2,1,0:T(8,128)(2,1)S(1)} collective-permute-done((bf16[17,16,128]{2,1,0:T(8,128)(2,1)S(1)}, bf16[17,16,128]{2,1,0:T(8,128)(2,1)S(1)}, u32[]{:S(2)}, u32[]{:S(2)}) %collective-permute-start.9) | collective-permute-done | bytes 69664 | tf_op jit(solution)/shard_map/ppermute | solution.py:196
  53.7 2.9 %collective-permute-done.8.refs_7_ = bf16[17,16,128]{2,1,0:T(8,128)(2,1)S(1)} collective-permute-done((bf16[17,16,128]{2,1,0:T(8,128)(2,1)S(1)}, bf16[17,16,128]{2,1,0:T(8,128)(2,1)S(1)}, u32[]{:S(2)}, u32[]{:S(2)}) %collective-permute-start.8) | collective-permute-done | bytes 69664 | tf_op jit(solution)/shard_map/ppermute | solution.py:196
  56.6 1.3 %shard_map.134 = (f32[8,4096]{1,0:T(8,128)}, f32[8,128]{1,0:T(8,128)S(1)}, f32[8,128]{1,0:T(8,128)S(1)}) custom-call(s32[1]{0:T(128)S(6)} %copy.14.count.refs_0_, s32[96]{0:T(128)S(1)} %copy-done.21, s32[96]{0:T(128)S(1)} %copy-done.25, s32[1]{0:T(128)} %bitcast.1.refs_3_, bf16[96,128,128]{2,1,0:T(8,128)(2,1)S(1)} %copy-done.1, ...), custom_call_target="tpu_custom_call" | custom-call | tf_op jit(solution)/shard_map/pallas_call | solution.py:184
  57.9 0.3 collective-permute-start.12
  58.2 0.8 %collective-permute-start.11 = (f32[8,128]{1,0:T(8,128)S(1)}, f32[8,128]{1,0:T(8,128)S(1)}, u32[]{:S(2)}, u32[]{:S(2)}) collective-permute-start(f32[8,128]{1,0:T(8,128)S(1)} %get-tuple-element.25), channel_id=1, source_target_pairs={{0,8},{4,12},{8,0},{12,4},{1,9},{5,13},{9,1},{13,5},{2,10},{6,14},... | collective-permute-start | bytes 12296 | tf_op jit(solution)/shard_map/ppermute | solution.py:196
  59.0 0.8 %collective-permute-start.10 = (f32[8,128]{1,0:T(8,128)S(1)}, f32[8,128]{1,0:T(8,128)S(1)}, u32[]{:S(2)}, u32[]{:S(2)}) collective-permute-start(f32[8,128]{1,0:T(8,128)S(1)} %get-tuple-element.25), channel_id=1, source_target_pairs={{0,4},{4,0},{8,12},{12,8},{1,5},{5,1},{9,13},{13,9},{2,6},{6,2},{1... | collective-permute-start | bytes 12296 | tf_op jit(solution)/shard_map/ppermute | solution.py:196
  59.8 0.1 add_reduce_fusion
  59.9 1.1 %collective-permute-done.12 = f32[8,128]{1,0:T(8,128)S(1)} collective-permute-done((f32[8,128]{1,0:T(8,128)S(1)}, f32[8,128]{1,0:T(8,128)S(1)}, u32[]{:S(2)}, u32[]{:S(2)}) %collective-permute-start.12) | collective-permute-done | bytes 4128 | tf_op jit(solution)/shard_map/ppermute | solution.py:196
  61.0 0.8 %collective-permute-done.11 = f32[8,128]{1,0:T(8,128)S(1)} collective-permute-done((f32[8,128]{1,0:T(8,128)S(1)}, f32[8,128]{1,0:T(8,128)S(1)}, u32[]{:S(2)}, u32[]{:S(2)}) %collective-permute-start.11) | collective-permute-done | bytes 4128 | tf_op jit(solution)/shard_map/ppermute | solution.py:196
  61.8 0.1 add_reduce_fusion.1
  61.9 0.5 multiply_sqrt_fusion
  (42 shorter events, 0.1 us)
Async XLA Ops:
  1.3 1.9 %copy-start = (bf16[96,128,128]{2,1,0:T(8,128)(2,1)S(1)}, bf16[96,128,128]{2,1,0:T(8,128)(2,1)}, u32[]{:S(2)}) copy-start(bf16[96,128,128]{2,1,0:T(8,128)(2,1)} %refs_4_.7) | copy-start | bytes 9437188
  3.2 0.9 %copy-start.3 = (f32[8,4096]{1,0:T(8,128)S(1)}, f32[8,4096]{1,0:T(8,128)}, u32[]{:S(2)}) copy-start(f32[8,4096]{1,0:T(8,128)} %refs_13_.7) | copy-start | bytes 393220
  4.1 0.7 %copy-start.19 = (s32[96]{0:T(128)S(1)}, s32[96]{0:T(128)}, u32[]{:S(2)}) copy-start(s32[96]{0:T(128)} %refs_1_.7) | copy-start | bytes 1156
  4.7 0.7 %copy-start.22 = (s32[96]{0:T(128)S(1)}, s32[96]{0:T(128)}, u32[]{:S(2)}) copy-start(s32[96]{0:T(128)} %refs_2_.7) | copy-start | bytes 1156
  5.4 10.5 %copy-start.1 = (bf16[96,128,128]{2,1,0:T(8,128)(2,1)S(1)}, bf16[96,128,128]{2,1,0:T(8,128)(2,1)}, u32[]{:S(2)}) copy-start(bf16[96,128,128]{2,1,0:T(8,128)(2,1)} %refs_4_.7) | copy-start | bytes 9437188
  5.4 10.5 %copy-start.2 = (f32[8,8192]{1,0:T(8,128)S(1)}, f32[8,8192]{1,0:T(8,128)}, u32[]{:S(2)}) copy-start(f32[8,8192]{1,0:T(8,128)} %refs_13_.6) | copy-start | bytes 786436
  5.4 28.1 %copy-start.4 = (f32[8,4096]{1,0:T(8,128)S(1)}, f32[8,4096]{1,0:T(8,128)}, u32[]{:S(2)}) copy-start(f32[8,4096]{1,0:T(8,128)} %refs_13_.7) | copy-start | bytes 393220
  5.4 28.1 %copy-start.15 = (s32[4096]{0:T(1024)S(1)}, s32[4096]{0:T(1024)}, u32[]{:S(2)}) copy-start(s32[4096]{0:T(1024)} %param.19) | copy-start | bytes 49156
  6.3 1.8 %collective-permute-start = (bf16[33,16,128]{2,1,0:T(8,128)(2,1)S(1)}, bf16[33,16,128]{2,1,0:T(8,128)(2,1)S(1)}, u32[]{:S(2)}, u32[]{:S(2)}) collective-permute-start(bf16[33,16,128]{2,1,0:T(8,128)(2,1)S(1)} %shard_map.130), channel_id=1, source_target_pairs={{0,4},{4,0},{8,12},{12,8},{1,5},{5,1},{9,13},{13,9},{2,6},{6,2},{1... | collective-permute-start | bytes 405512 | tf_op jit(solution)/shard_map/ppermute | solution.py:196
  8.8 7.1 %collective-permute-start.1 = (bf16[33,16,128]{2,1,0:T(8,128)(2,1)}, bf16[33,16,128]{2,1,0:T(8,128)(2,1)}, u32[]{:S(2)}, u32[]{:S(2)}) collective-permute-start(bf16[33,16,128]{2,1,0:T(8,128)(2,1)} %add_convert_fusion.1.refs_5_), channel_id=1, source_target_pairs={{0,8},{4,12},{8,0},{12,4},{1,9},{5,13},{9,1},{13,5},{2,10},{6,14},... | collective-permute-start | bytes 405512 | tf_op jit(solution)/shard_map/ppermute | solution.py:196
  15.9 0.8 %copy-start.9 = (f32[8192]{0:T(1024)S(1)}, f32[8192]{0:T(1024)}, u32[]{:S(2)}) copy-start(f32[8192]{0:T(1024)} %param.15) | copy-start | bytes 98308
  16.6 0.8 %copy-start.11 = (f32[8192]{0:T(1024)S(1)}, f32[8192]{0:T(1024)}, u32[]{:S(2)}) copy-start(f32[8192]{0:T(1024)} %param.17) | copy-start | bytes 98308
  17.4 0.8 %copy-start.13 = (s32[8192]{0:T(1024)S(1)}, s32[8192]{0:T(1024)}, u32[]{:S(2)}) copy-start(s32[8192]{0:T(1024)} %param.18) | copy-start | bytes 98308
  18.2 0.7 %copy-start.20 = (s32[96]{0:T(128)S(1)}, s32[96]{0:T(128)}, u32[]{:S(2)}) copy-start(s32[96]{0:T(128)} %refs_1_.7) | copy-start | bytes 1156
  18.8 0.7 %copy-start.23 = (s32[96]{0:T(128)S(1)}, s32[96]{0:T(128)}, u32[]{:S(2)}) copy-start(s32[96]{0:T(128)} %refs_2_.7) | copy-start | bytes 1156
  21.9 0.7 %copy-start.7 = (f32[8,8192]{1,0:T(8,128)}, f32[8,8192]{1,0:T(8,128)S(1)}, u32[]{:S(2)}) copy-start(f32[8,8192]{1,0:T(8,128)S(1)} %get-tuple-element.19.refs_12_) | copy-start | bytes 786436
  22.6 0.6 copy-start.16
  23.2 7.6 %collective-permute-start.4 = (bf16[17,16,128]{2,1,0:T(8,128)(2,1)}, bf16[17,16,128]{2,1,0:T(8,128)(2,1)}, u32[]{:S(2)}, u32[]{:S(2)}) collective-permute-start(bf16[17,16,128]{2,1,0:T(8,128)(2,1)} %get-tuple-element.15.refs_5_), channel_id=1, source_target_pairs={{0,3},{1,2},{2,1},{3,0},{4,7},{5,6},{6,5},{7,4},{8,11},{9,10},{10,... | collective-permute-start | bytes 208904 | tf_op jit(solution)/shard_map/ppermute | solution.py:196
  27.5 6.0 %collective-permute-start.3 = (bf16[17,16,128]{2,1,0:T(8,128)(2,1)}, bf16[17,16,128]{2,1,0:T(8,128)(2,1)}, u32[]{:S(2)}, u32[]{:S(2)}) collective-permute-start(bf16[17,16,128]{2,1,0:T(8,128)(2,1)} %get-tuple-element.15.refs_5_), channel_id=1, source_target_pairs={{0,2},{1,3},{2,0},{3,1},{4,6},{5,7},{6,4},{7,5},{8,10},{9,11},{10,... | collective-permute-start | bytes 208904 | tf_op jit(solution)/shard_map/ppermute | solution.py:196
  27.5 6.0 %collective-permute-start.2 = (bf16[17,16,128]{2,1,0:T(8,128)(2,1)}, bf16[17,16,128]{2,1,0:T(8,128)(2,1)}, u32[]{:S(2)}, u32[]{:S(2)}) collective-permute-start(bf16[17,16,128]{2,1,0:T(8,128)(2,1)} %get-tuple-element.15.refs_5_), channel_id=1, source_target_pairs={{0,1},{1,0},{2,3},{3,2},{4,5},{5,4},{6,7},{7,6},{8,9},{9,8},{10,11... | collective-permute-start | bytes 208904 | tf_op jit(solution)/shard_map/ppermute | solution.py:196
  28.1 17.0 %copy-start.18 = (f32[8,128]{1,0:T(8,128)S(1)}, f32[8,128]{1,0:T(8,128)}, u32[]{:S(2)}) copy-start(f32[8,128]{1,0:T(8,128)} %copy-done.16) | copy-start | bytes 12292
  28.1 17.1 %copy-start.25 = (s32[96]{0:T(128)S(1)}, s32[96]{0:T(128)}, u32[]{:S(2)}) copy-start(s32[96]{0:T(128)} %refs_2_.7) | copy-start | bytes 1156
  33.5 0.9 %copy-start.5 = (f32[8,4096]{1,0:T(8,128)S(1)}, f32[8,4096]{1,0:T(8,128)}, u32[]{:S(2)}) copy-start(f32[8,4096]{1,0:T(8,128)} %refs_10_.3) | copy-start | bytes 393220
  34.4 0.7 %copy-start.17 = (f32[8,128]{1,0:T(8,128)S(1)}, f32[8,128]{1,0:T(8,128)}, u32[]{:S(2)}) copy-start(f32[8,128]{1,0:T(8,128)} %copy-done.16) | copy-start | bytes 12292
  35.1 0.7 %copy-start.21 = (s32[96]{0:T(128)S(1)}, s32[96]{0:T(128)}, u32[]{:S(2)}) copy-start(s32[96]{0:T(128)} %refs_1_.7) | copy-start | bytes 1156
  35.8 0.7 %copy-start.24 = (s32[96]{0:T(128)S(1)}, s32[96]{0:T(128)}, u32[]{:S(2)}) copy-start(s32[96]{0:T(128)} %refs_2_.7) | copy-start | bytes 1156
  36.4 8.7 %copy-start.8 = (f32[8,8192]{1,0:T(8,128)S(1)}, f32[8,8192]{1,0:T(8,128)}, u32[]{:S(2)}) copy-start(f32[8,8192]{1,0:T(8,128)} %copy-done.7) | copy-start | bytes 786436
  36.4 8.7 %copy-start.10 = (f32[8192]{0:T(1024)S(1)}, f32[8192]{0:T(1024)}, u32[]{:S(2)}) copy-start(f32[8192]{0:T(1024)} %param.15) | copy-start | bytes 98308
  36.4 8.7 %copy-start.12 = (f32[8192]{0:T(1024)S(1)}, f32[8192]{0:T(1024)}, u32[]{:S(2)}) copy-start(f32[8192]{0:T(1024)} %param.17) | copy-start | bytes 98308
  36.4 8.7 %copy-start.14 = (s32[8192]{0:T(1024)S(1)}, s32[8192]{0:T(1024)}, u32[]{:S(2)}) copy-start(s32[8192]{0:T(1024)} %param.18) | copy-start | bytes 98308
  37.9 18.7 %copy-start.6 = (f32[8,4096]{1,0:T(8,128)S(1)}, f32[8,4096]{1,0:T(8,128)}, u32[]{:S(2)}) copy-start(f32[8,4096]{1,0:T(8,128)} %refs_10_.3) | copy-start | bytes 393220
  37.9 1.4 %collective-permute-start.5 = (bf16[33,16,128]{2,1,0:T(8,128)(2,1)S(1)}, bf16[33,16,128]{2,1,0:T(8,128)(2,1)S(1)}, u32[]{:S(2)}, u32[]{:S(2)}) collective-permute-start(bf16[33,16,128]{2,1,0:T(8,128)(2,1)S(1)} %get-tuple-element.17), channel_id=1, source_target_pairs={{0,4},{4,0},{8,12},{12,8},{1,5},{5,1},{9,13},{13,9},{2,6},{6,2},{1... | collective-permute-start | bytes 405512 | tf_op jit(solution)/shard_map/ppermute | solution.py:196
  39.4 5.7 %collective-permute-start.6 = (bf16[33,16,128]{2,1,0:T(8,128)(2,1)S(1)}, bf16[33,16,128]{2,1,0:T(8,128)(2,1)S(1)}, u32[]{:S(2)}, u32[]{:S(2)}) collective-permute-start(bf16[33,16,128]{2,1,0:T(8,128)(2,1)S(1)} %add_convert_fusion.refs_5_), channel_id=1, source_target_pairs={{0,8},{4,12},{8,0},{12,4},{1,9},{5,13},{9,1},{13,5},{2,10},{6,14},... | collective-permute-start | bytes 405512 | tf_op jit(solution)/shard_map/ppermute | solution.py:196
  47.2 6.5 %collective-permute-start.9 = (bf16[17,16,128]{2,1,0:T(8,128)(2,1)S(1)}, bf16[17,16,128]{2,1,0:T(8,128)(2,1)S(1)}, u32[]{:S(2)}, u32[]{:S(2)}) collective-permute-start(bf16[17,16,128]{2,1,0:T(8,128)(2,1)S(1)} %get-tuple-element.21.refs_5_), channel_id=1, source_target_pairs={{0,3},{1,2},{2,1},{3,0},{4,7},{5,6},{6,5},{7,4},{8,11},{9,10},{10,... | collective-permute-start | bytes 208904 | tf_op jit(solution)/shard_map/ppermute | solution.py:196
  50.3 6.3 %collective-permute-start.8 = (bf16[17,16,128]{2,1,0:T(8,128)(2,1)S(1)}, bf16[17,16,128]{2,1,0:T(8,128)(2,1)S(1)}, u32[]{:S(2)}, u32[]{:S(2)}) collective-permute-start(bf16[17,16,128]{2,1,0:T(8,128)(2,1)S(1)} %get-tuple-element.21.refs_5_), channel_id=1, source_target_pairs={{0,2},{1,3},{2,0},{3,1},{4,6},{5,7},{6,4},{7,5},{8,10},{9,11},{10,... | collective-permute-start | bytes 208904 | tf_op jit(solution)/shard_map/ppermute | solution.py:196
  50.3 6.3 %collective-permute-start.7 = (bf16[17,16,128]{2,1,0:T(8,128)(2,1)S(1)}, bf16[17,16,128]{2,1,0:T(8,128)(2,1)S(1)}, u32[]{:S(2)}, u32[]{:S(2)}) collective-permute-start(bf16[17,16,128]{2,1,0:T(8,128)(2,1)S(1)} %get-tuple-element.21.refs_5_), channel_id=1, source_target_pairs={{0,1},{1,0},{2,3},{3,2},{4,5},{5,4},{6,7},{7,6},{8,9},{9,8},{10,11... | collective-permute-start | bytes 208904 | tf_op jit(solution)/shard_map/ppermute | solution.py:196
  57.9 3.0 %collective-permute-start.12 = (f32[8,128]{1,0:T(8,128)S(1)}, f32[8,128]{1,0:T(8,128)S(1)}, u32[]{:S(2)}, u32[]{:S(2)}) collective-permute-start(f32[8,128]{1,0:T(8,128)S(1)} %get-tuple-element.25), channel_id=1, source_target_pairs={{0,12},{4,8},{8,4},{12,0},{1,13},{5,9},{9,5},{13,1},{2,14},{6,10},... | collective-permute-start | bytes 12296 | tf_op jit(solution)/shard_map/ppermute | solution.py:196
  58.2 3.6 %collective-permute-start.11 = (f32[8,128]{1,0:T(8,128)S(1)}, f32[8,128]{1,0:T(8,128)S(1)}, u32[]{:S(2)}, u32[]{:S(2)}) collective-permute-start(f32[8,128]{1,0:T(8,128)S(1)} %get-tuple-element.25), channel_id=1, source_target_pairs={{0,8},{4,12},{8,0},{12,4},{1,9},{5,13},{9,1},{13,5},{2,10},{6,14},... | collective-permute-start | bytes 12296 | tf_op jit(solution)/shard_map/ppermute | solution.py:196
  59.0 2.8 %collective-permute-start.10 = (f32[8,128]{1,0:T(8,128)S(1)}, f32[8,128]{1,0:T(8,128)S(1)}, u32[]{:S(2)}, u32[]{:S(2)}) collective-permute-start(f32[8,128]{1,0:T(8,128)S(1)} %get-tuple-element.25), channel_id=1, source_target_pairs={{0,4},{4,0},{8,12},{12,8},{1,5},{5,1},{9,13},{13,9},{2,6},{6,2},{1... | collective-permute-start | bytes 12296 | tf_op jit(solution)/shard_map/ppermute | solution.py:196

commit v2 on v1

--- a/solution.py
+++ b/solution.py
@@ -11,10 +11,11 @@
 ETA = 0.3
 EPS = 1e-06
 PART = 32
-VMEM_LIMIT = 40 * 1024 * 1024
+VMEM_LIMIT = 8 * 1024 * 1024
 
 SMEM_SPEC = pl.BlockSpec(memory_space=pltpu.SMEM)
 VMEM_SPEC = pl.BlockSpec(memory_space=pltpu.VMEM)
+FAR_SPEC = pl.BlockSpec(memory_space=pltpu.HBM)
 
 
 def split_rows(value):
@@ -23,12 +24,15 @@
     return jnp.concatenate([high, low], axis=0)
 
 
-def join_rows(value):
-    half = value.shape[0] // 2
-    return value[:half].astype(jnp.float32) + value[half:].astype(jnp.float32)
-
-
-def tile_products(count, rows, cols, tiles, source, acc, backward):
+def fetch_grid(grid, held, sems):
+    copies = [pltpu.make_async_copy(a, b, sems.at[i]) for i, (a, b) in enumerate(zip(grid[1:], held))]
+    for copy in copies:
+        copy.start()
+    return copies
+
+
+def tile_products(grid, tiles, source, acc, backward, ready=None):
+    count, rows, cols = grid
     total, tile = tiles.shape[0], tiles.shape[1]
     spare = acc.shape[0] - 1
     scen = acc.shape[1]
@@ -38,6 +42,8 @@
     acc[...] = jnp.zeros_like(acc)
 
     def part(first, size):
+        if ready is not None:
+            ready(first)
         landing, results = [], []
         for g in range(first, first + size):
             goes = cols[g] if backward else rows[g]
@@ -80,37 +86,59 @@
     out[half] = split_rows(jnp.where(lanes == slot, norm, 0.0))
 
 
-def unpack(parts, b, half):
-    scen = parts[0].shape[1] // 2
-    rows = slice(0, scen) if b < half else slice(scen, 2 * scen)
-    k = b if b < half else b - half
-    terms = [p[k, rows, :].astype(jnp.float32) for p in parts]
+def add_up(terms):
     while len(terms) > 1:
         terms = [terms[i] + terms[i + 1] for i in range(0, len(terms), 2)]
     return terms[0]
 
 
+def unpack(parts, half):
+    scen = parts[0].shape[1] // 2
+    for k in range(half):
+        both = add_up([p[k].astype(jnp.float32) for p in parts])
+        yield k, both[:scen]
+        yield k + half, both[scen:]
+
+
 def unpack_norm(parts, half):
-    terms = [join_rows(p[half]) for p in parts]
-    while len(terms) > 1:
-        terms = [terms[i] + terms[i + 1] for i in range(0, len(terms), 2)]
-    return jnp.sum(terms[0], axis=1, keepdims=True)
-
-
-def first_kernel(count, rows, cols, tiles, dual, out, source, acc):
+    both = add_up([p[half].astype(jnp.float32) for p in parts])
+    scen = both.shape[0] // 2
+    return jnp.sum(both[:scen] + both[scen:], axis=1, keepdims=True)
+
+
+def first_kernel(*refs):
+    grid, (tiles_far, dual_far), (out, tiles), (source, acc), held, (dual, sems) = (
+        refs[:3], refs[3:5], refs[5:7], refs[7:9], refs[9:11], refs[11:]
+    )
     tile = tiles.shape[1]
+    get_dual = pltpu.make_async_copy(dual_far, dual, sems.at[2])
+    get_dual.start()
+    copies = fetch_grid(grid, held, sems)
+    get_tiles = {}
+    for n, first in enumerate(range(0, tiles.shape[0], PART)):
+        span = pl.ds(first, min(PART, tiles.shape[0] - first))
+        get_tiles[first] = pltpu.make_async_copy(tiles_far.at[span], tiles.at[span], sems.at[3 + n])
+        get_tiles[first].start()
+    get_dual.wait()
     for b in range(source.shape[0]):
         source[b] = split_rows(dual[:, b * tile : (b + 1) * tile])
-    tile_products(count, rows, cols, tiles, source, acc, True)
+    for copy in copies:
+        copy.wait()
+    tile_products((grid[0], *held), tiles, source, acc, True, lambda first: get_tiles[first].wait())
+    for first in list(get_tiles)[1:]:
+        pl.when(first >= grid[0][0])(get_tiles[first].wait)
     pack(acc, out, 0.0, 0)
 
 
-def primal_kernel(mix, n_parts, *refs):
-    count, rows, cols, slot, tiles = refs[:5]
+def primal_kernel(mix, last, n_parts, *refs):
+    grid, slot, tiles = refs[:3], refs[3], refs[4]
     parts = refs[5 : 5 + n_parts]
     refs = refs[5 + n_parts :]
     weight_in, primal_norm, cost, upper, flag, point, start = refs[:7]
-    point_out, weight_out, out, source, acc = refs[7:]
+    point_out, weight_out, out, source, acc, *held = refs[7:14]
+    sems = refs[14]
+    copies = fetch_grid(grid, held, sems)
+    made = refs[15] if last else point_out
     tile = tiles.shape[1]
     blocks = source.shape[0]
     half = blocks // 2
@@ -126,9 +154,8 @@
         tau = ETA / weight_in[:, :1]
     tau = jnp.broadcast_to(tau, (tau.shape[0], tile))
     moved_norm = jnp.zeros_like(tau)
-    for b in range(blocks):
+    for b, value in unpack(parts, half):
         lanes = slice(b * tile, (b + 1) * tile)
-        value = unpack(parts, b, half)
         old = point[:, lanes]
         moved = old - tau * (cost[b : b + 1, :] - value)
         limit = jnp.where(flag[b : b + 1, :] > 0, upper[b : b + 1, :], jnp.inf)
@@ -136,30 +163,41 @@
         step = x_hat - old
         moved_norm += step * step
         x_bar = 2.0 * x_hat - old
-        point_out[:, lanes] = mix * x_bar + (1.0 - mix) * start[:, lanes]
+        made[:, lanes] = mix * x_bar + (1.0 - mix) * start[:, lanes]
         source[b] = split_rows(x_bar)
-    tile_products(count, rows, cols, tiles, source, acc, False)
+    if last:
+        put = pltpu.make_async_copy(made, point_out, sems.at[2])
+        put.start()
+    for copy in copies:
+        copy.wait()
+    tile_products((grid[0], *held), tiles, source, acc, False)
     pack(acc, out, jnp.sum(moved_norm, axis=1, keepdims=True), slot[0])
+    if last:
+        put.wait()
 
 
 def dual_kernel(mix, last, n_parts, *refs):
-    count, rows, cols, slot, tiles = refs[:5]
-    parts = refs[5 : 5 + n_parts]
-    refs = refs[5 + n_parts :]
+    if last:
+        slot, refs = refs[0], refs[1:]
+    else:
+        grid, slot, tiles, refs = refs[:3], refs[3], refs[4], refs[5:]
+    parts = refs[:n_parts]
+    refs = refs[n_parts:]
     weight, demand, flag, dual, start = refs[:5]
     if last:
-        dual_out, primal_norm, out = refs[5:]
+        dual_out, primal_norm, out, made, sems = refs[5:]
     else:
-        dual_out, primal_norm, out, source, acc = refs[5:]
+        dual_out, primal_norm, out, source, acc, *held = refs[5:12]
+        copies = fetch_grid(grid, held, refs[12])
+        made = dual_out
     tile = flag.shape[1]
     blocks = flag.shape[0]
     half = blocks // 2
     primal_norm[...] = jnp.broadcast_to(unpack_norm(parts, half), primal_norm.shape)
     sigma = ETA * weight[...]
     moved_norm = jnp.zeros_like(sigma)
-    for b in range(blocks):
+    for b, value in unpack(parts, half):
         lanes = slice(b * tile, (b + 1) * tile)
-        value = unpack(parts, b, half)
         old = dual[:, lanes]
         moved = old + sigma * (demand[:, lanes] - value)
         floor = jnp.where(flag[b : b + 1, :] > 0, 0.0, -jnp.inf)
@@ -167,37 +205,42 @@
         step = y_hat - old
         moved_norm += step * step
         new = mix * (2.0 * y_hat - old) + (1.0 - mix) * start[:, lanes]
-        dual_out[:, lanes] = new
+        made[:, lanes] = new
         if not last:
             source[b] = split_rows(new)
+    if last:
+        put = pltpu.make_async_copy(made, dual_out, sems.at[0])
+        put.start()
     dual_norm = jnp.sum(moved_norm, axis=1, keepdims=True)
     if last:
         lanes = lax.broadcasted_iota(jnp.int32, out.shape, 1)
         out[...] = jnp.where(lanes == slot[0], dual_norm, 0.0)
+        put.wait()
     else:
-        tile_products(count, rows, cols, tiles, source, acc, True)
+        for copy in copies:
+            copy.wait()
+        tile_products((grid[0], *held), tiles, source, acc, True)
         pack(acc, out, dual_norm, slot[0])
 
 
-def call(kernel, inputs, outputs, scratch, scalars):
-    specs = [SMEM_SPEC] * scalars + [VMEM_SPEC] * (len(inputs) - scalars)
+def call(kernel, inputs, in_specs, outputs, out_specs, scratch):
     return pl.pallas_call(
         kernel,
         out_shape=outputs,
-        in_specs=specs,
-        out_specs=[VMEM_SPEC] * len(outputs),
+        in_specs=in_specs,
+        out_specs=out_specs,
         scratch_shapes=scratch,
         compiler_params=pltpu.CompilerParams(vmem_limit_bytes=VMEM_LIMIT),
     )(*inputs)
 
 
+def far(value):
+    return pltpu.with_memory_space_constraint(value, pltpu.HBM)
+
+
 def swap(value, axis, mask):
     size = lax.axis_size(axis)
     return lax.ppermute(value, axis, [(i, i ^ mask) for i in range(size)])
-
-
-def plus(a, b):
-    return (a.astype(jnp.float32) + b.astype(jnp.float32)).astype(a.dtype)
 
 
 def butterfly(value, axis, radix):
@@ -206,10 +249,7 @@
         return [lax.psum(value.astype(jnp.float32), axis)]
     mask, parts = 1, [value]
     while mask < size:
-        terms = [p.astype(jnp.float32) for p in parts]
-        while len(terms) > 1:
-            terms = [terms[i] + terms[i + 1] for i in range(0, len(terms), 2)]
-        total = terms[0].astype(value.dtype)
+        total = add_up([p.astype(jnp.float32) for p in parts]).astype(value.dtype)
         span = min(radix, size // mask)
         parts = [total] + [swap(total, axis, mask * k) for k in range(1, span)]
         mask *= span
@@ -238,45 +278,70 @@
     row_flag = row_flag.reshape(row_blocks, tile)
     row_slot = lax.axis_index("rowblk").astype(jnp.int32).reshape(1)
     col_slot = lax.axis_index("colblk").astype(jnp.int32).reshape(1)
-    grid = [tile_count, tile_row, tile_col]
-
+    grid = [tile_count, far(tile_row), far(tile_col)]
+
+    total = tile_row.shape[0]
     small = jax.ShapeDtypeStruct((scen, tile), f32)
     col_parts = jax.ShapeDtypeStruct((col_blocks // 2 + 1, 2 * scen, tile), bf16)
     row_parts = jax.ShapeDtypeStruct((row_blocks // 2 + 1, 2 * scen, tile), bf16)
     primal = jax.ShapeDtypeStruct(primal_start.shape, f32)
     dual_like = jax.ShapeDtypeStruct(dual_start.shape, f32)
+    held = [pltpu.SMEM((total,), jnp.int32)] * 2
+    sems = pltpu.SemaphoreType.DMA((3 + pl.cdiv(total, PART),))
     to_cols = [
         pltpu.VMEM((row_blocks, 2 * scen, tile), bf16),
         pltpu.VMEM((col_blocks + 1, scen, tile), f32),
+        *held,
     ]
     to_rows = [
         pltpu.VMEM((col_blocks, 2 * scen, tile), bf16),
         pltpu.VMEM((row_blocks + 1, scen, tile), f32),
+        *held,
     ]
 
     point, dual = primal_start, dual_start
     weight = jnp.ones((scen, tile), f32)
     primal_norm = weight
-    (terms,) = call(first_kernel, [*grid, tiles, dual], [col_parts], to_cols, 3)
+    terms, tiles = call(
+        first_kernel,
+        [*grid, far(tiles), far(dual)],
+        [SMEM_SPEC] + [FAR_SPEC] * 4,
+        [col_parts, pltpu.VMEM(tiles.shape, tiles.dtype)],
+        [VMEM_SPEC] * 2,
+        [*to_cols, pltpu.VMEM(dual.shape, f32), sems],
+    )
     for step in range(ITERS):
         mix = (step + 1.0) / (step + 2.0)
         last = step == ITERS - 1
         parts = butterfly(terms, "rowblk", 2)
         point, weight, terms = call(
-            functools.partial(primal_kernel, mix, len(parts)),
+            functools.partial(primal_kernel, mix, last, len(parts)),
             [*grid, col_slot, tiles, *parts, weight, primal_norm, cost, upper, col_flag, point, primal_start],
+            [SMEM_SPEC] + [FAR_SPEC] * 2 + [SMEM_SPEC] + [VMEM_SPEC] * (8 + len(parts)),
             [primal, small, row_parts],
-            to_rows,
-            4,
+            [FAR_SPEC if last else VMEM_SPEC, VMEM_SPEC, VMEM_SPEC],
+            [*to_rows, sems] + [pltpu.VMEM(primal.shape, f32)] * last,
         )
         parts = butterfly(terms, "colblk", 4)
-        dual, primal_norm, terms = call(
-            functools.partial(dual_kernel, mix, last, len(parts)),
-            [*grid, row_slot, tiles, *parts, weight, demand, row_flag, dual, dual_start],
-            [dual_like, small, small if last else col_parts],
-            [] if last else to_cols,
-            4,
-        )
+        vectors = [*parts, weight, demand, row_flag, dual, dual_start]
+        if last:
+            dual, primal_norm, terms = call(
+                functools.partial(dual_kernel, mix, last, len(parts)),
+                [row_slot, *vectors],
+                [SMEM_SPEC] + [VMEM_SPEC] * len(vectors),
+                [dual_like, small, small],
+                [FAR_SPEC, VMEM_SPEC, VMEM_SPEC],
+                [pltpu.VMEM(dual.shape, f32), sems],
+            )
+        else:
+            dual, primal_norm, terms = call(
+                functools.partial(dual_kernel, mix, last, len(parts)),
+                [*grid, row_slot, tiles, *vectors],
+                [SMEM_SPEC] + [FAR_SPEC] * 2 + [SMEM_SPEC] + [VMEM_SPEC] * (1 + len(vectors)),
+                [dual_like, small, col_parts],
+                [VMEM_SPEC] * 3,
+                [*to_cols, sems],
+            )
     parts = butterfly(terms, "rowblk", 4)
     dual_norm = jnp.sum(functools.reduce(jnp.add, parts), axis=1)
     ratio = (dual_norm + EPS) / (primal_norm[:, 0] + EPS)

time: 62.9 us -> 56.4 us (0.90)
  local copies, waits for them, and re-layouts: 12 us -> 5.3 us
  Pallas kernels: 8.2 us -> 10.2 us
  waiting for transfers between devices: 22.9 us -> 21.7 us
    unnamed x52 -> x32, local copies, waits for them, and re-layouts: 11.9 us -> 5.19 us
    pallas_call x5, Pallas kernels: 8.2 us -> 10.2 us  [call(): pl.pallas_call(kernel, out_shape=outputs, in_specs=in_specs, out_specs=ou...]
    ppermute x13, waiting for transfers between devices: 22.9 us -> 21.7 us  [swap(): return lax.ppermute(value, axis, [(i, i ^ mask) for i in range(size)])]
  transfers between devices with their start and end apart: 13 -> 13, of which waited for: 10 -> 11; matrix products, arithmetic and copies ran while one was open for 0% -> 0% of each run, Pallas kernels for 0% -> 0%
where the time goes in v2:
time: 56.4 us; the launch traced here: 56.1 us
  waiting for transfers between devices  21.7 us (38%)
  starting transfers between devices  16 us (28%)
  Pallas kernels  10.2 us (18%)
  local copies, waits for them, and re-layouts  5.3 us (9%)
  other arithmetic  1.51 us (3%)
  between operations  1.46 us (3%)
    ppermute x13, waiting for transfers between devices, swap(): return lax.ppermute(value, axis, [(i, i ^ mask) for i in range(size)])  21.7 us
    ppermute x13, starting transfers between devices, swap(): return lax.ppermute(value, axis, [(i, i ^ mask) for i in range(size)])  16 us
    pallas_call x5, Pallas kernels, call(): pl.pallas_call(kernel, out_shape=outputs, in_specs=in_specs, out_specs=ou...  10.2 us
    unnamed x32, local copies, waits for them, and re-layouts  5.19 us
  transfers between devices with their start and end apart: 13, of which 11 were waited for; matrix products, arithmetic and copies ran while one was open for 0% of the time, Pallas kernels for 0%

profile of v2, /device:TPU:0, one launch (start us, length us, event | category | flops | bytes accessed | tf_op | source)
XLA Modules:
  0.0 56.1 jit_solution(4529628625851436489)
XLA Ops:
  0.6 0.0 copy-start
  1.4 2.1 %shard_map.130 = (bf16[33,16,128]{2,1,0:T(8,128)(2,1)S(1)}, bf16[96,128,128]{2,1,0:T(8,128)(2,1)S(1)}) custom-call(s32[1]{0:T(128)S(6)} %copy.14.refs_0_, s32[96]{0:T(128)} %refs_1_.7, s32[96]{0:T(128)} %refs_2_.7, bf16[96,128,128]{2,1,0:T(8,128)(2,1)} %refs_3_.1, f32[8,4096]{1,0:T(8,128)} %refs_9_.1), custom_call_target="tpu_custom_call" | custom-call | tf_op jit(solution)/shard_map/pallas_call | solution.py:227
  3.4 0.5 collective-permute-start
  3.9 1.0 %collective-permute-done = bf16[33,16,128]{2,1,0:T(8,128)(2,1)S(1)} collective-permute-done((bf16[33,16,128]{2,1,0:T(8,128)(2,1)S(1)}, bf16[33,16,128]{2,1,0:T(8,128)(2,1)S(1)}, u32[]{:S(2)}, u32[]{:S(2)}) %collective-permute-start) | collective-permute-done | bytes 135200 | tf_op jit(solution)/shard_map/ppermute | solution.py:243
  4.9 0.7 %add_convert_fusion.1.refs_5_ = bf16[33,16,128]{2,1,0:T(8,128)(2,1)} fusion(bf16[33,16,128]{2,1,0:T(8,128)(2,1)S(1)} %collective-permute-done, bf16[33,16,128]{2,1,0:T(8,128)(2,1)S(1)} %get-tuple-element.18), kind=kLoop, calls=%fused_computation.1 | loop fusion | flops 270336 | bytes 405504 | tf_op jit(solution)/shard_map/convert_element_type | solution.py:252
  5.6 2.8 %collective-permute-start.1 = (bf16[33,16,128]{2,1,0:T(8,128)(2,1)}, bf16[33,16,128]{2,1,0:T(8,128)(2,1)}, u32[]{:S(2)}, u32[]{:S(2)}) collective-permute-start(bf16[33,16,128]{2,1,0:T(8,128)(2,1)} %add_convert_fusion.1.refs_5_), channel_id=1, source_target_pairs={{0,8},{4,12},{8,0},{12,4},{1,9},{5,13},{9,1},{13,5},{2,10},{6,14},... | collective-permute-start | bytes 405512 | tf_op jit(solution)/shard_map/ppermute | solution.py:243
  8.4 4.2 %collective-permute-done.1.refs_6_ = bf16[33,16,128]{2,1,0:T(8,128)(2,1)} collective-permute-done((bf16[33,16,128]{2,1,0:T(8,128)(2,1)}, bf16[33,16,128]{2,1,0:T(8,128)(2,1)}, u32[]{:S(2)}, u32[]{:S(2)}) %collective-permute-start.1) | collective-permute-done | bytes 135200 | tf_op jit(solution)/shard_map/ppermute | solution.py:243
  12.7 0.8 %copy-done.6 = f32[8192]{0:T(1024)S(1)} copy-done((f32[8192]{0:T(1024)S(1)}, f32[8192]{0:T(1024)}, u32[]{:S(2)}) %copy-start.6) | copy-done | bytes 32792
  13.4 0.8 %copy-done.8 = f32[8192]{0:T(1024)S(1)} copy-done((f32[8192]{0:T(1024)S(1)}, f32[8192]{0:T(1024)}, u32[]{:S(2)}) %copy-start.8) | copy-done | bytes 32792
  14.2 0.8 %copy-done.10 = s32[8192]{0:T(1024)S(1)} copy-done((s32[8192]{0:T(1024)S(1)}, s32[8192]{0:T(1024)}, u32[]{:S(2)}) %copy-start.10) | copy-done | bytes 32792
  14.9 3.2 %shard_map.131 = (f32[8,8192]{1,0:T(8,128)S(1)}, f32[8,128]{1,0:T(8,128)S(1)}, bf16[17,16,128]{2,1,0:T(8,128)(2,1)}) custom-call(s32[1]{0:T(128)S(6)} %copy.14.refs_0_, s32[96]{0:T(128)} %refs_1_.7, s32[96]{0:T(128)} %refs_2_.7, s32[1]{0:T(128)} %bitcast.refs_3_, bf16[96,128,128]{2,1,0:T(8,128)(2,1)S(1)} %get-tuple-element.17.refs_4_, ...), custom_call_target="tpu_custom_call" | custom-call | tf_op jit(solution)/shard_map/pallas_call | solution.py:227
  18.2 0.0 copy-start.4
  18.2 0.7 %copy-done.4 = f32[8,8192]{1,0:T(8,128)} copy-done((f32[8,8192]{1,0:T(8,128)}, f32[8,8192]{1,0:T(8,128)S(1)}, u32[]{:S(2)}) %copy-start.4) | copy-done | bytes 262168
  18.9 0.6 %copy-done.13 = f32[8,128]{1,0:T(8,128)} copy-done((f32[8,128]{1,0:T(8,128)}, f32[8,128]{1,0:T(8,128)S(1)}, u32[]{:S(2)}) %copy-start.13) | copy-done | bytes 4120
  19.5 3.5 %collective-permute-start.4 = (bf16[17,16,128]{2,1,0:T(8,128)(2,1)}, bf16[17,16,128]{2,1,0:T(8,128)(2,1)}, u32[]{:S(2)}, u32[]{:S(2)}) collective-permute-start(bf16[17,16,128]{2,1,0:T(8,128)(2,1)} %get-tuple-element.19.refs_5_), channel_id=1, source_target_pairs={{0,3},{1,2},{2,1},{3,0},{4,7},{5,6},{6,5},{7,4},{8,11},{9,10},{10,... | collective-permute-start | bytes 208904 | tf_op jit(solution)/shard_map/ppermute | solution.py:243
  23.0 0.0 collective-permute-start.3
  23.0 0.9 %collective-permute-start.2 = (bf16[17,16,128]{2,1,0:T(8,128)(2,1)}, bf16[17,16,128]{2,1,0:T(8,128)(2,1)}, u32[]{:S(2)}, u32[]{:S(2)}) collective-permute-start(bf16[17,16,128]{2,1,0:T(8,128)(2,1)} %get-tuple-element.19.refs_5_), channel_id=1, source_target_pairs={{0,1},{1,0},{2,3},{3,2},{4,5},{5,4},{6,7},{7,6},{8,9},{9,8},{10,11... | collective-permute-start | bytes 208904 | tf_op jit(solution)/shard_map/ppermute | solution.py:243
  23.9 2.8 %collective-permute-done.4.refs_8_ = bf16[17,16,128]{2,1,0:T(8,128)(2,1)} collective-permute-done((bf16[17,16,128]{2,1,0:T(8,128)(2,1)}, bf16[17,16,128]{2,1,0:T(8,128)(2,1)}, u32[]{:S(2)}, u32[]{:S(2)}) %collective-permute-start.4) | collective-permute-done | bytes 69664 | tf_op jit(solution)/shard_map/ppermute | solution.py:243
  26.7 2.2 %collective-permute-done.3.refs_7_ = bf16[17,16,128]{2,1,0:T(8,128)(2,1)} collective-permute-done((bf16[17,16,128]{2,1,0:T(8,128)(2,1)}, bf16[17,16,128]{2,1,0:T(8,128)(2,1)}, u32[]{:S(2)}, u32[]{:S(2)}) %collective-permute-start.3) | collective-permute-done | bytes 69664 | tf_op jit(solution)/shard_map/ppermute | solution.py:243
  28.9 0.1 collective-permute-done.2.refs_6_
  29.0 0.9 %copy-done.2 = f32[8,4096]{1,0:T(8,128)S(1)} copy-done((f32[8,4096]{1,0:T(8,128)S(1)}, f32[8,4096]{1,0:T(8,128)}, u32[]{:S(2)}) %copy-start.2) | copy-done | bytes 131096
  29.9 0.7 %copy-done.14 = f32[8,128]{1,0:T(8,128)S(1)} copy-done((f32[8,128]{1,0:T(8,128)S(1)}, f32[8,128]{1,0:T(8,128)}, u32[]{:S(2)}) %copy-start.14) | copy-done | bytes 4120
  30.6 2.4 %shard_map.132 = (f32[8,4096]{1,0:T(8,128)S(1)}, f32[8,128]{1,0:T(8,128)S(1)}, bf16[33,16,128]{2,1,0:T(8,128)(2,1)S(1)}) custom-call(s32[1]{0:T(128)S(6)} %copy.14.refs_0_, s32[96]{0:T(128)} %refs_1_.7, s32[96]{0:T(128)} %refs_2_.7, s32[1]{0:T(128)} %bitcast.1.refs_3_.refs_0_, bf16[96,128,128]{2,1,0:T(8,128)(2,1)S(1)} %get-tuple-element.17.refs_4_, ...), custom_call_target="tpu_custom_call" | custom-call | tf_op jit(solution)/shard_map/pallas_call | solution.py:227
  33.0 0.0 copy-start.3
  33.0 0.1 collective-permute-start.5
  33.1 1.3 %collective-permute-done.5 = bf16[33,16,128]{2,1,0:T(8,128)(2,1)S(1)} collective-permute-done((bf16[33,16,128]{2,1,0:T(8,128)(2,1)S(1)}, bf16[33,16,128]{2,1,0:T(8,128)(2,1)S(1)}, u32[]{:S(2)}, u32[]{:S(2)}) %collective-permute-start.5) | collective-permute-done | bytes 135200 | tf_op jit(solution)/shard_map/ppermute | solution.py:243
  34.5 1.8 %collective-permute-start.6 = (bf16[33,16,128]{2,1,0:T(8,128)(2,1)S(1)}, bf16[33,16,128]{2,1,0:T(8,128)(2,1)S(1)}, u32[]{:S(2)}, u32[]{:S(2)}) collective-permute-start(bf16[33,16,128]{2,1,0:T(8,128)(2,1)S(1)} %add_convert_fusion.refs_5_), channel_id=1, source_target_pairs={{0,8},{4,12},{8,0},{12,4},{1,9},{5,13},{9,1},{13,5},{2,10},{6,14},... | collective-permute-start | bytes 405512 | tf_op jit(solution)/shard_map/ppermute | solution.py:243
  36.3 3.9 %collective-permute-done.6.refs_6_ = bf16[33,16,128]{2,1,0:T(8,128)(2,1)S(1)} collective-permute-done((bf16[33,16,128]{2,1,0:T(8,128)(2,1)S(1)}, bf16[33,16,128]{2,1,0:T(8,128)(2,1)S(1)}, u32[]{:S(2)}, u32[]{:S(2)}) %collective-permute-start.6) | collective-permute-done | bytes 135200 | tf_op jit(solution)/shard_map/ppermute | solution.py:243
  40.2 0.0 copy-done.7
  40.2 1.7 %shard_map.133 = (f32[8,8192]{1,0:T(8,128)}, f32[8,128]{1,0:T(8,128)S(1)}, bf16[17,16,128]{2,1,0:T(8,128)(2,1)S(1)}) custom-call(s32[1]{0:T(128)S(6)} %copy.14.refs_0_, s32[96]{0:T(128)} %refs_1_.7, s32[96]{0:T(128)} %refs_2_.7, s32[1]{0:T(128)} %bitcast.refs_3_, bf16[96,128,128]{2,1,0:T(8,128)(2,1)S(1)} %get-tuple-element.17.refs_4_, ...), custom_call_target="tpu_custom_call" | custom-call | tf_op jit(solution)/shard_map/pallas_call | solution.py:227
  41.9 1.9 %collective-permute-start.9 = (bf16[17,16,128]{2,1,0:T(8,128)(2,1)S(1)}, bf16[17,16,128]{2,1,0:T(8,128)(2,1)S(1)}, u32[]{:S(2)}, u32[]{:S(2)}) collective-permute-start(bf16[17,16,128]{2,1,0:T(8,128)(2,1)S(1)} %get-tuple-element.25.refs_1_), channel_id=1, source_target_pairs={{0,3},{1,2},{2,1},{3,0},{4,7},{5,6},{6,5},{7,4},{8,11},{9,10},{10,... | collective-permute-start | bytes 208904 | tf_op jit(solution)/shard_map/ppermute | solution.py:243
  43.7 0.0 collective-permute-start.8
  43.8 2.6 %collective-permute-start.7 = (bf16[17,16,128]{2,1,0:T(8,128)(2,1)S(1)}, bf16[17,16,128]{2,1,0:T(8,128)(2,1)S(1)}, u32[]{:S(2)}, u32[]{:S(2)}) collective-permute-start(bf16[17,16,128]{2,1,0:T(8,128)(2,1)S(1)} %get-tuple-element.25.refs_1_), channel_id=1, source_target_pairs={{0,1},{1,0},{2,3},{3,2},{4,5},{5,4},{6,7},{7,6},{8,9},{9,8},{10,11... | collective-permute-start | bytes 208904 | tf_op jit(solution)/shard_map/ppermute | solution.py:243
  46.3 0.1 slice_reduce_fusion
  46.5 2.2 %collective-permute-done.9.refs_4_ = bf16[17,16,128]{2,1,0:T(8,128)(2,1)S(1)} collective-permute-done((bf16[17,16,128]{2,1,0:T(8,128)(2,1)S(1)}, bf16[17,16,128]{2,1,0:T(8,128)(2,1)S(1)}, u32[]{:S(2)}, u32[]{:S(2)}) %collective-permute-start.9) | collective-permute-done | bytes 69664 | tf_op jit(solution)/shard_map/ppermute | solution.py:243
  48.7 1.8 %collective-permute-done.8.refs_3_ = bf16[17,16,128]{2,1,0:T(8,128)(2,1)S(1)} collective-permute-done((bf16[17,16,128]{2,1,0:T(8,128)(2,1)S(1)}, bf16[17,16,128]{2,1,0:T(8,128)(2,1)S(1)}, u32[]{:S(2)}, u32[]{:S(2)}) %collective-permute-start.8) | collective-permute-done | bytes 69664 | tf_op jit(solution)/shard_map/ppermute | solution.py:243
  50.5 0.0 collective-permute-done.7.refs_2_
  50.5 0.0 copy-done.3
  50.5 0.8 %shard_map.134 = (f32[8,4096]{1,0:T(8,128)}, f32[8,128]{1,0:T(8,128)S(1)}, f32[8,128]{1,0:T(8,128)S(1)}) custom-call(s32[1]{0:T(128)} %bitcast.1.refs_3_.refs_0_, bf16[17,16,128]{2,1,0:T(8,128)(2,1)S(1)} %get-tuple-element.25.refs_1_, bf16[17,16,128]{2,1,0:T(8,128)(2,1)S(1)} %collective-permute-done.7.refs_2_, ...), custom_call_target="tpu_custom_call" | custom-call | tf_op jit(solution)/shard_map/pallas_call | solution.py:227
  51.3 0.5 collective-permute-start.12
  51.8 1.4 %collective-permute-start.11 = (f32[8,128]{1,0:T(8,128)S(1)}, f32[8,128]{1,0:T(8,128)S(1)}, u32[]{:S(2)}, u32[]{:S(2)}) collective-permute-start(f32[8,128]{1,0:T(8,128)S(1)} %get-tuple-element.29), channel_id=1, source_target_pairs={{0,8},{4,12},{8,0},{12,4},{1,9},{5,13},{9,1},{13,5},{2,10},{6,14},... | collective-permute-start | bytes 12296 | tf_op jit(solution)/shard_map/ppermute | solution.py:243
  53.2 0.1 collective-permute-start.10
  53.3 0.1 add_reduce_fusion
  53.4 1.0 %collective-permute-done.12 = f32[8,128]{1,0:T(8,128)S(1)} collective-permute-done((f32[8,128]{1,0:T(8,128)S(1)}, f32[8,128]{1,0:T(8,128)S(1)}, u32[]{:S(2)}, u32[]{:S(2)}) %collective-permute-start.12) | collective-permute-done | bytes 4128 | tf_op jit(solution)/shard_map/ppermute | solution.py:243
  54.4 1.0 %collective-permute-done.11 = f32[8,128]{1,0:T(8,128)S(1)} collective-permute-done((f32[8,128]{1,0:T(8,128)S(1)}, f32[8,128]{1,0:T(8,128)S(1)}, u32[]{:S(2)}, u32[]{:S(2)}) %collective-permute-start.11) | collective-permute-done | bytes 4128 | tf_op jit(solution)/shard_map/ppermute | solution.py:243
  55.4 0.0 collective-permute-done.10
  55.4 0.1 add_reduce_fusion.1
  55.6 0.5 multiply_sqrt_fusion
  (22 shorter events, 0.1 us)
Async XLA Ops:
  0.6 12.0 %copy-start = (f32[8,8192]{1,0:T(8,128)S(1)}, f32[8,8192]{1,0:T(8,128)}, u32[]{:S(2)}) copy-start(f32[8,8192]{1,0:T(8,128)} %refs_13_.5) | copy-start | bytes 786436
  1.3 27.7 %copy-start.1 = (f32[8,4096]{1,0:T(8,128)S(1)}, f32[8,4096]{1,0:T(8,128)}, u32[]{:S(2)}) copy-start(f32[8,4096]{1,0:T(8,128)} %refs_9_.1) | copy-start | bytes 393220
  1.3 27.7 %copy-start.12 = (s32[4096]{0:T(1024)S(1)}, s32[4096]{0:T(1024)}, u32[]{:S(2)}) copy-start(s32[4096]{0:T(1024)} %param.19) | copy-start | bytes 49156
  3.4 1.5 %collective-permute-start = (bf16[33,16,128]{2,1,0:T(8,128)(2,1)S(1)}, bf16[33,16,128]{2,1,0:T(8,128)(2,1)S(1)}, u32[]{:S(2)}, u32[]{:S(2)}) collective-permute-start(bf16[33,16,128]{2,1,0:T(8,128)(2,1)S(1)} %get-tuple-element.18), channel_id=1, source_target_pairs={{0,4},{4,0},{8,12},{12,8},{1,5},{5,1},{9,13},{13,9},{2,6},{6,2},{1... | collective-permute-start | bytes 405512 | tf_op jit(solution)/shard_map/ppermute | solution.py:243
  5.6 7.1 %collective-permute-start.1 = (bf16[33,16,128]{2,1,0:T(8,128)(2,1)}, bf16[33,16,128]{2,1,0:T(8,128)(2,1)}, u32[]{:S(2)}, u32[]{:S(2)}) collective-permute-start(bf16[33,16,128]{2,1,0:T(8,128)(2,1)} %add_convert_fusion.1.refs_5_), channel_id=1, source_target_pairs={{0,8},{4,12},{8,0},{12,4},{1,9},{5,13},{9,1},{13,5},{2,10},{6,14},... | collective-permute-start | bytes 405512 | tf_op jit(solution)/shard_map/ppermute | solution.py:243
  12.7 0.8 %copy-start.6 = (f32[8192]{0:T(1024)S(1)}, f32[8192]{0:T(1024)}, u32[]{:S(2)}) copy-start(f32[8192]{0:T(1024)} %param.15) | copy-start | bytes 98308
  13.4 0.8 %copy-start.8 = (f32[8192]{0:T(1024)S(1)}, f32[8192]{0:T(1024)}, u32[]{:S(2)}) copy-start(f32[8192]{0:T(1024)} %param.17) | copy-start | bytes 98308
  14.2 0.8 %copy-start.10 = (s32[8192]{0:T(1024)S(1)}, s32[8192]{0:T(1024)}, u32[]{:S(2)}) copy-start(s32[8192]{0:T(1024)} %param.18) | copy-start | bytes 98308
  18.2 0.7 %copy-start.4 = (f32[8,8192]{1,0:T(8,128)}, f32[8,8192]{1,0:T(8,128)S(1)}, u32[]{:S(2)}) copy-start(f32[8,8192]{1,0:T(8,128)S(1)} %get-tuple-element.23.refs_12_) | copy-start | bytes 786436
  18.9 0.6 %copy-start.13 = (f32[8,128]{1,0:T(8,128)}, f32[8,128]{1,0:T(8,128)S(1)}, u32[]{:S(2)}) copy-start(f32[8,128]{1,0:T(8,128)S(1)} %get-tuple-element.20.refs_9_.refs_7_) | copy-start | bytes 12292
  19.5 7.2 %collective-permute-start.4 = (bf16[17,16,128]{2,1,0:T(8,128)(2,1)}, bf16[17,16,128]{2,1,0:T(8,128)(2,1)}, u32[]{:S(2)}, u32[]{:S(2)}) collective-permute-start(bf16[17,16,128]{2,1,0:T(8,128)(2,1)} %get-tuple-element.19.refs_5_), channel_id=1, source_target_pairs={{0,3},{1,2},{2,1},{3,0},{4,7},{5,6},{6,5},{7,4},{8,11},{9,10},{10,... | collective-permute-start | bytes 208904 | tf_op jit(solution)/shard_map/ppermute | solution.py:243
  23.0 6.0 %collective-permute-start.3 = (bf16[17,16,128]{2,1,0:T(8,128)(2,1)}, bf16[17,16,128]{2,1,0:T(8,128)(2,1)}, u32[]{:S(2)}, u32[]{:S(2)}) collective-permute-start(bf16[17,16,128]{2,1,0:T(8,128)(2,1)} %get-tuple-element.19.refs_5_), channel_id=1, source_target_pairs={{0,2},{1,3},{2,0},{3,1},{4,6},{5,7},{6,4},{7,5},{8,10},{9,11},{10,... | collective-permute-start | bytes 208904 | tf_op jit(solution)/shard_map/ppermute | solution.py:243
  23.0 6.0 %collective-permute-start.2 = (bf16[17,16,128]{2,1,0:T(8,128)(2,1)}, bf16[17,16,128]{2,1,0:T(8,128)(2,1)}, u32[]{:S(2)}, u32[]{:S(2)}) collective-permute-start(bf16[17,16,128]{2,1,0:T(8,128)(2,1)} %get-tuple-element.19.refs_5_), channel_id=1, source_target_pairs={{0,1},{1,0},{2,3},{3,2},{4,5},{5,4},{6,7},{7,6},{8,9},{9,8},{10,11... | collective-permute-start | bytes 208904 | tf_op jit(solution)/shard_map/ppermute | solution.py:243
  23.9 16.3 %copy-start.15 = (f32[8,128]{1,0:T(8,128)S(1)}, f32[8,128]{1,0:T(8,128)}, u32[]{:S(2)}) copy-start(f32[8,128]{1,0:T(8,128)} %copy-done.13) | copy-start | bytes 12292
  29.0 0.9 %copy-start.2 = (f32[8,4096]{1,0:T(8,128)S(1)}, f32[8,4096]{1,0:T(8,128)}, u32[]{:S(2)}) copy-start(f32[8,4096]{1,0:T(8,128)} %refs_6_.1) | copy-start | bytes 393220
  29.9 0.7 %copy-start.14 = (f32[8,128]{1,0:T(8,128)S(1)}, f32[8,128]{1,0:T(8,128)}, u32[]{:S(2)}) copy-start(f32[8,128]{1,0:T(8,128)} %copy-done.13) | copy-start | bytes 12292
  30.6 9.6 %copy-start.5 = (f32[8,8192]{1,0:T(8,128)S(1)}, f32[8,8192]{1,0:T(8,128)}, u32[]{:S(2)}) copy-start(f32[8,8192]{1,0:T(8,128)} %copy-done.4) | copy-start | bytes 786436
  30.6 9.6 %copy-start.7 = (f32[8192]{0:T(1024)S(1)}, f32[8192]{0:T(1024)}, u32[]{:S(2)}) copy-start(f32[8192]{0:T(1024)} %param.15) | copy-start | bytes 98308
  30.6 9.6 %copy-start.9 = (f32[8192]{0:T(1024)S(1)}, f32[8192]{0:T(1024)}, u32[]{:S(2)}) copy-start(f32[8192]{0:T(1024)} %param.17) | copy-start | bytes 98308
  30.6 9.6 %copy-start.11 = (s32[8192]{0:T(1024)S(1)}, s32[8192]{0:T(1024)}, u32[]{:S(2)}) copy-start(s32[8192]{0:T(1024)} %param.18) | copy-start | bytes 98308
  33.0 17.5 %copy-start.3 = (f32[8,4096]{1,0:T(8,128)S(1)}, f32[8,4096]{1,0:T(8,128)}, u32[]{:S(2)}) copy-start(f32[8,4096]{1,0:T(8,128)} %refs_6_.1) | copy-start | bytes 393220
  33.0 1.4 %collective-permute-start.5 = (bf16[33,16,128]{2,1,0:T(8,128)(2,1)S(1)}, bf16[33,16,128]{2,1,0:T(8,128)(2,1)S(1)}, u32[]{:S(2)}, u32[]{:S(2)}) collective-permute-start(bf16[33,16,128]{2,1,0:T(8,128)(2,1)S(1)} %get-tuple-element.21), channel_id=1, source_target_pairs={{0,4},{4,0},{8,12},{12,8},{1,5},{5,1},{9,13},{13,9},{2,6},{6,2},{1... | collective-permute-start | bytes 405512 | tf_op jit(solution)/shard_map/ppermute | solution.py:243
  34.5 5.7 %collective-permute-start.6 = (bf16[33,16,128]{2,1,0:T(8,128)(2,1)S(1)}, bf16[33,16,128]{2,1,0:T(8,128)(2,1)S(1)}, u32[]{:S(2)}, u32[]{:S(2)}) collective-permute-start(bf16[33,16,128]{2,1,0:T(8,128)(2,1)S(1)} %add_convert_fusion.refs_5_), channel_id=1, source_target_pairs={{0,8},{4,12},{8,0},{12,4},{1,9},{5,13},{9,1},{13,5},{2,10},{6,14},... | collective-permute-start | bytes 405512 | tf_op jit(solution)/shard_map/ppermute | solution.py:243
  41.9 6.8 %collective-permute-start.9 = (bf16[17,16,128]{2,1,0:T(8,128)(2,1)S(1)}, bf16[17,16,128]{2,1,0:T(8,128)(2,1)S(1)}, u32[]{:S(2)}, u32[]{:S(2)}) collective-permute-start(bf16[17,16,128]{2,1,0:T(8,128)(2,1)S(1)} %get-tuple-element.25.refs_1_), channel_id=1, source_target_pairs={{0,3},{1,2},{2,1},{3,0},{4,7},{5,6},{6,5},{7,4},{8,11},{9,10},{10,... | collective-permute-start | bytes 208904 | tf_op jit(solution)/shard_map/ppermute | solution.py:243
  43.7 6.8 %collective-permute-start.8 = (bf16[17,16,128]{2,1,0:T(8,128)(2,1)S(1)}, bf16[17,16,128]{2,1,0:T(8,128)(2,1)S(1)}, u32[]{:S(2)}, u32[]{:S(2)}) collective-permute-start(bf16[17,16,128]{2,1,0:T(8,128)(2,1)S(1)} %get-tuple-element.25.refs_1_), channel_id=1, source_target_pairs={{0,2},{1,3},{2,0},{3,1},{4,6},{5,7},{6,4},{7,5},{8,10},{9,11},{10,... | collective-permute-start | bytes 208904 | tf_op jit(solution)/shard_map/ppermute | solution.py:243
  43.8 6.8 %collective-permute-start.7 = (bf16[17,16,128]{2,1,0:T(8,128)(2,1)S(1)}, bf16[17,16,128]{2,1,0:T(8,128)(2,1)S(1)}, u32[]{:S(2)}, u32[]{:S(2)}) collective-permute-start(bf16[17,16,128]{2,1,0:T(8,128)(2,1)S(1)} %get-tuple-element.25.refs_1_), channel_id=1, source_target_pairs={{0,1},{1,0},{2,3},{3,2},{4,5},{5,4},{6,7},{7,6},{8,9},{9,8},{10,11... | collective-permute-start | bytes 208904 | tf_op jit(solution)/shard_map/ppermute | solution.py:243
  51.3 3.1 %collective-permute-start.12 = (f32[8,128]{1,0:T(8,128)S(1)}, f32[8,128]{1,0:T(8,128)S(1)}, u32[]{:S(2)}, u32[]{:S(2)}) collective-permute-start(f32[8,128]{1,0:T(8,128)S(1)} %get-tuple-element.29), channel_id=1, source_target_pairs={{0,12},{4,8},{8,4},{12,0},{1,13},{5,9},{9,5},{13,1},{2,14},{6,10},... | collective-permute-start | bytes 12296 | tf_op jit(solution)/shard_map/ppermute | solution.py:243
  51.8 3.6 %collective-permute-start.11 = (f32[8,128]{1,0:T(8,128)S(1)}, f32[8,128]{1,0:T(8,128)S(1)}, u32[]{:S(2)}, u32[]{:S(2)}) collective-permute-start(f32[8,128]{1,0:T(8,128)S(1)} %get-tuple-element.29), channel_id=1, source_target_pairs={{0,8},{4,12},{8,0},{12,4},{1,9},{5,13},{9,1},{13,5},{2,10},{6,14},... | collective-permute-start | bytes 12296 | tf_op jit(solution)/shard_map/ppermute | solution.py:243
  53.2 2.2 %collective-permute-start.10 = (f32[8,128]{1,0:T(8,128)S(1)}, f32[8,128]{1,0:T(8,128)S(1)}, u32[]{:S(2)}, u32[]{:S(2)}) collective-permute-start(f32[8,128]{1,0:T(8,128)S(1)} %get-tuple-element.29), channel_id=1, source_target_pairs={{0,4},{4,0},{8,12},{12,8},{1,5},{5,1},{9,13},{13,9},{2,6},{6,2},{1... | collective-permute-start | bytes 12296 | tf_op jit(solution)/shard_map/ppermute | solution.py:243

commit v3 on v2

--- a/solution.py
+++ b/solution.py
@@ -131,9 +131,10 @@
 
 
 def primal_kernel(mix, last, n_parts, *refs):
-    grid, slot, tiles = refs[:3], refs[3], refs[4]
-    parts = refs[5 : 5 + n_parts]
-    refs = refs[5 + n_parts :]
+    grid, tiles = refs[:3], refs[3]
+    parts = refs[4 : 4 + n_parts]
+    refs = refs[4 + n_parts :]
+    slot = lax.axis_index("colblk")
     weight_in, primal_norm, cost, upper, flag, point, start = refs[:7]
     point_out, weight_out, out, source, acc, *held = refs[7:14]
     sems = refs[14]
@@ -171,16 +172,15 @@
     for copy in copies:
         copy.wait()
     tile_products((grid[0], *held), tiles, source, acc, False)
-    pack(acc, out, jnp.sum(moved_norm, axis=1, keepdims=True), slot[0])
+    pack(acc, out, jnp.sum(moved_norm, axis=1, keepdims=True), slot)
     if last:
         put.wait()
 
 
 def dual_kernel(mix, last, n_parts, *refs):
-    if last:
-        slot, refs = refs[0], refs[1:]
-    else:
-        grid, slot, tiles, refs = refs[:3], refs[3], refs[4], refs[5:]
+    if not last:
+        grid, tiles, refs = refs[:3], refs[3], refs[4:]
+    slot = lax.axis_index("rowblk")
     parts = refs[:n_parts]
     refs = refs[n_parts:]
     weight, demand, flag, dual, start = refs[:5]
@@ -214,13 +214,13 @@
     dual_norm = jnp.sum(moved_norm, axis=1, keepdims=True)
     if last:
         lanes = lax.broadcasted_iota(jnp.int32, out.shape, 1)
-        out[...] = jnp.where(lanes == slot[0], dual_norm, 0.0)
+        out[...] = jnp.where(lanes == slot, dual_norm, 0.0)
         put.wait()
     else:
         for copy in copies:
             copy.wait()
         tile_products((grid[0], *held), tiles, source, acc, True)
-        pack(acc, out, dual_norm, slot[0])
+        pack(acc, out, dual_norm, slot)
 
 
 def call(kernel, inputs, in_specs, outputs, out_specs, scratch):
@@ -276,8 +276,6 @@
     bf16, f32 = jnp.bfloat16, jnp.float32
     cost, upper, col_flag = (v.reshape(col_blocks, tile) for v in (cost, upper, col_flag))
     row_flag = row_flag.reshape(row_blocks, tile)
-    row_slot = lax.axis_index("rowblk").astype(jnp.int32).reshape(1)
-    col_slot = lax.axis_index("colblk").astype(jnp.int32).reshape(1)
     grid = [tile_count, far(tile_row), far(tile_col)]
 
     total = tile_row.shape[0]
@@ -316,8 +314,8 @@
         parts = butterfly(terms, "rowblk", 2)
         point, weight, terms = call(
             functools.partial(primal_kernel, mix, last, len(parts)),
-            [*grid, col_slot, tiles, *parts, weight, primal_norm, cost, upper, col_flag, point, primal_start],
-            [SMEM_SPEC] + [FAR_SPEC] * 2 + [SMEM_SPEC] + [VMEM_SPEC] * (8 + len(parts)),
+            [*grid, tiles, *parts, weight, primal_norm, cost, upper, col_flag, point, primal_start],
+            [SMEM_SPEC] + [FAR_SPEC] * 2 + [VMEM_SPEC] * (8 + len(parts)),
             [primal, small, row_parts],
             [FAR_SPEC if last else VMEM_SPEC, VMEM_SPEC, VMEM_SPEC],
             [*to_rows, sems] + [pltpu.VMEM(primal.shape, f32)] * last,
@@ -327,8 +325,8 @@
         if last:
             dual, primal_norm, terms = call(
                 functools.partial(dual_kernel, mix, last, len(parts)),
-                [row_slot, *vectors],
-                [SMEM_SPEC] + [VMEM_SPEC] * len(vectors),
+                vectors,
+                [VMEM_SPEC] * len(vectors),
                 [dual_like, small, small],
                 [FAR_SPEC, VMEM_SPEC, VMEM_SPEC],
                 [pltpu.VMEM(dual.shape, f32), sems],
@@ -336,8 +334,8 @@
         else:
             dual, primal_norm, terms = call(
                 functools.partial(dual_kernel, mix, last, len(parts)),
-                [*grid, row_slot, tiles, *vectors],
-                [SMEM_SPEC] + [FAR_SPEC] * 2 + [SMEM_SPEC] + [VMEM_SPEC] * (1 + len(vectors)),
+                [*grid, tiles, *vectors],
+                [SMEM_SPEC] + [FAR_SPEC] * 2 + [VMEM_SPEC] * (1 + len(vectors)),
                 [dual_like, small, col_parts],
                 [VMEM_SPEC] * 3,
                 [*to_cols, sems],

time: 56.4 us -> 48.5 us (0.86)
  local copies, waits for them, and re-layouts: 5.3 us -> 0.15 us
  Pallas kernels: 10.2 us -> 7.71 us
  other arithmetic: 1.51 us -> 0.85 us
    unnamed x32 -> x14, local copies, waits for them, and re-layouts: 5.19 us -> 0.03 us
    pallas_call x5, Pallas kernels: 10.2 us -> 7.71 us  [call(): pl.pallas_call(kernel, out_shape=outputs, in_specs=in_specs, out_specs=ou...]
    convert_element_type x2, other arithmetic: 0.74 us -> 0.08 us  [butterfly(): total = add_up([p.astype(jnp.float32) for p in parts]).astype(value.dtype)]
  transfers between devices with their start and end apart: 13 -> 13, of which waited for: 11 -> 10; matrix products, arithmetic and copies ran while one was open for 0% -> 0% of each run, Pallas kernels for 0% -> 0%
where the time goes in v3:
time: 48.5 us; the launch traced here: 47.9 us
  waiting for transfers between devices  21.5 us (44%)
  starting transfers between devices  16.3 us (34%)
  Pallas kernels  7.71 us (16%)
  between operations  1.47 us (3%)
  other arithmetic  0.85 us (2%)
    ppermute x13, waiting for transfers between devices, swap(): return lax.ppermute(value, axis, [(i, i ^ mask) for i in range(size)])  21.5 us
    ppermute x13, starting transfers between devices, swap(): return lax.ppermute(value, axis, [(i, i ^ mask) for i in range(size)])  16.3 us
    pallas_call x5, Pallas kernels, call(): pl.pallas_call(kernel, out_shape=outputs, in_specs=in_specs, out_specs=ou...  7.71 us
  transfers between devices with their start and end apart: 13, of which 10 were waited for; matrix products, arithmetic and copies ran while one was open for 0% of the time, Pallas kernels for 0%

profile of v3, /device:TPU:0, one launch (start us, length us, event | category | flops | bytes accessed | tf_op | source)
XLA Modules:
  0.0 47.9 jit_solution(10716283957441377576)
XLA Ops:
  0.6 0.0 copy-start
  0.6 0.0 copy-start.5
  0.7 0.0 copy-start.4
  0.7 0.0 copy-start.3
  1.4 0.0 copy-start.1
  1.4 0.0 copy-start.2
  1.4 0.0 copy-start.6
  1.4 2.1 %shard_map.130 = (bf16[33,16,128]{2,1,0:T(8,128)(2,1)S(1)}, bf16[96,128,128]{2,1,0:T(8,128)(2,1)S(1)}) custom-call(s32[1]{0:T(128)S(6)} %copy.14.refs_0_, s32[96]{0:T(128)} %refs_1_.7, s32[96]{0:T(128)} %refs_2_.7, bf16[96,128,128]{2,1,0:T(8,128)(2,1)} %refs_3_.1, f32[8,4096]{1,0:T(8,128)} %refs_8_.1), custom_call_target="tpu_custom_call" | custom-call | tf_op jit(solution)/shard_map/pallas_call | solution.py:227
  3.5 0.5 %collective-permute-start = (bf16[33,16,128]{2,1,0:T(8,128)(2,1)S(1)}, bf16[33,16,128]{2,1,0:T(8,128)(2,1)S(1)}, u32[]{:S(2)}, u32[]{:S(2)}) collective-permute-start(bf16[33,16,128]{2,1,0:T(8,128)(2,1)S(1)} %get-tuple-element.18), channel_id=1, source_target_pairs={{0,4},{4,0},{8,12},{12,8},{1,5},{5,1},{9,13},{13,9},{2,6},{6,2},{1... | collective-permute-start | bytes 405512 | tf_op jit(solution)/shard_map/ppermute | solution.py:243
  4.0 1.0 %collective-permute-done = bf16[33,16,128]{2,1,0:T(8,128)(2,1)S(1)} collective-permute-done((bf16[33,16,128]{2,1,0:T(8,128)(2,1)S(1)}, bf16[33,16,128]{2,1,0:T(8,128)(2,1)S(1)}, u32[]{:S(2)}, u32[]{:S(2)}) %collective-permute-start) | collective-permute-done | bytes 135200 | tf_op jit(solution)/shard_map/ppermute | solution.py:243
  5.0 2.9 %collective-permute-start.1 = (bf16[33,16,128]{2,1,0:T(8,128)(2,1)S(1)}, bf16[33,16,128]{2,1,0:T(8,128)(2,1)S(1)}, u32[]{:S(2)}, u32[]{:S(2)}) collective-permute-start(bf16[33,16,128]{2,1,0:T(8,128)(2,1)S(1)} %add_convert_fusion.1.refs_4_), channel_id=1, source_target_pairs={{0,8},{4,12},{8,0},{12,4},{1,9},{5,13},{9,1},{13,5},{2,10},{6,14},... | collective-permute-start | bytes 405512 | tf_op jit(solution)/shard_map/ppermute | solution.py:243
  7.9 3.9 %collective-permute-done.1.refs_5_ = bf16[33,16,128]{2,1,0:T(8,128)(2,1)S(1)} collective-permute-done((bf16[33,16,128]{2,1,0:T(8,128)(2,1)S(1)}, bf16[33,16,128]{2,1,0:T(8,128)(2,1)S(1)}, u32[]{:S(2)}, u32[]{:S(2)}) %collective-permute-start.1) | collective-permute-done | bytes 135200 | tf_op jit(solution)/shard_map/ppermute | solution.py:243
  11.8 0.0 copy-done
  11.8 0.0 copy-done.5
  11.8 0.0 copy-done.4
  11.8 0.0 copy-done.3
  11.8 1.7 %shard_map.131 = (f32[8,8192]{1,0:T(8,128)S(1)}, f32[8,128]{1,0:T(8,128)S(1)}, bf16[17,16,128]{2,1,0:T(8,128)(2,1)S(1)}) custom-call(s32[1]{0:T(128)S(6)} %copy.14.refs_0_, s32[96]{0:T(128)} %refs_1_.7, s32[96]{0:T(128)} %refs_2_.7, bf16[96,128,128]{2,1,0:T(8,128)(2,1)S(1)} %get-tuple-element.17.refs_3_, bf16[33,16,128]{2,1,0:T(8,128)(2,1)S(1)} %add_convert_fusion.1.refs_4_, ...), custom_call_target="tpu_custom_call" | custom-call | tf_op jit(solution)/shard_map/pallas_call | solution.py:227
  13.6 3.5 %collective-permute-start.4 = (bf16[17,16,128]{2,1,0:T(8,128)(2,1)S(1)}, bf16[17,16,128]{2,1,0:T(8,128)(2,1)S(1)}, u32[]{:S(2)}, u32[]{:S(2)}) collective-permute-start(bf16[17,16,128]{2,1,0:T(8,128)(2,1)S(1)} %get-tuple-element.19.refs_4_), channel_id=1, source_target_pairs={{0,3},{1,2},{2,1},{3,0},{4,7},{5,6},{6,5},{7,4},{8,11},{9,10},{10,... | collective-permute-start | bytes 208904 | tf_op jit(solution)/shard_map/ppermute | solution.py:243
  17.0 0.0 collective-permute-start.3
  17.0 1.0 %collective-permute-start.2 = (bf16[17,16,128]{2,1,0:T(8,128)(2,1)S(1)}, bf16[17,16,128]{2,1,0:T(8,128)(2,1)S(1)}, u32[]{:S(2)}, u32[]{:S(2)}) collective-permute-start(bf16[17,16,128]{2,1,0:T(8,128)(2,1)S(1)} %get-tuple-element.19.refs_4_), channel_id=1, source_target_pairs={{0,1},{1,0},{2,3},{3,2},{4,5},{5,4},{6,7},{7,6},{8,9},{9,8},{10,11... | collective-permute-start | bytes 208904 | tf_op jit(solution)/shard_map/ppermute | solution.py:243
  18.0 2.6 %collective-permute-done.4.refs_7_ = bf16[17,16,128]{2,1,0:T(8,128)(2,1)S(1)} collective-permute-done((bf16[17,16,128]{2,1,0:T(8,128)(2,1)S(1)}, bf16[17,16,128]{2,1,0:T(8,128)(2,1)S(1)}, u32[]{:S(2)}, u32[]{:S(2)}) %collective-permute-start.4) | collective-permute-done | bytes 69664 | tf_op jit(solution)/shard_map/ppermute | solution.py:243
  20.6 2.3 %collective-permute-done.3.refs_6_ = bf16[17,16,128]{2,1,0:T(8,128)(2,1)S(1)} collective-permute-done((bf16[17,16,128]{2,1,0:T(8,128)(2,1)S(1)}, bf16[17,16,128]{2,1,0:T(8,128)(2,1)S(1)}, u32[]{:S(2)}, u32[]{:S(2)}) %collective-permute-start.3) | collective-permute-done | bytes 69664 | tf_op jit(solution)/shard_map/ppermute | solution.py:243
  22.9 0.0 collective-permute-done.2.refs_5_
  22.9 0.0 copy-done.1
  22.9 0.0 copy-done.6
  22.9 1.4 %shard_map.132 = (f32[8,4096]{1,0:T(8,128)S(1)}, f32[8,128]{1,0:T(8,128)S(1)}, bf16[33,16,128]{2,1,0:T(8,128)(2,1)S(1)}) custom-call(s32[1]{0:T(128)S(6)} %copy.14.refs_0_, s32[96]{0:T(128)} %refs_1_.7, s32[96]{0:T(128)} %refs_2_.7, bf16[96,128,128]{2,1,0:T(8,128)(2,1)S(1)} %get-tuple-element.17.refs_3_, bf16[17,16,128]{2,1,0:T(8,128)(2,1)S(1)} %get-tuple-element.19.refs_4_, ...), custom_call_target="tpu_custom_call" | custom-call | tf_op jit(solution)/shard_map/pallas_call | solution.py:227
  24.3 0.1 collective-permute-start.5
  24.3 1.3 %collective-permute-done.5 = bf16[33,16,128]{2,1,0:T(8,128)(2,1)S(1)} collective-permute-done((bf16[33,16,128]{2,1,0:T(8,128)(2,1)S(1)}, bf16[33,16,128]{2,1,0:T(8,128)(2,1)S(1)}, u32[]{:S(2)}, u32[]{:S(2)}) %collective-permute-start.5) | collective-permute-done | bytes 135200 | tf_op jit(solution)/shard_map/ppermute | solution.py:243
  25.7 1.7 %collective-permute-start.6 = (bf16[33,16,128]{2,1,0:T(8,128)(2,1)S(1)}, bf16[33,16,128]{2,1,0:T(8,128)(2,1)S(1)}, u32[]{:S(2)}, u32[]{:S(2)}) collective-permute-start(bf16[33,16,128]{2,1,0:T(8,128)(2,1)S(1)} %add_convert_fusion.refs_4_), channel_id=1, source_target_pairs={{0,8},{4,12},{8,0},{12,4},{1,9},{5,13},{9,1},{13,5},{2,10},{6,14},... | collective-permute-start | bytes 405512 | tf_op jit(solution)/shard_map/ppermute | solution.py:243
  27.4 4.0 %collective-permute-done.6.refs_5_ = bf16[33,16,128]{2,1,0:T(8,128)(2,1)S(1)} collective-permute-done((bf16[33,16,128]{2,1,0:T(8,128)(2,1)S(1)}, bf16[33,16,128]{2,1,0:T(8,128)(2,1)S(1)}, u32[]{:S(2)}, u32[]{:S(2)}) %collective-permute-start.6) | collective-permute-done | bytes 135200 | tf_op jit(solution)/shard_map/ppermute | solution.py:243
  31.4 1.7 %shard_map.133 = (f32[8,8192]{1,0:T(8,128)}, f32[8,128]{1,0:T(8,128)S(1)}, bf16[17,16,128]{2,1,0:T(8,128)(2,1)S(1)}) custom-call(s32[1]{0:T(128)S(6)} %copy.14.refs_0_, s32[96]{0:T(128)} %refs_1_.7, s32[96]{0:T(128)} %refs_2_.7, bf16[96,128,128]{2,1,0:T(8,128)(2,1)S(1)} %get-tuple-element.17.refs_3_, bf16[33,16,128]{2,1,0:T(8,128)(2,1)S(1)} %add_convert_fusion.refs_4_, ...), custom_call_target="tpu_custom_call" | custom-call | tf_op jit(solution)/shard_map/pallas_call | solution.py:227
  33.2 2.0 %collective-permute-start.9 = (bf16[17,16,128]{2,1,0:T(8,128)(2,1)S(1)}, bf16[17,16,128]{2,1,0:T(8,128)(2,1)S(1)}, u32[]{:S(2)}, u32[]{:S(2)}) collective-permute-start(bf16[17,16,128]{2,1,0:T(8,128)(2,1)S(1)} %get-tuple-element.25.refs_0_), channel_id=1, source_target_pairs={{0,3},{1,2},{2,1},{3,0},{4,7},{5,6},{6,5},{7,4},{8,11},{9,10},{10,... | collective-permute-start | bytes 208904 | tf_op jit(solution)/shard_map/ppermute | solution.py:243
  35.2 0.0 collective-permute-start.8
  35.2 2.4 %collective-permute-start.7 = (bf16[17,16,128]{2,1,0:T(8,128)(2,1)S(1)}, bf16[17,16,128]{2,1,0:T(8,128)(2,1)S(1)}, u32[]{:S(2)}, u32[]{:S(2)}) collective-permute-start(bf16[17,16,128]{2,1,0:T(8,128)(2,1)S(1)} %get-tuple-element.25.refs_0_), channel_id=1, source_target_pairs={{0,1},{1,0},{2,3},{3,2},{4,5},{5,4},{6,7},{7,6},{8,9},{9,8},{10,11... | collective-permute-start | bytes 208904 | tf_op jit(solution)/shard_map/ppermute | solution.py:243
  37.6 0.1 slice_reduce_fusion
  37.7 1.7 %collective-permute-done.9.refs_3_ = bf16[17,16,128]{2,1,0:T(8,128)(2,1)S(1)} collective-permute-done((bf16[17,16,128]{2,1,0:T(8,128)(2,1)S(1)}, bf16[17,16,128]{2,1,0:T(8,128)(2,1)S(1)}, u32[]{:S(2)}, u32[]{:S(2)}) %collective-permute-start.9) | collective-permute-done | bytes 69664 | tf_op jit(solution)/shard_map/ppermute | solution.py:243
  39.5 2.3 %collective-permute-done.8.refs_2_ = bf16[17,16,128]{2,1,0:T(8,128)(2,1)S(1)} collective-permute-done((bf16[17,16,128]{2,1,0:T(8,128)(2,1)S(1)}, bf16[17,16,128]{2,1,0:T(8,128)(2,1)S(1)}, u32[]{:S(2)}, u32[]{:S(2)}) %collective-permute-start.8) | collective-permute-done | bytes 69664 | tf_op jit(solution)/shard_map/ppermute | solution.py:243
  41.7 0.0 collective-permute-done.7.refs_1_
  41.7 0.8 %shard_map.134 = (f32[8,4096]{1,0:T(8,128)}, f32[8,128]{1,0:T(8,128)S(1)}, f32[8,128]{1,0:T(8,128)S(1)}) custom-call(bf16[17,16,128]{2,1,0:T(8,128)(2,1)S(1)} %get-tuple-element.25.refs_0_, bf16[17,16,128]{2,1,0:T(8,128)(2,1)S(1)} %collective-permute-done.7.refs_1_, bf16[17,16,128]{2,1,0:T(8,128)(2,1)S(1)} %collective-permute-done.8.refs_2_, ...), custom_call_target="tpu_custom_call" | custom-call | tf_op jit(solution)/shard_map/pallas_call | solution.py:227
  42.6 1.1 %collective-permute-start.12 = (f32[8,128]{1,0:T(8,128)S(1)}, f32[8,128]{1,0:T(8,128)S(1)}, u32[]{:S(2)}, u32[]{:S(2)}) collective-permute-start(f32[8,128]{1,0:T(8,128)S(1)} %get-tuple-element.29), channel_id=1, source_target_pairs={{0,12},{4,8},{8,4},{12,0},{1,13},{5,9},{9,5},{13,1},{2,14},{6,10},... | collective-permute-start | bytes 12296 | tf_op jit(solution)/shard_map/ppermute | solution.py:243
  43.6 1.1 %collective-permute-start.11 = (f32[8,128]{1,0:T(8,128)S(1)}, f32[8,128]{1,0:T(8,128)S(1)}, u32[]{:S(2)}, u32[]{:S(2)}) collective-permute-start(f32[8,128]{1,0:T(8,128)S(1)} %get-tuple-element.29), channel_id=1, source_target_pairs={{0,8},{4,12},{8,0},{12,4},{1,9},{5,13},{9,1},{13,5},{2,10},{6,14},... | collective-permute-start | bytes 12296 | tf_op jit(solution)/shard_map/ppermute | solution.py:243
  44.7 0.0 collective-permute-start.10
  44.8 0.1 add_reduce_fusion
  44.9 0.8 %collective-permute-done.12 = f32[8,128]{1,0:T(8,128)S(1)} collective-permute-done((f32[8,128]{1,0:T(8,128)S(1)}, f32[8,128]{1,0:T(8,128)S(1)}, u32[]{:S(2)}, u32[]{:S(2)}) %collective-permute-start.12) | collective-permute-done | bytes 4128 | tf_op jit(solution)/shard_map/ppermute | solution.py:243
  45.6 1.6 %collective-permute-done.11 = f32[8,128]{1,0:T(8,128)S(1)} collective-permute-done((f32[8,128]{1,0:T(8,128)S(1)}, f32[8,128]{1,0:T(8,128)S(1)}, u32[]{:S(2)}, u32[]{:S(2)}) %collective-permute-start.11) | collective-permute-done | bytes 4128 | tf_op jit(solution)/shard_map/ppermute | solution.py:243
  47.2 0.0 collective-permute-done.10
  47.2 0.1 add_reduce_fusion.1
  47.4 0.5 %multiply_sqrt_fusion = f32[8]{0:T(128)} fusion(f32[8]{0:T(128)S(1)} %slice_reduce_fusion, f32[8]{0:T(128)S(1)} %add_reduce_fusion, f32[8]{0:T(128)S(1)} %add_reduce_fusion.1), kind=kLoop, calls=%fused_computation.5 | loop fusion | flops 24 | bytes 128 | tf_op jit(solution)/shard_map/sqrt | solution.py:346
  (4 shorter events, 0.1 us)
Async XLA Ops:
  0.6 11.2 %copy-start = (f32[8,8192]{1,0:T(8,128)S(1)}, f32[8,8192]{1,0:T(8,128)}, u32[]{:S(2)}) copy-start(f32[8,8192]{1,0:T(8,128)} %refs_12_.5) | copy-start | bytes 786436
  0.6 11.2 %copy-start.5 = (s32[8192]{0:T(1024)S(1)}, s32[8192]{0:T(1024)}, u32[]{:S(2)}) copy-start(s32[8192]{0:T(1024)} %param.18) | copy-start | bytes 98308
  0.7 11.2 %copy-start.4 = (f32[8192]{0:T(1024)S(1)}, f32[8192]{0:T(1024)}, u32[]{:S(2)}) copy-start(f32[8192]{0:T(1024)} %param.17) | copy-start | bytes 98308
  0.7 11.2 %copy-start.3 = (f32[8192]{0:T(1024)S(1)}, f32[8192]{0:T(1024)}, u32[]{:S(2)}) copy-start(f32[8192]{0:T(1024)} %param.15) | copy-start | bytes 98308
  1.4 21.5 %copy-start.1 = (f32[8,4096]{1,0:T(8,128)S(1)}, f32[8,4096]{1,0:T(8,128)}, u32[]{:S(2)}) copy-start(f32[8,4096]{1,0:T(8,128)} %refs_8_.1) | copy-start | bytes 393220
  1.4 21.5 %copy-start.2 = (f32[8,4096]{1,0:T(8,128)S(1)}, f32[8,4096]{1,0:T(8,128)}, u32[]{:S(2)}) copy-start(f32[8,4096]{1,0:T(8,128)} %refs_5_.1) | copy-start | bytes 393220
  1.4 21.5 %copy-start.6 = (s32[4096]{0:T(1024)S(1)}, s32[4096]{0:T(1024)}, u32[]{:S(2)}) copy-start(s32[4096]{0:T(1024)} %param.19) | copy-start | bytes 49156
  3.5 1.5 %collective-permute-start = (bf16[33,16,128]{2,1,0:T(8,128)(2,1)S(1)}, bf16[33,16,128]{2,1,0:T(8,128)(2,1)S(1)}, u32[]{:S(2)}, u32[]{:S(2)}) collective-permute-start(bf16[33,16,128]{2,1,0:T(8,128)(2,1)S(1)} %get-tuple-element.18), channel_id=1, source_target_pairs={{0,4},{4,0},{8,12},{12,8},{1,5},{5,1},{9,13},{13,9},{2,6},{6,2},{1... | collective-permute-start | bytes 405512 | tf_op jit(solution)/shard_map/ppermute | solution.py:243
  5.0 6.8 %collective-permute-start.1 = (bf16[33,16,128]{2,1,0:T(8,128)(2,1)S(1)}, bf16[33,16,128]{2,1,0:T(8,128)(2,1)S(1)}, u32[]{:S(2)}, u32[]{:S(2)}) collective-permute-start(bf16[33,16,128]{2,1,0:T(8,128)(2,1)S(1)} %add_convert_fusion.1.refs_4_), channel_id=1, source_target_pairs={{0,8},{4,12},{8,0},{12,4},{1,9},{5,13},{9,1},{13,5},{2,10},{6,14},... | collective-permute-start | bytes 405512 | tf_op jit(solution)/shard_map/ppermute | solution.py:243
  13.6 7.0 %collective-permute-start.4 = (bf16[17,16,128]{2,1,0:T(8,128)(2,1)S(1)}, bf16[17,16,128]{2,1,0:T(8,128)(2,1)S(1)}, u32[]{:S(2)}, u32[]{:S(2)}) collective-permute-start(bf16[17,16,128]{2,1,0:T(8,128)(2,1)S(1)} %get-tuple-element.19.refs_4_), channel_id=1, source_target_pairs={{0,3},{1,2},{2,1},{3,0},{4,7},{5,6},{6,5},{7,4},{8,11},{9,10},{10,... | collective-permute-start | bytes 208904 | tf_op jit(solution)/shard_map/ppermute | solution.py:243
  17.0 5.8 %collective-permute-start.3 = (bf16[17,16,128]{2,1,0:T(8,128)(2,1)S(1)}, bf16[17,16,128]{2,1,0:T(8,128)(2,1)S(1)}, u32[]{:S(2)}, u32[]{:S(2)}) collective-permute-start(bf16[17,16,128]{2,1,0:T(8,128)(2,1)S(1)} %get-tuple-element.19.refs_4_), channel_id=1, source_target_pairs={{0,2},{1,3},{2,0},{3,1},{4,6},{5,7},{6,4},{7,5},{8,10},{9,11},{10,... | collective-permute-start | bytes 208904 | tf_op jit(solution)/shard_map/ppermute | solution.py:243
  17.0 5.8 %collective-permute-start.2 = (bf16[17,16,128]{2,1,0:T(8,128)(2,1)S(1)}, bf16[17,16,128]{2,1,0:T(8,128)(2,1)S(1)}, u32[]{:S(2)}, u32[]{:S(2)}) collective-permute-start(bf16[17,16,128]{2,1,0:T(8,128)(2,1)S(1)} %get-tuple-element.19.refs_4_), channel_id=1, source_target_pairs={{0,1},{1,0},{2,3},{3,2},{4,5},{5,4},{6,7},{7,6},{8,9},{9,8},{10,11... | collective-permute-start | bytes 208904 | tf_op jit(solution)/shard_map/ppermute | solution.py:243
  24.3 1.4 %collective-permute-start.5 = (bf16[33,16,128]{2,1,0:T(8,128)(2,1)S(1)}, bf16[33,16,128]{2,1,0:T(8,128)(2,1)S(1)}, u32[]{:S(2)}, u32[]{:S(2)}) collective-permute-start(bf16[33,16,128]{2,1,0:T(8,128)(2,1)S(1)} %get-tuple-element.21), channel_id=1, source_target_pairs={{0,4},{4,0},{8,12},{12,8},{1,5},{5,1},{9,13},{13,9},{2,6},{6,2},{1... | collective-permute-start | bytes 405512 | tf_op jit(solution)/shard_map/ppermute | solution.py:243
  25.7 5.7 %collective-permute-start.6 = (bf16[33,16,128]{2,1,0:T(8,128)(2,1)S(1)}, bf16[33,16,128]{2,1,0:T(8,128)(2,1)S(1)}, u32[]{:S(2)}, u32[]{:S(2)}) collective-permute-start(bf16[33,16,128]{2,1,0:T(8,128)(2,1)S(1)} %add_convert_fusion.refs_4_), channel_id=1, source_target_pairs={{0,8},{4,12},{8,0},{12,4},{1,9},{5,13},{9,1},{13,5},{2,10},{6,14},... | collective-permute-start | bytes 405512 | tf_op jit(solution)/shard_map/ppermute | solution.py:243
  33.2 6.3 %collective-permute-start.9 = (bf16[17,16,128]{2,1,0:T(8,128)(2,1)S(1)}, bf16[17,16,128]{2,1,0:T(8,128)(2,1)S(1)}, u32[]{:S(2)}, u32[]{:S(2)}) collective-permute-start(bf16[17,16,128]{2,1,0:T(8,128)(2,1)S(1)} %get-tuple-element.25.refs_0_), channel_id=1, source_target_pairs={{0,3},{1,2},{2,1},{3,0},{4,7},{5,6},{6,5},{7,4},{8,11},{9,10},{10,... | collective-permute-start | bytes 208904 | tf_op jit(solution)/shard_map/ppermute | solution.py:243
  35.2 6.5 %collective-permute-start.8 = (bf16[17,16,128]{2,1,0:T(8,128)(2,1)S(1)}, bf16[17,16,128]{2,1,0:T(8,128)(2,1)S(1)}, u32[]{:S(2)}, u32[]{:S(2)}) collective-permute-start(bf16[17,16,128]{2,1,0:T(8,128)(2,1)S(1)} %get-tuple-element.25.refs_0_), channel_id=1, source_target_pairs={{0,2},{1,3},{2,0},{3,1},{4,6},{5,7},{6,4},{7,5},{8,10},{9,11},{10,... | collective-permute-start | bytes 208904 | tf_op jit(solution)/shard_map/ppermute | solution.py:243
  35.2 6.5 %collective-permute-start.7 = (bf16[17,16,128]{2,1,0:T(8,128)(2,1)S(1)}, bf16[17,16,128]{2,1,0:T(8,128)(2,1)S(1)}, u32[]{:S(2)}, u32[]{:S(2)}) collective-permute-start(bf16[17,16,128]{2,1,0:T(8,128)(2,1)S(1)} %get-tuple-element.25.refs_0_), channel_id=1, source_target_pairs={{0,1},{1,0},{2,3},{3,2},{4,5},{5,4},{6,7},{7,6},{8,9},{9,8},{10,11... | collective-permute-start | bytes 208904 | tf_op jit(solution)/shard_map/ppermute | solution.py:243
  42.6 3.1 %collective-permute-start.12 = (f32[8,128]{1,0:T(8,128)S(1)}, f32[8,128]{1,0:T(8,128)S(1)}, u32[]{:S(2)}, u32[]{:S(2)}) collective-permute-start(f32[8,128]{1,0:T(8,128)S(1)} %get-tuple-element.29), channel_id=1, source_target_pairs={{0,12},{4,8},{8,4},{12,0},{1,13},{5,9},{9,5},{13,1},{2,14},{6,10},... | collective-permute-start | bytes 12296 | tf_op jit(solution)/shard_map/ppermute | solution.py:243
  43.6 3.6 %collective-permute-start.11 = (f32[8,128]{1,0:T(8,128)S(1)}, f32[8,128]{1,0:T(8,128)S(1)}, u32[]{:S(2)}, u32[]{:S(2)}) collective-permute-start(f32[8,128]{1,0:T(8,128)S(1)} %get-tuple-element.29), channel_id=1, source_target_pairs={{0,8},{4,12},{8,0},{12,4},{1,9},{5,13},{9,1},{13,5},{2,10},{6,14},... | collective-permute-start | bytes 12296 | tf_op jit(solution)/shard_map/ppermute | solution.py:243
  44.7 2.5 %collective-permute-start.10 = (f32[8,128]{1,0:T(8,128)S(1)}, f32[8,128]{1,0:T(8,128)S(1)}, u32[]{:S(2)}, u32[]{:S(2)}) collective-permute-start(f32[8,128]{1,0:T(8,128)S(1)} %get-tuple-element.29), channel_id=1, source_target_pairs={{0,4},{4,0},{8,12},{12,8},{1,5},{5,1},{9,13},{13,9},{2,6},{6,2},{1... | collective-permute-start | bytes 12296 | tf_op jit(solution)/shard_map/ppermute | solution.py:243

commit v4 on v3

--- a/solution.py
+++ b/solution.py
@@ -10,7 +10,7 @@
 ITERS = 2
 ETA = 0.3
 EPS = 1e-06
-PART = 32
+PART = 24
 VMEM_LIMIT = 8 * 1024 * 1024
 
 SMEM_SPEC = pl.BlockSpec(memory_space=pltpu.SMEM)
@@ -22,13 +22,6 @@
     high = value.astype(jnp.bfloat16)
     low = (value - high.astype(jnp.float32)).astype(jnp.bfloat16)
     return jnp.concatenate([high, low], axis=0)
-
-
-def fetch_grid(grid, held, sems):
-    copies = [pltpu.make_async_copy(a, b, sems.at[i]) for i, (a, b) in enumerate(zip(grid[1:], held))]
-    for copy in copies:
-        copy.start()
-    return copies
 
 
 def tile_products(grid, tiles, source, acc, backward, ready=None):
@@ -37,8 +30,6 @@
     spare = acc.shape[0] - 1
     scen = acc.shape[1]
     live = count[0]
-    depth = 0 if backward else 1
-    dims = (((1,), (depth,)), ((), ()))
     acc[...] = jnp.zeros_like(acc)
 
     def part(first, size):
@@ -60,10 +51,10 @@
                     ],
                     axis=0,
                 )
-                right = jnp.concatenate([tiles[g], tiles[g + 1]], axis=depth)
+                right = jnp.concatenate([tiles[g], tiles[g + 1]], axis=0)
             else:
                 left, right = picked[0], tiles[g]
-            product = lax.dot_general(left, right, dims, preferred_element_type=jnp.float32)
+            product = jnp.dot(left, right, preferred_element_type=jnp.float32)
             for k in range(pair):
                 own = product[2 * scen * k : 2 * scen * (k + 1)]
                 results.append(own[:scen] + own[scen:])
@@ -107,13 +98,16 @@
 
 
 def first_kernel(*refs):
-    grid, (tiles_far, dual_far), (out, tiles), (source, acc), held, (dual, sems) = (
-        refs[:3], refs[3:5], refs[5:7], refs[7:9], refs[9:11], refs[11:]
-    )
+    count, rows_far, cols_far, tiles_far, dual_far, out, tiles, rows, cols, source, acc, dual, sems = refs
     tile = tiles.shape[1]
     get_dual = pltpu.make_async_copy(dual_far, dual, sems.at[2])
     get_dual.start()
-    copies = fetch_grid(grid, held, sems)
+    copies = [
+        pltpu.make_async_copy(rows_far, rows, sems.at[0]),
+        pltpu.make_async_copy(cols_far, cols, sems.at[1]),
+    ]
+    for copy in copies:
+        copy.start()
     get_tiles = {}
     for n, first in enumerate(range(0, tiles.shape[0], PART)):
         span = pl.ds(first, min(PART, tiles.shape[0] - first))
@@ -124,10 +118,22 @@
         source[b] = split_rows(dual[:, b * tile : (b + 1) * tile])
     for copy in copies:
         copy.wait()
-    tile_products((grid[0], *held), tiles, source, acc, True, lambda first: get_tiles[first].wait())
+    tile_products((count, rows, cols), tiles, source, acc, True, lambda first: get_tiles[first].wait())
     for first in list(get_tiles)[1:]:
-        pl.when(first >= grid[0][0])(get_tiles[first].wait)
+        pl.when(first >= count[0])(get_tiles[first].wait)
     pack(acc, out, 0.0, 0)
+
+
+def turn_kernel(count, tiles, after, turned):
+    del after
+    total = tiles.shape[0]
+
+    def part(first):
+        for g in range(first, min(first + PART, total)):
+            turned[g] = tiles[g].T
+
+    for first in range(0, total, PART):
+        pl.when(first < count[0])(functools.partial(part, first))
 
 
 def primal_kernel(mix, last, n_parts, *refs):
@@ -136,10 +142,8 @@
     refs = refs[4 + n_parts :]
     slot = lax.axis_index("colblk")
     weight_in, primal_norm, cost, upper, flag, point, start = refs[:7]
-    point_out, weight_out, out, source, acc, *held = refs[7:14]
-    sems = refs[14]
-    copies = fetch_grid(grid, held, sems)
-    made = refs[15] if last else point_out
+    point_out, weight_out, out, source, acc, sems = refs[7:13]
+    made = point_out
     tile = tiles.shape[1]
     blocks = source.shape[0]
     half = blocks // 2
@@ -166,15 +170,8 @@
         x_bar = 2.0 * x_hat - old
         made[:, lanes] = mix * x_bar + (1.0 - mix) * start[:, lanes]
         source[b] = split_rows(x_bar)
-    if last:
-        put = pltpu.make_async_copy(made, point_out, sems.at[2])
-        put.start()
-    for copy in copies:
-        copy.wait()
-    tile_products((grid[0], *held), tiles, source, acc, False)
+    tile_products(grid, tiles, source, acc, False)
     pack(acc, out, jnp.sum(moved_norm, axis=1, keepdims=True), slot)
-    if last:
-        put.wait()
 
 
 def dual_kernel(mix, last, n_parts, *refs):
@@ -185,10 +182,10 @@
     refs = refs[n_parts:]
     weight, demand, flag, dual, start = refs[:5]
     if last:
-        dual_out, primal_norm, out, made, sems = refs[5:]
+        dual_out, primal_norm, out = refs[5:]
+        made = dual_out
     else:
-        dual_out, primal_norm, out, source, acc, *held = refs[5:12]
-        copies = fetch_grid(grid, held, refs[12])
+        dual_out, primal_norm, out, source, acc, sems = refs[5:]
         made = dual_out
     tile = flag.shape[1]
     blocks = flag.shape[0]
@@ -208,28 +205,23 @@
         made[:, lanes] = new
         if not last:
             source[b] = split_rows(new)
-    if last:
-        put = pltpu.make_async_copy(made, dual_out, sems.at[0])
-        put.start()
     dual_norm = jnp.sum(moved_norm, axis=1, keepdims=True)
     if last:
         lanes = lax.broadcasted_iota(jnp.int32, out.shape, 1)
         out[...] = jnp.where(lanes == slot, dual_norm, 0.0)
-        put.wait()
     else:
-        for copy in copies:
-            copy.wait()
-        tile_products((grid[0], *held), tiles, source, acc, True)
+        tile_products(grid, tiles, source, acc, True)
         pack(acc, out, dual_norm, slot)
 
 
-def call(kernel, inputs, in_specs, outputs, out_specs, scratch):
+def call(kernel, inputs, in_specs, outputs, out_specs, scratch, cost=None):
     return pl.pallas_call(
         kernel,
         out_shape=outputs,
         in_specs=in_specs,
         out_specs=out_specs,
         scratch_shapes=scratch,
+        cost_estimate=cost,
         compiler_params=pltpu.CompilerParams(vmem_limit_bytes=VMEM_LIMIT),
     )(*inputs)
 
@@ -284,41 +276,49 @@
     row_parts = jax.ShapeDtypeStruct((row_blocks // 2 + 1, 2 * scen, tile), bf16)
     primal = jax.ShapeDtypeStruct(primal_start.shape, f32)
     dual_like = jax.ShapeDtypeStruct(dual_start.shape, f32)
-    held = [pltpu.SMEM((total,), jnp.int32)] * 2
     sems = pltpu.SemaphoreType.DMA((3 + pl.cdiv(total, PART),))
     to_cols = [
         pltpu.VMEM((row_blocks, 2 * scen, tile), bf16),
         pltpu.VMEM((col_blocks + 1, scen, tile), f32),
-        *held,
     ]
     to_rows = [
         pltpu.VMEM((col_blocks, 2 * scen, tile), bf16),
         pltpu.VMEM((row_blocks + 1, scen, tile), f32),
-        *held,
     ]
 
     point, dual = primal_start, dual_start
     weight = jnp.ones((scen, tile), f32)
     primal_norm = weight
-    terms, tiles = call(
+    terms, tiles, *slots = call(
         first_kernel,
         [*grid, far(tiles), far(dual)],
         [SMEM_SPEC] + [FAR_SPEC] * 4,
-        [col_parts, pltpu.VMEM(tiles.shape, tiles.dtype)],
-        [VMEM_SPEC] * 2,
+        [col_parts, pltpu.VMEM(tiles.shape, tiles.dtype), *[pltpu.SMEM((total,), jnp.int32)] * 2],
+        [VMEM_SPEC] * 2 + [SMEM_SPEC] * 2,
         [*to_cols, pltpu.VMEM(dual.shape, f32), sems],
     )
+    grid = [tile_count, *slots]
     for step in range(ITERS):
         mix = (step + 1.0) / (step + 2.0)
         last = step == ITERS - 1
         parts = butterfly(terms, "rowblk", 2)
+        if step == 0:
+            (turned,) = call(
+                turn_kernel,
+                [tile_count, tiles, parts[0]],
+                [SMEM_SPEC] + [VMEM_SPEC] * 2,
+                [pltpu.VMEM(tiles.shape, tiles.dtype)],
+                [VMEM_SPEC],
+                [],
+                pl.CostEstimate(flops=0, bytes_accessed=2 * tiles.size * 2, transcendentals=0),
+            )
         point, weight, terms = call(
             functools.partial(primal_kernel, mix, last, len(parts)),
-            [*grid, tiles, *parts, weight, primal_norm, cost, upper, col_flag, point, primal_start],
-            [SMEM_SPEC] + [FAR_SPEC] * 2 + [VMEM_SPEC] * (8 + len(parts)),
-            [primal, small, row_parts],
-            [FAR_SPEC if last else VMEM_SPEC, VMEM_SPEC, VMEM_SPEC],
-            [*to_rows, sems] + [pltpu.VMEM(primal.shape, f32)] * last,
+            [*grid, turned, *parts, weight, primal_norm, cost, upper, col_flag, point, primal_start],
+            [SMEM_SPEC] * 3 + [VMEM_SPEC] * (8 + len(parts)),
+            [pltpu.VMEM(primal.shape, f32), small, row_parts],
+            [VMEM_SPEC, VMEM_SPEC, VMEM_SPEC],
+            [*to_rows, sems],
         )
         parts = butterfly(terms, "colblk", 4)
         vectors = [*parts, weight, demand, row_flag, dual, dual_start]
@@ -327,15 +327,15 @@
                 functools.partial(dual_kernel, mix, last, len(parts)),
                 vectors,
                 [VMEM_SPEC] * len(vectors),
-                [dual_like, small, small],
-                [FAR_SPEC, VMEM_SPEC, VMEM_SPEC],
-                [pltpu.VMEM(dual.shape, f32), sems],
+                [pltpu.VMEM(dual.shape, f32), small, small],
+                [VMEM_SPEC] * 3,
+                [],
             )
         else:
             dual, primal_norm, terms = call(
                 functools.partial(dual_kernel, mix, last, len(parts)),
                 [*grid, tiles, *vectors],
-                [SMEM_SPEC] + [FAR_SPEC] * 2 + [VMEM_SPEC] * (1 + len(vectors)),
+                [SMEM_SPEC] * 3 + [VMEM_SPEC] * (1 + len(vectors)),
                 [dual_like, small, col_parts],
                 [VMEM_SPEC] * 3,
                 [*to_cols, sems],

time: 48.5 us -> 44.9 us (0.926)
  waiting for transfers between devices: 21.5 us -> 18.5 us
  Pallas kernels: 7.71 us -> 5.51 us
  local copies, waits for them, and re-layouts: 0.15 us -> 1.51 us
  starting transfers between devices: 16.3 us -> 16.8 us
    ppermute x13, waiting for transfers between devices: 21.5 us -> 18.5 us  [swap(): return lax.ppermute(value, axis, [(i, i ^ mask) for i in range(size)])]
    pallas_call x5 -> x6, Pallas kernels: 7.71 us -> 5.51 us  [call(): pl.pallas_call(kernel, out_shape=outputs, in_specs=in_specs, out_specs=ou...]
    unnamed x14 -> x16, local copies, waits for them, and re-layouts: 0.03 us -> 1.39 us
    ppermute x13, starting transfers between devices: 16.3 us -> 16.8 us  [swap(): return lax.ppermute(value, axis, [(i, i ^ mask) for i in range(size)])]
  transfers between devices with their start and end apart: 13 -> 13, of which waited for: 10 -> 10; matrix products, arithmetic and copies ran while one was open for 0% -> 4% of each run, Pallas kernels for 0% -> 1%
where the time goes in v4:
time: 44.9 us; the launch traced here: 44.6 us
  waiting for transfers between devices  18.5 us (41%)
  starting transfers between devices  16.8 us (37%)
  Pallas kernels  5.51 us (12%)
  local copies, waits for them, and re-layouts  1.51 us (3%)
  between operations  1.41 us (3%)
  other arithmetic  0.85 us (2%)
    ppermute x13, waiting for transfers between devices, swap(): return lax.ppermute(value, axis, [(i, i ^ mask) for i in range(size)])  18.5 us
    ppermute x13, starting transfers between devices, swap(): return lax.ppermute(value, axis, [(i, i ^ mask) for i in range(size)])  16.8 us
    pallas_call x6, Pallas kernels, call(): pl.pallas_call(kernel, out_shape=outputs, in_specs=in_specs, out_specs=ou...  5.51 us
    unnamed x16, local copies, waits for them, and re-layouts  1.39 us
  transfers between devices with their start and end apart: 13, of which 10 were waited for; matrix products, arithmetic and copies ran while one was open for 4% of the time, Pallas kernels for 1%

profile of v4, /device:TPU:0, one launch (start us, length us, event | category | flops | bytes accessed | tf_op | source)
XLA Modules:
  0.0 44.6 jit_solution(5942445782614684584)
XLA Ops:
  1.3 2.0 %shard_map.130 = (bf16[33,16,128]{2,1,0:T(8,128)(2,1)S(1)}, bf16[96,128,128]{2,1,0:T(8,128)(2,1)S(1)}, s32[96]{0:T(128)S(4)}, s32[96]{0:T(128)S(4)}) custom-call(s32[1]{0:T(128)S(6)} %copy.16.refs_0_.count, s32[96]{0:T(128)} %refs_1_.1, s32[96]{0:T(128)} %refs_2_.1, bf16[96,128,128]{2,1,0:T(8,128)(2,1)} %refs_3_.1, f32[8,4096]{1,0:T(8,128)} %refs_8_.1), custom_call_target="tpu_custom_call" | custom-call | tf_op jit(solution)/shard_map/pallas_call | solution.py:218
  3.3 0.5 %collective-permute-start = (bf16[33,16,128]{2,1,0:T(8,128)(2,1)S(1)}, bf16[33,16,128]{2,1,0:T(8,128)(2,1)S(1)}, u32[]{:S(2)}, u32[]{:S(2)}) collective-permute-start(bf16[33,16,128]{2,1,0:T(8,128)(2,1)S(1)} %get-tuple-element.22), channel_id=1, source_target_pairs={{0,4},{4,0},{8,12},{12,8},{1,5},{5,1},{9,13},{13,9},{2,6},{6,2},{1... | collective-permute-start | bytes 405512 | tf_op jit(solution)/shard_map/ppermute | solution.py:235
  3.8 1.0 %collective-permute-done = bf16[33,16,128]{2,1,0:T(8,128)(2,1)S(1)} collective-permute-done((bf16[33,16,128]{2,1,0:T(8,128)(2,1)S(1)}, bf16[33,16,128]{2,1,0:T(8,128)(2,1)S(1)}, u32[]{:S(2)}, u32[]{:S(2)}) %collective-permute-start) | collective-permute-done | bytes 135200 | tf_op jit(solution)/shard_map/ppermute | solution.py:235
  4.8 3.2 %collective-permute-start.1 = (bf16[33,16,128]{2,1,0:T(8,128)(2,1)S(1)}, bf16[33,16,128]{2,1,0:T(8,128)(2,1)S(1)}, u32[]{:S(2)}, u32[]{:S(2)}) collective-permute-start(bf16[33,16,128]{2,1,0:T(8,128)(2,1)S(1)} %add_convert_fusion.1.after.refs_4_), channel_id=1, source_target_pairs={{0,8},{4,12},{8,0},{12,4},{1,9},{5,13},{9,1},{13,5},{2,10},{6,14},... | collective-permute-start | bytes 405512 | tf_op jit(solution)/shard_map/ppermute | solution.py:235
  8.1 0.5 %shard_map.131.refs_3_ = bf16[96,128,128]{2,1,0:T(8,128)(2,1)S(1)} custom-call(s32[1]{0:T(128)S(6)} %copy.16.refs_0_.count, bf16[96,128,128]{2,1,0:T(8,128)(2,1)S(1)} %get-tuple-element.21.tiles.refs_3_, bf16[33,16,128]{2,1,0:T(8,128)(2,1)S(1)} %add_convert_fusion.1.after.refs_4_), custom_call_target="tpu_custom_call" | custom-call | bytes 6291456 | tf_op jit(solution)/shard_map/pallas_call | solution.py:218
  8.6 0.0 copy-start.1
  8.6 0.0 copy-start.2
  8.7 0.0 copy-start.6
  8.7 3.3 %collective-permute-done.1.refs_5_ = bf16[33,16,128]{2,1,0:T(8,128)(2,1)S(1)} collective-permute-done((bf16[33,16,128]{2,1,0:T(8,128)(2,1)S(1)}, bf16[33,16,128]{2,1,0:T(8,128)(2,1)S(1)}, u32[]{:S(2)}, u32[]{:S(2)}) %collective-permute-start.1) | collective-permute-done | bytes 135200 | tf_op jit(solution)/shard_map/ppermute | solution.py:235
  12.0 0.0 copy-done
  12.0 0.0 copy-done.3
  12.0 0.0 copy-done.4
  12.0 0.0 copy-done.5
  12.0 1.0 %shard_map.132 = (f32[8,8192]{1,0:T(8,128)S(1)}, f32[8,128]{1,0:T(8,128)S(1)}, bf16[17,16,128]{2,1,0:T(8,128)(2,1)S(1)}) custom-call(s32[1]{0:T(128)S(6)} %copy.16.refs_0_.count, s32[96]{0:T(128)S(4)} %get-tuple-element.19.refs_1_, s32[96]{0:T(128)S(4)} %get-tuple-element.20.refs_2_, bf16[96,128,128]{2,1,0:T(8,128)(2,1)S(1)} %shard_map.131.refs_3_, ...), custom_call_target="tpu_custom_call" | custom-call | tf_op jit(solution)/shard_map/pallas_call | solution.py:218
  13.0 3.3 %collective-permute-start.4 = (bf16[17,16,128]{2,1,0:T(8,128)(2,1)S(1)}, bf16[17,16,128]{2,1,0:T(8,128)(2,1)S(1)}, u32[]{:S(2)}, u32[]{:S(2)}) collective-permute-start(bf16[17,16,128]{2,1,0:T(8,128)(2,1)S(1)} %get-tuple-element.23.refs_4_), channel_id=1, source_target_pairs={{0,3},{1,2},{2,1},{3,0},{4,7},{5,6},{6,5},{7,4},{8,11},{9,10},{10,... | collective-permute-start | bytes 208904 | tf_op jit(solution)/shard_map/ppermute | solution.py:235
  16.3 0.0 collective-permute-start.3
  16.3 1.1 %collective-permute-start.2 = (bf16[17,16,128]{2,1,0:T(8,128)(2,1)S(1)}, bf16[17,16,128]{2,1,0:T(8,128)(2,1)S(1)}, u32[]{:S(2)}, u32[]{:S(2)}) collective-permute-start(bf16[17,16,128]{2,1,0:T(8,128)(2,1)S(1)} %get-tuple-element.23.refs_4_), channel_id=1, source_target_pairs={{0,1},{1,0},{2,3},{3,2},{4,5},{5,4},{6,7},{7,6},{8,9},{9,8},{10,11... | collective-permute-start | bytes 208904 | tf_op jit(solution)/shard_map/ppermute | solution.py:235
  17.4 2.0 %collective-permute-done.4.refs_7_ = bf16[17,16,128]{2,1,0:T(8,128)(2,1)S(1)} collective-permute-done((bf16[17,16,128]{2,1,0:T(8,128)(2,1)S(1)}, bf16[17,16,128]{2,1,0:T(8,128)(2,1)S(1)}, u32[]{:S(2)}, u32[]{:S(2)}) %collective-permute-start.4) | collective-permute-done | bytes 69664 | tf_op jit(solution)/shard_map/ppermute | solution.py:235
  19.4 2.6 %collective-permute-done.3.refs_6_ = bf16[17,16,128]{2,1,0:T(8,128)(2,1)S(1)} collective-permute-done((bf16[17,16,128]{2,1,0:T(8,128)(2,1)S(1)}, bf16[17,16,128]{2,1,0:T(8,128)(2,1)S(1)}, u32[]{:S(2)}, u32[]{:S(2)}) %collective-permute-start.3) | collective-permute-done | bytes 69664 | tf_op jit(solution)/shard_map/ppermute | solution.py:235
  22.0 0.0 collective-permute-done.2.refs_5_
  22.1 0.0 copy-done.1
  22.1 0.0 copy-done.2
  22.1 0.0 copy-done.6
  22.1 0.7 %shard_map.133 = (f32[8,4096]{1,0:T(8,128)S(1)}, f32[8,128]{1,0:T(8,128)S(1)}, bf16[33,16,128]{2,1,0:T(8,128)(2,1)S(1)}) custom-call(s32[1]{0:T(128)S(6)} %copy.16.refs_0_.count, s32[96]{0:T(128)S(4)} %get-tuple-element.19.refs_1_, s32[96]{0:T(128)S(4)} %get-tuple-element.20.refs_2_, bf16[96,128,128]{2,1,0:T(8,128)(2,1)S(1)} %get-tuple-element.21.tiles.refs_3_, ...), custom_call_target="tpu_custom_call" | custom-call | tf_op jit(solution)/shard_map/pallas_call | solution.py:218
  22.8 0.1 collective-permute-start.5
  22.9 1.3 %collective-permute-done.5 = bf16[33,16,128]{2,1,0:T(8,128)(2,1)S(1)} collective-permute-done((bf16[33,16,128]{2,1,0:T(8,128)(2,1)S(1)}, bf16[33,16,128]{2,1,0:T(8,128)(2,1)S(1)}, u32[]{:S(2)}, u32[]{:S(2)}) %collective-permute-start.5) | collective-permute-done | bytes 135200 | tf_op jit(solution)/shard_map/ppermute | solution.py:235
  24.3 2.2 %collective-permute-start.6 = (bf16[33,16,128]{2,1,0:T(8,128)(2,1)S(1)}, bf16[33,16,128]{2,1,0:T(8,128)(2,1)S(1)}, u32[]{:S(2)}, u32[]{:S(2)}) collective-permute-start(bf16[33,16,128]{2,1,0:T(8,128)(2,1)S(1)} %add_convert_fusion.refs_4_), channel_id=1, source_target_pairs={{0,8},{4,12},{8,0},{12,4},{1,9},{5,13},{9,1},{13,5},{2,10},{6,14},... | collective-permute-start | bytes 405512 | tf_op jit(solution)/shard_map/ppermute | solution.py:235
  26.5 3.9 %collective-permute-done.6.refs_5_ = bf16[33,16,128]{2,1,0:T(8,128)(2,1)S(1)} collective-permute-done((bf16[33,16,128]{2,1,0:T(8,128)(2,1)S(1)}, bf16[33,16,128]{2,1,0:T(8,128)(2,1)S(1)}, u32[]{:S(2)}, u32[]{:S(2)}) %collective-permute-start.6) | collective-permute-done | bytes 135200 | tf_op jit(solution)/shard_map/ppermute | solution.py:235
  30.4 1.1 %shard_map.134 = (f32[8,8192]{1,0:T(8,128)S(1)}, f32[8,128]{1,0:T(8,128)S(1)}, bf16[17,16,128]{2,1,0:T(8,128)(2,1)S(1)}) custom-call(s32[1]{0:T(128)S(6)} %copy.16.refs_0_.count, s32[96]{0:T(128)S(4)} %get-tuple-element.19.refs_1_, s32[96]{0:T(128)S(4)} %get-tuple-element.20.refs_2_, bf16[96,128,128]{2,1,0:T(8,128)(2,1)S(1)} %shard_map.131.refs_3_, ...), custom_call_target="tpu_custom_call" | custom-call | tf_op jit(solution)/shard_map/pallas_call | solution.py:218
  31.5 1.8 %collective-permute-start.9 = (bf16[17,16,128]{2,1,0:T(8,128)(2,1)S(1)}, bf16[17,16,128]{2,1,0:T(8,128)(2,1)S(1)}, u32[]{:S(2)}, u32[]{:S(2)}) collective-permute-start(bf16[17,16,128]{2,1,0:T(8,128)(2,1)S(1)} %get-tuple-element.29.refs_0_), channel_id=1, source_target_pairs={{0,3},{1,2},{2,1},{3,0},{4,7},{5,6},{6,5},{7,4},{8,11},{9,10},{10,... | collective-permute-start | bytes 208904 | tf_op jit(solution)/shard_map/ppermute | solution.py:235
  33.3 0.0 collective-permute-start.8
  33.3 2.7 %collective-permute-start.7 = (bf16[17,16,128]{2,1,0:T(8,128)(2,1)S(1)}, bf16[17,16,128]{2,1,0:T(8,128)(2,1)S(1)}, u32[]{:S(2)}, u32[]{:S(2)}) collective-permute-start(bf16[17,16,128]{2,1,0:T(8,128)(2,1)S(1)} %get-tuple-element.29.refs_0_), channel_id=1, source_target_pairs={{0,1},{1,0},{2,3},{3,2},{4,5},{5,4},{6,7},{7,6},{8,9},{9,8},{10,11... | collective-permute-start | bytes 208904 | tf_op jit(solution)/shard_map/ppermute | solution.py:235
  36.0 0.7 %copy.14 = f32[8,8192]{1,0:T(8,128)} copy(f32[8,8192]{1,0:T(8,128)S(1)} %get-tuple-element.35) | data formatting | bytes 524288
  36.7 0.1 slice_reduce_fusion
  36.8 1.7 %collective-permute-done.9.refs_3_ = bf16[17,16,128]{2,1,0:T(8,128)(2,1)S(1)} collective-permute-done((bf16[17,16,128]{2,1,0:T(8,128)(2,1)S(1)}, bf16[17,16,128]{2,1,0:T(8,128)(2,1)S(1)}, u32[]{:S(2)}, u32[]{:S(2)}) %collective-permute-start.9) | collective-permute-done | bytes 69664 | tf_op jit(solution)/shard_map/ppermute | solution.py:235
  38.4 1.6 %collective-permute-done.8.refs_2_ = bf16[17,16,128]{2,1,0:T(8,128)(2,1)S(1)} collective-permute-done((bf16[17,16,128]{2,1,0:T(8,128)(2,1)S(1)}, bf16[17,16,128]{2,1,0:T(8,128)(2,1)S(1)}, u32[]{:S(2)}, u32[]{:S(2)}) %collective-permute-start.8) | collective-permute-done | bytes 69664 | tf_op jit(solution)/shard_map/ppermute | solution.py:235
  40.0 0.0 collective-permute-done.7.refs_1_
  40.0 0.2 shard_map.135
  40.2 0.0 collective-permute-start.12
  40.2 1.7 %collective-permute-start.11 = (f32[8,128]{1,0:T(8,128)S(1)}, f32[8,128]{1,0:T(8,128)S(1)}, u32[]{:S(2)}, u32[]{:S(2)}) collective-permute-start(f32[8,128]{1,0:T(8,128)S(1)} %get-tuple-element.33), channel_id=1, source_target_pairs={{0,8},{4,12},{8,0},{12,4},{1,9},{5,13},{9,1},{13,5},{2,10},{6,14},... | collective-permute-start | bytes 12296 | tf_op jit(solution)/shard_map/ppermute | solution.py:235
  42.0 0.1 collective-permute-start.10
  42.1 0.1 add_reduce_fusion
  42.2 0.7 %copy.15 = f32[8,4096]{1,0:T(8,128)} copy(f32[8,4096]{1,0:T(8,128)S(1)} %get-tuple-element.36) | data formatting | bytes 262144
  42.9 0.4 collective-permute-done.12
  43.3 0.7 %collective-permute-done.11 = f32[8,128]{1,0:T(8,128)S(1)} collective-permute-done((f32[8,128]{1,0:T(8,128)S(1)}, f32[8,128]{1,0:T(8,128)S(1)}, u32[]{:S(2)}, u32[]{:S(2)}) %collective-permute-start.11) | collective-permute-done | bytes 4128 | tf_op jit(solution)/shard_map/ppermute | solution.py:235
  43.9 0.0 collective-permute-done.10
  43.9 0.1 add_reduce_fusion.1
  44.0 0.5 %multiply_sqrt_fusion = f32[8]{0:T(128)} fusion(f32[8]{0:T(128)S(1)} %slice_reduce_fusion, f32[8]{0:T(128)S(1)} %add_reduce_fusion, f32[8]{0:T(128)S(1)} %add_reduce_fusion.1), kind=kLoop, calls=%fused_computation.5 | loop fusion | flops 24 | bytes 128 | tf_op jit(solution)/shard_map/sqrt | solution.py:346
  (7 shorter events, 0.1 us)
Async XLA Ops:
  3.3 1.5 %collective-permute-start = (bf16[33,16,128]{2,1,0:T(8,128)(2,1)S(1)}, bf16[33,16,128]{2,1,0:T(8,128)(2,1)S(1)}, u32[]{:S(2)}, u32[]{:S(2)}) collective-permute-start(bf16[33,16,128]{2,1,0:T(8,128)(2,1)S(1)} %get-tuple-element.22), channel_id=1, source_target_pairs={{0,4},{4,0},{8,12},{12,8},{1,5},{5,1},{9,13},{13,9},{2,6},{6,2},{1... | collective-permute-start | bytes 405512 | tf_op jit(solution)/shard_map/ppermute | solution.py:235
  4.8 7.1 %collective-permute-start.1 = (bf16[33,16,128]{2,1,0:T(8,128)(2,1)S(1)}, bf16[33,16,128]{2,1,0:T(8,128)(2,1)S(1)}, u32[]{:S(2)}, u32[]{:S(2)}) collective-permute-start(bf16[33,16,128]{2,1,0:T(8,128)(2,1)S(1)} %add_convert_fusion.1.after.refs_4_), channel_id=1, source_target_pairs={{0,8},{4,12},{8,0},{12,4},{1,9},{5,13},{9,1},{13,5},{2,10},{6,14},... | collective-permute-start | bytes 405512 | tf_op jit(solution)/shard_map/ppermute | solution.py:235
  8.1 3.9 %copy-start = (f32[8,8192]{1,0:T(8,128)S(1)}, f32[8,8192]{1,0:T(8,128)}, u32[]{:S(2)}) copy-start(f32[8,8192]{1,0:T(8,128)} %refs_12_.5) | copy-start | bytes 786436
  8.1 3.9 %copy-start.3 = (f32[8192]{0:T(1024)S(1)}, f32[8192]{0:T(1024)}, u32[]{:S(2)}) copy-start(f32[8192]{0:T(1024)} %param.15) | copy-start | bytes 98308
  8.1 3.9 %copy-start.4 = (f32[8192]{0:T(1024)S(1)}, f32[8192]{0:T(1024)}, u32[]{:S(2)}) copy-start(f32[8192]{0:T(1024)} %param.17) | copy-start | bytes 98308
  8.1 3.9 %copy-start.5 = (s32[8192]{0:T(1024)S(1)}, s32[8192]{0:T(1024)}, u32[]{:S(2)}) copy-start(s32[8192]{0:T(1024)} %param.18) | copy-start | bytes 98308
  8.6 13.4 %copy-start.1 = (f32[8,4096]{1,0:T(8,128)S(1)}, f32[8,4096]{1,0:T(8,128)}, u32[]{:S(2)}) copy-start(f32[8,4096]{1,0:T(8,128)} %refs_8_.1) | copy-start | bytes 393220
  8.6 13.4 %copy-start.2 = (f32[8,4096]{1,0:T(8,128)S(1)}, f32[8,4096]{1,0:T(8,128)}, u32[]{:S(2)}) copy-start(f32[8,4096]{1,0:T(8,128)} %refs_5_.1) | copy-start | bytes 393220
  8.7 13.4 %copy-start.6 = (s32[4096]{0:T(1024)S(1)}, s32[4096]{0:T(1024)}, u32[]{:S(2)}) copy-start(s32[4096]{0:T(1024)} %param.19) | copy-start | bytes 49156
  13.0 6.4 %collective-permute-start.4 = (bf16[17,16,128]{2,1,0:T(8,128)(2,1)S(1)}, bf16[17,16,128]{2,1,0:T(8,128)(2,1)S(1)}, u32[]{:S(2)}, u32[]{:S(2)}) collective-permute-start(bf16[17,16,128]{2,1,0:T(8,128)(2,1)S(1)} %get-tuple-element.23.refs_4_), channel_id=1, source_target_pairs={{0,3},{1,2},{2,1},{3,0},{4,7},{5,6},{6,5},{7,4},{8,11},{9,10},{10,... | collective-permute-start | bytes 208904 | tf_op jit(solution)/shard_map/ppermute | solution.py:235
  16.3 5.7 %collective-permute-start.3 = (bf16[17,16,128]{2,1,0:T(8,128)(2,1)S(1)}, bf16[17,16,128]{2,1,0:T(8,128)(2,1)S(1)}, u32[]{:S(2)}, u32[]{:S(2)}) collective-permute-start(bf16[17,16,128]{2,1,0:T(8,128)(2,1)S(1)} %get-tuple-element.23.refs_4_), channel_id=1, source_target_pairs={{0,2},{1,3},{2,0},{3,1},{4,6},{5,7},{6,4},{7,5},{8,10},{9,11},{10,... | collective-permute-start | bytes 208904 | tf_op jit(solution)/shard_map/ppermute | solution.py:235
  16.3 5.7 %collective-permute-start.2 = (bf16[17,16,128]{2,1,0:T(8,128)(2,1)S(1)}, bf16[17,16,128]{2,1,0:T(8,128)(2,1)S(1)}, u32[]{:S(2)}, u32[]{:S(2)}) collective-permute-start(bf16[17,16,128]{2,1,0:T(8,128)(2,1)S(1)} %get-tuple-element.23.refs_4_), channel_id=1, source_target_pairs={{0,1},{1,0},{2,3},{3,2},{4,5},{5,4},{6,7},{7,6},{8,9},{9,8},{10,11... | collective-permute-start | bytes 208904 | tf_op jit(solution)/shard_map/ppermute | solution.py:235
  22.8 1.4 %collective-permute-start.5 = (bf16[33,16,128]{2,1,0:T(8,128)(2,1)S(1)}, bf16[33,16,128]{2,1,0:T(8,128)(2,1)S(1)}, u32[]{:S(2)}, u32[]{:S(2)}) collective-permute-start(bf16[33,16,128]{2,1,0:T(8,128)(2,1)S(1)} %get-tuple-element.25), channel_id=1, source_target_pairs={{0,4},{4,0},{8,12},{12,8},{1,5},{5,1},{9,13},{13,9},{2,6},{6,2},{1... | collective-permute-start | bytes 405512 | tf_op jit(solution)/shard_map/ppermute | solution.py:235
  24.3 6.1 %collective-permute-start.6 = (bf16[33,16,128]{2,1,0:T(8,128)(2,1)S(1)}, bf16[33,16,128]{2,1,0:T(8,128)(2,1)S(1)}, u32[]{:S(2)}, u32[]{:S(2)}) collective-permute-start(bf16[33,16,128]{2,1,0:T(8,128)(2,1)S(1)} %add_convert_fusion.refs_4_), channel_id=1, source_target_pairs={{0,8},{4,12},{8,0},{12,4},{1,9},{5,13},{9,1},{13,5},{2,10},{6,14},... | collective-permute-start | bytes 405512 | tf_op jit(solution)/shard_map/ppermute | solution.py:235
  31.5 6.9 %collective-permute-start.9 = (bf16[17,16,128]{2,1,0:T(8,128)(2,1)S(1)}, bf16[17,16,128]{2,1,0:T(8,128)(2,1)S(1)}, u32[]{:S(2)}, u32[]{:S(2)}) collective-permute-start(bf16[17,16,128]{2,1,0:T(8,128)(2,1)S(1)} %get-tuple-element.29.refs_0_), channel_id=1, source_target_pairs={{0,3},{1,2},{2,1},{3,0},{4,7},{5,6},{6,5},{7,4},{8,11},{9,10},{10,... | collective-permute-start | bytes 208904 | tf_op jit(solution)/shard_map/ppermute | solution.py:235
  33.3 6.8 %collective-permute-start.8 = (bf16[17,16,128]{2,1,0:T(8,128)(2,1)S(1)}, bf16[17,16,128]{2,1,0:T(8,128)(2,1)S(1)}, u32[]{:S(2)}, u32[]{:S(2)}) collective-permute-start(bf16[17,16,128]{2,1,0:T(8,128)(2,1)S(1)} %get-tuple-element.29.refs_0_), channel_id=1, source_target_pairs={{0,2},{1,3},{2,0},{3,1},{4,6},{5,7},{6,4},{7,5},{8,10},{9,11},{10,... | collective-permute-start | bytes 208904 | tf_op jit(solution)/shard_map/ppermute | solution.py:235
  33.3 6.8 %collective-permute-start.7 = (bf16[17,16,128]{2,1,0:T(8,128)(2,1)S(1)}, bf16[17,16,128]{2,1,0:T(8,128)(2,1)S(1)}, u32[]{:S(2)}, u32[]{:S(2)}) collective-permute-start(bf16[17,16,128]{2,1,0:T(8,128)(2,1)S(1)} %get-tuple-element.29.refs_0_), channel_id=1, source_target_pairs={{0,1},{1,0},{2,3},{3,2},{4,5},{5,4},{6,7},{7,6},{8,9},{9,8},{10,11... | collective-permute-start | bytes 208904 | tf_op jit(solution)/shard_map/ppermute | solution.py:235
  40.2 3.1 %collective-permute-start.12 = (f32[8,128]{1,0:T(8,128)S(1)}, f32[8,128]{1,0:T(8,128)S(1)}, u32[]{:S(2)}, u32[]{:S(2)}) collective-permute-start(f32[8,128]{1,0:T(8,128)S(1)} %get-tuple-element.33), channel_id=1, source_target_pairs={{0,12},{4,8},{8,4},{12,0},{1,13},{5,9},{9,5},{13,1},{2,14},{6,10},... | collective-permute-start | bytes 12296 | tf_op jit(solution)/shard_map/ppermute | solution.py:235
  40.2 3.7 %collective-permute-start.11 = (f32[8,128]{1,0:T(8,128)S(1)}, f32[8,128]{1,0:T(8,128)S(1)}, u32[]{:S(2)}, u32[]{:S(2)}) collective-permute-start(f32[8,128]{1,0:T(8,128)S(1)} %get-tuple-element.33), channel_id=1, source_target_pairs={{0,8},{4,12},{8,0},{12,4},{1,9},{5,13},{9,1},{13,5},{2,10},{6,14},... | collective-permute-start | bytes 12296 | tf_op jit(solution)/shard_map/ppermute | solution.py:235
  42.0 2.0 %collective-permute-start.10 = (f32[8,128]{1,0:T(8,128)S(1)}, f32[8,128]{1,0:T(8,128)S(1)}, u32[]{:S(2)}, u32[]{:S(2)}) collective-permute-start(f32[8,128]{1,0:T(8,128)S(1)} %get-tuple-element.33), channel_id=1, source_target_pairs={{0,4},{4,0},{8,12},{12,8},{1,5},{5,1},{9,13},{13,9},{2,6},{6,2},{1... | collective-permute-start | bytes 12296 | tf_op jit(solution)/shard_map/ppermute | solution.py:235

commit v5 on v4

--- a/solution.py
+++ b/solution.py
@@ -63,10 +63,7 @@
 
     for first in range(0, total, PART):
         size = min(PART, total - first)
-        if first == 0:
-            part(first, size)
-        else:
-            pl.when(first < live)(functools.partial(part, first, size))
+        pl.when(first < live)(functools.partial(part, first, size))
 
 
 def pack(acc, out, norm, slot):
@@ -112,15 +109,13 @@
     for n, first in enumerate(range(0, tiles.shape[0], PART)):
         span = pl.ds(first, min(PART, tiles.shape[0] - first))
         get_tiles[first] = pltpu.make_async_copy(tiles_far.at[span], tiles.at[span], sems.at[3 + n])
-        get_tiles[first].start()
+        pl.when(first < count[0])(get_tiles[first].start)
     get_dual.wait()
     for b in range(source.shape[0]):
         source[b] = split_rows(dual[:, b * tile : (b + 1) * tile])
     for copy in copies:
         copy.wait()
     tile_products((count, rows, cols), tiles, source, acc, True, lambda first: get_tiles[first].wait())
-    for first in list(get_tiles)[1:]:
-        pl.when(first >= count[0])(get_tiles[first].wait)
     pack(acc, out, 0.0, 0)
 
 
@@ -179,6 +174,7 @@
         grid, tiles, refs = refs[:3], refs[3], refs[4:]
     slot = lax.axis_index("rowblk")
     parts = refs[:n_parts]
+    parts = [parts[0], parts[2], parts[1], parts[3]]
     refs = refs[n_parts:]
     weight, demand, flag, dual, start = refs[:5]
     if last:
@@ -321,6 +317,7 @@
             [*to_rows, sems],
         )
         parts = butterfly(terms, "colblk", 4)
+        parts = [parts[0]] + [parts[m] for m in (2, 1, 3)]
         vectors = [*parts, weight, demand, row_flag, dual, dual_start]
         if last:
             dual, primal_norm, terms = call(

time: 44.9 us -> 45.1 us (level); the launches traced: 44.6 us -> 45.3 us
  waiting for transfers between devices: 18.5 us -> 20 us
  Pallas kernels: 5.51 us -> 4.06 us
  starting transfers between devices: 16.8 us -> 17.5 us
    ppermute x13, waiting for transfers between devices: 18.5 us -> 20 us  [swap(): return lax.ppermute(value, axis, [(i, i ^ mask) for i in range(size)])]
    pallas_call x6, Pallas kernels: 5.51 us -> 4.06 us  [call(): pl.pallas_call(kernel, out_shape=outputs, in_specs=in_specs, out_specs=ou...]
    ppermute x13, starting transfers between devices: 16.8 us -> 17.5 us  [swap(): return lax.ppermute(value, axis, [(i, i ^ mask) for i in range(size)])]
  transfers between devices with their start and end apart: 13 -> 13, of which waited for: 10 -> 12; matrix products, arithmetic and copies ran while one was open for 4% -> 4% of each run, Pallas kernels for 1% -> 1%
where the time goes in v5:
time: 45.1 us; the launch traced here: 45.3 us
  waiting for transfers between devices  20 us (44%)
  starting transfers between devices  17.5 us (39%)
  Pallas kernels  4.06 us (9%)
  local copies, waits for them, and re-layouts  1.51 us (3%)
  between operations  1.4 us (3%)
  other arithmetic  0.85 us (2%)
    ppermute x13, waiting for transfers between devices, swap(): return lax.ppermute(value, axis, [(i, i ^ mask) for i in range(size)])  20 us
    ppermute x13, starting transfers between devices, swap(): return lax.ppermute(value, axis, [(i, i ^ mask) for i in range(size)])  17.5 us
    pallas_call x6, Pallas kernels, call(): pl.pallas_call(kernel, out_shape=outputs, in_specs=in_specs, out_specs=ou...  4.06 us
    unnamed x16, local copies, waits for them, and re-layouts  1.39 us
  transfers between devices with their start and end apart: 13, of which 12 were waited for; matrix products, arithmetic and copies ran while one was open for 4% of the time, Pallas kernels for 1%

profile of v5, /device:TPU:0, one launch (start us, length us, event | category | flops | bytes accessed | tf_op | source)
XLA Modules:
  0.0 45.3 jit_solution(6224847566876787054)
XLA Ops:
  1.3 1.6 %shard_map.130 = (bf16[33,16,128]{2,1,0:T(8,128)(2,1)S(1)}, bf16[96,128,128]{2,1,0:T(8,128)(2,1)S(1)}, s32[96]{0:T(128)S(4)}, s32[96]{0:T(128)S(4)}) custom-call(s32[1]{0:T(128)S(6)} %copy.16.refs_0_.count, s32[96]{0:T(128)} %refs_1_.1, s32[96]{0:T(128)} %refs_2_.1, bf16[96,128,128]{2,1,0:T(8,128)(2,1)} %refs_3_.1, f32[8,4096]{1,0:T(8,128)} %refs_8_.1), custom_call_target="tpu_custom_call" | custom-call | tf_op jit(solution)/shard_map/pallas_call | solution.py:214
  2.9 0.8 %collective-permute-start = (bf16[33,16,128]{2,1,0:T(8,128)(2,1)S(1)}, bf16[33,16,128]{2,1,0:T(8,128)(2,1)S(1)}, u32[]{:S(2)}, u32[]{:S(2)}) collective-permute-start(bf16[33,16,128]{2,1,0:T(8,128)(2,1)S(1)} %get-tuple-element.22), channel_id=1, source_target_pairs={{0,4},{4,0},{8,12},{12,8},{1,5},{5,1},{9,13},{13,9},{2,6},{6,2},{1... | collective-permute-start | bytes 405512 | tf_op jit(solution)/shard_map/ppermute | solution.py:231
  3.6 1.0 %collective-permute-done = bf16[33,16,128]{2,1,0:T(8,128)(2,1)S(1)} collective-permute-done((bf16[33,16,128]{2,1,0:T(8,128)(2,1)S(1)}, bf16[33,16,128]{2,1,0:T(8,128)(2,1)S(1)}, u32[]{:S(2)}, u32[]{:S(2)}) %collective-permute-start) | collective-permute-done | bytes 135200 | tf_op jit(solution)/shard_map/ppermute | solution.py:231
  4.7 2.9 %collective-permute-start.1 = (bf16[33,16,128]{2,1,0:T(8,128)(2,1)S(1)}, bf16[33,16,128]{2,1,0:T(8,128)(2,1)S(1)}, u32[]{:S(2)}, u32[]{:S(2)}) collective-permute-start(bf16[33,16,128]{2,1,0:T(8,128)(2,1)S(1)} %add_convert_fusion.1.after.refs_4_), channel_id=1, source_target_pairs={{0,8},{4,12},{8,0},{12,4},{1,9},{5,13},{9,1},{13,5},{2,10},{6,14},... | collective-permute-start | bytes 405512 | tf_op jit(solution)/shard_map/ppermute | solution.py:231
  7.6 0.3 shard_map.131.refs_3_
  7.9 0.0 copy-start.1
  7.9 0.0 copy-start.2
  7.9 0.0 copy-start.6
  7.9 3.6 %collective-permute-done.1.refs_5_ = bf16[33,16,128]{2,1,0:T(8,128)(2,1)S(1)} collective-permute-done((bf16[33,16,128]{2,1,0:T(8,128)(2,1)S(1)}, bf16[33,16,128]{2,1,0:T(8,128)(2,1)S(1)}, u32[]{:S(2)}, u32[]{:S(2)}) %collective-permute-start.1) | collective-permute-done | bytes 135200 | tf_op jit(solution)/shard_map/ppermute | solution.py:231
  11.5 0.0 copy-done
  11.5 0.0 copy-done.3
  11.5 0.0 copy-done.4
  11.5 0.0 copy-done.5
  11.5 0.7 %shard_map.132 = (f32[8,8192]{1,0:T(8,128)S(1)}, f32[8,128]{1,0:T(8,128)S(1)}, bf16[17,16,128]{2,1,0:T(8,128)(2,1)S(1)}) custom-call(s32[1]{0:T(128)S(6)} %copy.16.refs_0_.count, s32[96]{0:T(128)S(4)} %get-tuple-element.19.refs_1_, s32[96]{0:T(128)S(4)} %get-tuple-element.20.refs_2_, bf16[96,128,128]{2,1,0:T(8,128)(2,1)S(1)} %shard_map.131.refs_3_, ...), custom_call_target="tpu_custom_call" | custom-call | tf_op jit(solution)/shard_map/pallas_call | solution.py:214
  12.2 4.4 %collective-permute-start.4 = (bf16[17,16,128]{2,1,0:T(8,128)(2,1)S(1)}, bf16[17,16,128]{2,1,0:T(8,128)(2,1)S(1)}, u32[]{:S(2)}, u32[]{:S(2)}) collective-permute-start(bf16[17,16,128]{2,1,0:T(8,128)(2,1)S(1)} %get-tuple-element.23.refs_4_), channel_id=1, source_target_pairs={{0,3},{1,2},{2,1},{3,0},{4,7},{5,6},{6,5},{7,4},{8,11},{9,10},{10,... | collective-permute-start | bytes 208904 | tf_op jit(solution)/shard_map/ppermute | solution.py:231
  16.7 0.0 collective-permute-start.3
  16.7 0.6 %collective-permute-start.2 = (bf16[17,16,128]{2,1,0:T(8,128)(2,1)S(1)}, bf16[17,16,128]{2,1,0:T(8,128)(2,1)S(1)}, u32[]{:S(2)}, u32[]{:S(2)}) collective-permute-start(bf16[17,16,128]{2,1,0:T(8,128)(2,1)S(1)} %get-tuple-element.23.refs_4_), channel_id=1, source_target_pairs={{0,2},{1,3},{2,0},{3,1},{4,6},{5,7},{6,4},{7,5},{8,10},{9,11},{10,... | collective-permute-start | bytes 208904 | tf_op jit(solution)/shard_map/ppermute | solution.py:231
  17.3 2.1 %collective-permute-done.4.refs_7_ = bf16[17,16,128]{2,1,0:T(8,128)(2,1)S(1)} collective-permute-done((bf16[17,16,128]{2,1,0:T(8,128)(2,1)S(1)}, bf16[17,16,128]{2,1,0:T(8,128)(2,1)S(1)}, u32[]{:S(2)}, u32[]{:S(2)}) %collective-permute-start.4) | collective-permute-done | bytes 69664 | tf_op jit(solution)/shard_map/ppermute | solution.py:231
  19.4 2.0 %collective-permute-done.3.refs_6_ = bf16[17,16,128]{2,1,0:T(8,128)(2,1)S(1)} collective-permute-done((bf16[17,16,128]{2,1,0:T(8,128)(2,1)S(1)}, bf16[17,16,128]{2,1,0:T(8,128)(2,1)S(1)}, u32[]{:S(2)}, u32[]{:S(2)}) %collective-permute-start.3) | collective-permute-done | bytes 69664 | tf_op jit(solution)/shard_map/ppermute | solution.py:231
  21.4 0.7 %collective-permute-done.2.refs_5_ = bf16[17,16,128]{2,1,0:T(8,128)(2,1)S(1)} collective-permute-done((bf16[17,16,128]{2,1,0:T(8,128)(2,1)S(1)}, bf16[17,16,128]{2,1,0:T(8,128)(2,1)S(1)}, u32[]{:S(2)}, u32[]{:S(2)}) %collective-permute-start.2) | collective-permute-done | bytes 69664 | tf_op jit(solution)/shard_map/ppermute | solution.py:231
  22.1 0.0 copy-done.1
  22.1 0.0 copy-done.2
  22.1 0.0 copy-done.6
  22.1 0.5 %shard_map.133 = (f32[8,4096]{1,0:T(8,128)S(1)}, f32[8,128]{1,0:T(8,128)S(1)}, bf16[33,16,128]{2,1,0:T(8,128)(2,1)S(1)}) custom-call(s32[1]{0:T(128)S(6)} %copy.16.refs_0_.count, s32[96]{0:T(128)S(4)} %get-tuple-element.19.refs_1_, s32[96]{0:T(128)S(4)} %get-tuple-element.20.refs_2_, bf16[96,128,128]{2,1,0:T(8,128)(2,1)S(1)} %get-tuple-element.21.tiles.refs_3_, ...), custom_call_target="tpu_custom_call" | custom-call | tf_op jit(solution)/shard_map/pallas_call | solution.py:214
  22.6 0.1 collective-permute-start.5
  22.7 1.3 %collective-permute-done.5 = bf16[33,16,128]{2,1,0:T(8,128)(2,1)S(1)} collective-permute-done((bf16[33,16,128]{2,1,0:T(8,128)(2,1)S(1)}, bf16[33,16,128]{2,1,0:T(8,128)(2,1)S(1)}, u32[]{:S(2)}, u32[]{:S(2)}) %collective-permute-start.5) | collective-permute-done | bytes 135200 | tf_op jit(solution)/shard_map/ppermute | solution.py:231
  24.1 2.3 %collective-permute-start.6 = (bf16[33,16,128]{2,1,0:T(8,128)(2,1)S(1)}, bf16[33,16,128]{2,1,0:T(8,128)(2,1)S(1)}, u32[]{:S(2)}, u32[]{:S(2)}) collective-permute-start(bf16[33,16,128]{2,1,0:T(8,128)(2,1)S(1)} %add_convert_fusion.refs_4_), channel_id=1, source_target_pairs={{0,8},{4,12},{8,0},{12,4},{1,9},{5,13},{9,1},{13,5},{2,10},{6,14},... | collective-permute-start | bytes 405512 | tf_op jit(solution)/shard_map/ppermute | solution.py:231
  26.4 3.9 %collective-permute-done.6.refs_5_ = bf16[33,16,128]{2,1,0:T(8,128)(2,1)S(1)} collective-permute-done((bf16[33,16,128]{2,1,0:T(8,128)(2,1)S(1)}, bf16[33,16,128]{2,1,0:T(8,128)(2,1)S(1)}, u32[]{:S(2)}, u32[]{:S(2)}) %collective-permute-start.6) | collective-permute-done | bytes 135200 | tf_op jit(solution)/shard_map/ppermute | solution.py:231
  30.3 0.8 %shard_map.134 = (f32[8,8192]{1,0:T(8,128)S(1)}, f32[8,128]{1,0:T(8,128)S(1)}, bf16[17,16,128]{2,1,0:T(8,128)(2,1)S(1)}) custom-call(s32[1]{0:T(128)S(6)} %copy.16.refs_0_.count, s32[96]{0:T(128)S(4)} %get-tuple-element.19.refs_1_, s32[96]{0:T(128)S(4)} %get-tuple-element.20.refs_2_, bf16[96,128,128]{2,1,0:T(8,128)(2,1)S(1)} %shard_map.131.refs_3_, ...), custom_call_target="tpu_custom_call" | custom-call | tf_op jit(solution)/shard_map/pallas_call | solution.py:214
  31.1 2.6 %collective-permute-start.9 = (bf16[17,16,128]{2,1,0:T(8,128)(2,1)S(1)}, bf16[17,16,128]{2,1,0:T(8,128)(2,1)S(1)}, u32[]{:S(2)}, u32[]{:S(2)}) collective-permute-start(bf16[17,16,128]{2,1,0:T(8,128)(2,1)S(1)} %get-tuple-element.29.refs_0_), channel_id=1, source_target_pairs={{0,3},{1,2},{2,1},{3,0},{4,7},{5,6},{6,5},{7,4},{8,11},{9,10},{10,... | collective-permute-start | bytes 208904 | tf_op jit(solution)/shard_map/ppermute | solution.py:231
  33.7 0.2 collective-permute-start.8
  33.9 1.7 %collective-permute-start.7 = (bf16[17,16,128]{2,1,0:T(8,128)(2,1)S(1)}, bf16[17,16,128]{2,1,0:T(8,128)(2,1)S(1)}, u32[]{:S(2)}, u32[]{:S(2)}) collective-permute-start(bf16[17,16,128]{2,1,0:T(8,128)(2,1)S(1)} %get-tuple-element.29.refs_0_), channel_id=1, source_target_pairs={{0,2},{1,3},{2,0},{3,1},{4,6},{5,7},{6,4},{7,5},{8,10},{9,11},{10,... | collective-permute-start | bytes 208904 | tf_op jit(solution)/shard_map/ppermute | solution.py:231
  35.6 0.7 %copy.14 = f32[8,8192]{1,0:T(8,128)} copy(f32[8,8192]{1,0:T(8,128)S(1)} %get-tuple-element.35) | data formatting | bytes 524288
  36.3 0.1 slice_reduce_fusion
  36.4 1.4 %collective-permute-done.9.refs_3_ = bf16[17,16,128]{2,1,0:T(8,128)(2,1)S(1)} collective-permute-done((bf16[17,16,128]{2,1,0:T(8,128)(2,1)S(1)}, bf16[17,16,128]{2,1,0:T(8,128)(2,1)S(1)}, u32[]{:S(2)}, u32[]{:S(2)}) %collective-permute-start.9) | collective-permute-done | bytes 69664 | tf_op jit(solution)/shard_map/ppermute | solution.py:231
  37.8 1.2 %collective-permute-done.8.refs_2_ = bf16[17,16,128]{2,1,0:T(8,128)(2,1)S(1)} collective-permute-done((bf16[17,16,128]{2,1,0:T(8,128)(2,1)S(1)}, bf16[17,16,128]{2,1,0:T(8,128)(2,1)S(1)}, u32[]{:S(2)}, u32[]{:S(2)}) %collective-permute-start.8) | collective-permute-done | bytes 69664 | tf_op jit(solution)/shard_map/ppermute | solution.py:231
  39.1 1.7 %collective-permute-done.7.refs_1_ = bf16[17,16,128]{2,1,0:T(8,128)(2,1)S(1)} collective-permute-done((bf16[17,16,128]{2,1,0:T(8,128)(2,1)S(1)}, bf16[17,16,128]{2,1,0:T(8,128)(2,1)S(1)}, u32[]{:S(2)}, u32[]{:S(2)}) %collective-permute-start.7) | collective-permute-done | bytes 69664 | tf_op jit(solution)/shard_map/ppermute | solution.py:231
  40.8 0.2 shard_map.135
  41.0 0.0 collective-permute-start.12
  41.0 0.8 %collective-permute-start.11 = (f32[8,128]{1,0:T(8,128)S(1)}, f32[8,128]{1,0:T(8,128)S(1)}, u32[]{:S(2)}, u32[]{:S(2)}) collective-permute-start(f32[8,128]{1,0:T(8,128)S(1)} %get-tuple-element.33), channel_id=1, source_target_pairs={{0,8},{4,12},{8,0},{12,4},{1,9},{5,13},{9,1},{13,5},{2,10},{6,14},... | collective-permute-start | bytes 12296 | tf_op jit(solution)/shard_map/ppermute | solution.py:231
  41.8 1.0 %collective-permute-start.10 = (f32[8,128]{1,0:T(8,128)S(1)}, f32[8,128]{1,0:T(8,128)S(1)}, u32[]{:S(2)}, u32[]{:S(2)}) collective-permute-start(f32[8,128]{1,0:T(8,128)S(1)} %get-tuple-element.33), channel_id=1, source_target_pairs={{0,4},{4,0},{8,12},{12,8},{1,5},{5,1},{9,13},{13,9},{2,6},{6,2},{1... | collective-permute-start | bytes 12296 | tf_op jit(solution)/shard_map/ppermute | solution.py:231
  42.8 0.1 add_reduce_fusion
  43.0 0.7 %copy.15 = f32[8,4096]{1,0:T(8,128)} copy(f32[8,4096]{1,0:T(8,128)S(1)} %get-tuple-element.36) | data formatting | bytes 262144
  43.6 0.4 collective-permute-done.12
  44.0 0.7 %collective-permute-done.11 = f32[8,128]{1,0:T(8,128)S(1)} collective-permute-done((f32[8,128]{1,0:T(8,128)S(1)}, f32[8,128]{1,0:T(8,128)S(1)}, u32[]{:S(2)}, u32[]{:S(2)}) %collective-permute-start.11) | collective-permute-done | bytes 4128 | tf_op jit(solution)/shard_map/ppermute | solution.py:231
  44.7 0.0 collective-permute-done.10
  44.7 0.1 add_reduce_fusion.1
  44.8 0.5 %multiply_sqrt_fusion = f32[8]{0:T(128)} fusion(f32[8]{0:T(128)S(1)} %slice_reduce_fusion, f32[8]{0:T(128)S(1)} %add_reduce_fusion, f32[8]{0:T(128)S(1)} %add_reduce_fusion.1), kind=kLoop, calls=%fused_computation.5 | loop fusion | flops 24 | bytes 128 | tf_op jit(solution)/shard_map/sqrt | solution.py:343
  (7 shorter events, 0.1 us)
Async XLA Ops:
  2.9 1.8 %collective-permute-start = (bf16[33,16,128]{2,1,0:T(8,128)(2,1)S(1)}, bf16[33,16,128]{2,1,0:T(8,128)(2,1)S(1)}, u32[]{:S(2)}, u32[]{:S(2)}) collective-permute-start(bf16[33,16,128]{2,1,0:T(8,128)(2,1)S(1)} %get-tuple-element.22), channel_id=1, source_target_pairs={{0,4},{4,0},{8,12},{12,8},{1,5},{5,1},{9,13},{13,9},{2,6},{6,2},{1... | collective-permute-start | bytes 405512 | tf_op jit(solution)/shard_map/ppermute | solution.py:231
  4.7 6.8 %collective-permute-start.1 = (bf16[33,16,128]{2,1,0:T(8,128)(2,1)S(1)}, bf16[33,16,128]{2,1,0:T(8,128)(2,1)S(1)}, u32[]{:S(2)}, u32[]{:S(2)}) collective-permute-start(bf16[33,16,128]{2,1,0:T(8,128)(2,1)S(1)} %add_convert_fusion.1.after.refs_4_), channel_id=1, source_target_pairs={{0,8},{4,12},{8,0},{12,4},{1,9},{5,13},{9,1},{13,5},{2,10},{6,14},... | collective-permute-start | bytes 405512 | tf_op jit(solution)/shard_map/ppermute | solution.py:231
  7.6 3.9 %copy-start = (f32[8,8192]{1,0:T(8,128)S(1)}, f32[8,8192]{1,0:T(8,128)}, u32[]{:S(2)}) copy-start(f32[8,8192]{1,0:T(8,128)} %refs_12_.5) | copy-start | bytes 786436
  7.6 3.9 %copy-start.3 = (f32[8192]{0:T(1024)S(1)}, f32[8192]{0:T(1024)}, u32[]{:S(2)}) copy-start(f32[8192]{0:T(1024)} %param.15) | copy-start | bytes 98308
  7.6 3.9 %copy-start.4 = (f32[8192]{0:T(1024)S(1)}, f32[8192]{0:T(1024)}, u32[]{:S(2)}) copy-start(f32[8192]{0:T(1024)} %param.17) | copy-start | bytes 98308
  7.6 3.9 %copy-start.5 = (s32[8192]{0:T(1024)S(1)}, s32[8192]{0:T(1024)}, u32[]{:S(2)}) copy-start(s32[8192]{0:T(1024)} %param.18) | copy-start | bytes 98308
  7.9 14.2 %copy-start.1 = (f32[8,4096]{1,0:T(8,128)S(1)}, f32[8,4096]{1,0:T(8,128)}, u32[]{:S(2)}) copy-start(f32[8,4096]{1,0:T(8,128)} %refs_8_.1) | copy-start | bytes 393220
  7.9 14.2 %copy-start.2 = (f32[8,4096]{1,0:T(8,128)S(1)}, f32[8,4096]{1,0:T(8,128)}, u32[]{:S(2)}) copy-start(f32[8,4096]{1,0:T(8,128)} %refs_5_.1) | copy-start | bytes 393220
  7.9 14.2 %copy-start.6 = (s32[4096]{0:T(1024)S(1)}, s32[4096]{0:T(1024)}, u32[]{:S(2)}) copy-start(s32[4096]{0:T(1024)} %param.19) | copy-start | bytes 49156
  12.2 7.2 %collective-permute-start.4 = (bf16[17,16,128]{2,1,0:T(8,128)(2,1)S(1)}, bf16[17,16,128]{2,1,0:T(8,128)(2,1)S(1)}, u32[]{:S(2)}, u32[]{:S(2)}) collective-permute-start(bf16[17,16,128]{2,1,0:T(8,128)(2,1)S(1)} %get-tuple-element.23.refs_4_), channel_id=1, source_target_pairs={{0,3},{1,2},{2,1},{3,0},{4,7},{5,6},{6,5},{7,4},{8,11},{9,10},{10,... | collective-permute-start | bytes 208904 | tf_op jit(solution)/shard_map/ppermute | solution.py:231
  16.7 4.7 %collective-permute-start.3 = (bf16[17,16,128]{2,1,0:T(8,128)(2,1)S(1)}, bf16[17,16,128]{2,1,0:T(8,128)(2,1)S(1)}, u32[]{:S(2)}, u32[]{:S(2)}) collective-permute-start(bf16[17,16,128]{2,1,0:T(8,128)(2,1)S(1)} %get-tuple-element.23.refs_4_), channel_id=1, source_target_pairs={{0,1},{1,0},{2,3},{3,2},{4,5},{5,4},{6,7},{7,6},{8,9},{9,8},{10,11... | collective-permute-start | bytes 208904 | tf_op jit(solution)/shard_map/ppermute | solution.py:231
  16.7 5.5 %collective-permute-start.2 = (bf16[17,16,128]{2,1,0:T(8,128)(2,1)S(1)}, bf16[17,16,128]{2,1,0:T(8,128)(2,1)S(1)}, u32[]{:S(2)}, u32[]{:S(2)}) collective-permute-start(bf16[17,16,128]{2,1,0:T(8,128)(2,1)S(1)} %get-tuple-element.23.refs_4_), channel_id=1, source_target_pairs={{0,2},{1,3},{2,0},{3,1},{4,6},{5,7},{6,4},{7,5},{8,10},{9,11},{10,... | collective-permute-start | bytes 208904 | tf_op jit(solution)/shard_map/ppermute | solution.py:231
  22.6 1.4 %collective-permute-start.5 = (bf16[33,16,128]{2,1,0:T(8,128)(2,1)S(1)}, bf16[33,16,128]{2,1,0:T(8,128)(2,1)S(1)}, u32[]{:S(2)}, u32[]{:S(2)}) collective-permute-start(bf16[33,16,128]{2,1,0:T(8,128)(2,1)S(1)} %get-tuple-element.25), channel_id=1, source_target_pairs={{0,4},{4,0},{8,12},{12,8},{1,5},{5,1},{9,13},{13,9},{2,6},{6,2},{1... | collective-permute-start | bytes 405512 | tf_op jit(solution)/shard_map/ppermute | solution.py:231
  24.1 6.2 %collective-permute-start.6 = (bf16[33,16,128]{2,1,0:T(8,128)(2,1)S(1)}, bf16[33,16,128]{2,1,0:T(8,128)(2,1)S(1)}, u32[]{:S(2)}, u32[]{:S(2)}) collective-permute-start(bf16[33,16,128]{2,1,0:T(8,128)(2,1)S(1)} %add_convert_fusion.refs_4_), channel_id=1, source_target_pairs={{0,8},{4,12},{8,0},{12,4},{1,9},{5,13},{9,1},{13,5},{2,10},{6,14},... | collective-permute-start | bytes 405512 | tf_op jit(solution)/shard_map/ppermute | solution.py:231
  31.1 6.7 %collective-permute-start.9 = (bf16[17,16,128]{2,1,0:T(8,128)(2,1)S(1)}, bf16[17,16,128]{2,1,0:T(8,128)(2,1)S(1)}, u32[]{:S(2)}, u32[]{:S(2)}) collective-permute-start(bf16[17,16,128]{2,1,0:T(8,128)(2,1)S(1)} %get-tuple-element.29.refs_0_), channel_id=1, source_target_pairs={{0,3},{1,2},{2,1},{3,0},{4,7},{5,6},{6,5},{7,4},{8,11},{9,10},{10,... | collective-permute-start | bytes 208904 | tf_op jit(solution)/shard_map/ppermute | solution.py:231
  33.7 5.4 %collective-permute-start.8 = (bf16[17,16,128]{2,1,0:T(8,128)(2,1)S(1)}, bf16[17,16,128]{2,1,0:T(8,128)(2,1)S(1)}, u32[]{:S(2)}, u32[]{:S(2)}) collective-permute-start(bf16[17,16,128]{2,1,0:T(8,128)(2,1)S(1)} %get-tuple-element.29.refs_0_), channel_id=1, source_target_pairs={{0,1},{1,0},{2,3},{3,2},{4,5},{5,4},{6,7},{7,6},{8,9},{9,8},{10,11... | collective-permute-start | bytes 208904 | tf_op jit(solution)/shard_map/ppermute | solution.py:231
  33.9 6.8 %collective-permute-start.7 = (bf16[17,16,128]{2,1,0:T(8,128)(2,1)S(1)}, bf16[17,16,128]{2,1,0:T(8,128)(2,1)S(1)}, u32[]{:S(2)}, u32[]{:S(2)}) collective-permute-start(bf16[17,16,128]{2,1,0:T(8,128)(2,1)S(1)} %get-tuple-element.29.refs_0_), channel_id=1, source_target_pairs={{0,2},{1,3},{2,0},{3,1},{4,6},{5,7},{6,4},{7,5},{8,10},{9,11},{10,... | collective-permute-start | bytes 208904 | tf_op jit(solution)/shard_map/ppermute | solution.py:231
  41.0 3.0 %collective-permute-start.12 = (f32[8,128]{1,0:T(8,128)S(1)}, f32[8,128]{1,0:T(8,128)S(1)}, u32[]{:S(2)}, u32[]{:S(2)}) collective-permute-start(f32[8,128]{1,0:T(8,128)S(1)} %get-tuple-element.33), channel_id=1, source_target_pairs={{0,12},{4,8},{8,4},{12,0},{1,13},{5,9},{9,5},{13,1},{2,14},{6,10},... | collective-permute-start | bytes 12296 | tf_op jit(solution)/shard_map/ppermute | solution.py:231
  41.0 3.7 %collective-permute-start.11 = (f32[8,128]{1,0:T(8,128)S(1)}, f32[8,128]{1,0:T(8,128)S(1)}, u32[]{:S(2)}, u32[]{:S(2)}) collective-permute-start(f32[8,128]{1,0:T(8,128)S(1)} %get-tuple-element.33), channel_id=1, source_target_pairs={{0,8},{4,12},{8,0},{12,4},{1,9},{5,13},{9,1},{13,5},{2,10},{6,14},... | collective-permute-start | bytes 12296 | tf_op jit(solution)/shard_map/ppermute | solution.py:231
  41.8 2.8 %collective-permute-start.10 = (f32[8,128]{1,0:T(8,128)S(1)}, f32[8,128]{1,0:T(8,128)S(1)}, u32[]{:S(2)}, u32[]{:S(2)}) collective-permute-start(f32[8,128]{1,0:T(8,128)S(1)} %get-tuple-element.33), channel_id=1, source_target_pairs={{0,4},{4,0},{8,12},{12,8},{1,5},{5,1},{9,13},{13,9},{2,6},{6,2},{1... | collective-permute-start | bytes 12296 | tf_op jit(solution)/shard_map/ppermute | solution.py:231

commit v6 on v5

v6 whole, which is shorter than its diff:
```python
import functools

import jax
import jax.numpy as jnp
from jax import lax
from jax.experimental import pallas as pl
from jax.experimental.pallas import tpu as pltpu
from jax.sharding import PartitionSpec as P

ITERS = 2
ETA = 0.3
EPS = 1e-06
PART = 24
HALF_PARTS = (32, 16, 24)
VMEM_LIMIT = 8 * 1024 * 1024

SMEM_SPEC = pl.BlockSpec(memory_space=pltpu.SMEM)
VMEM_SPEC = pl.BlockSpec(memory_space=pltpu.VMEM)
FAR_SPEC = pl.BlockSpec(memory_space=pltpu.HBM)


def top(shape):
    return lax.broadcasted_iota(jnp.int32, shape, 0) < shape[0] // 2


def turn_rows(value):
    return pltpu.roll(value, value.shape[0] // 2, 0)


def upper_half(a, b):
    return jnp.where(top(a.shape), a, turn_rows(b))


def lower_half(a, b):
    return jnp.where(top(a.shape), turn_rows(a), b)


def mine_first(value, odd):
    return jnp.where(odd, turn_rows(value), value)


def split_rows(value):
    high = value.astype(jnp.bfloat16)
    low = (value - high.astype(jnp.float32)).astype(jnp.bfloat16)
    return jnp.concatenate([high, low], axis=0)


def add_up(terms):
    while len(terms) > 1:
        terms = [terms[i] + terms[i + 1] for i in range(0, len(terms), 2)]
    return terms[0]


def over_parts(tiles, live, part, sizes=(PART,)):
    total, first, n = tiles.shape[0], 0, 0
    while first < total:
        size = min(sizes[min(n, len(sizes) - 1)], total - first)
        pl.when(first < live)(functools.partial(part, first, size))
        first, n = first + size, n + 1


def first_products(count, rows, cols, tiles, source, acc, ready):
    spare, scen = acc.shape[0] - 1, acc.shape[1]
    live = count[0]
    acc[...] = jnp.zeros_like(acc)

    def part(first, size):
        ready(first)
        landing, results = [], []
        for g in range(first, first + size):
            landing.append(jnp.where(g < live, cols[g], spare))
        pair = 2 if size % 2 == 0 else 1
        for g in range(first, first + size, pair):
            picked = [source[rows[g + k]] for k in range(pair)]
            if pair == 2:
                blank = jnp.zeros_like(picked[0])
                left = jnp.concatenate(
                    [
                        jnp.concatenate([picked[0], blank], axis=1),
                        jnp.concatenate([blank, picked[1]], axis=1),
                    ],
                    axis=0,
                )
                right = jnp.concatenate([tiles[g], tiles[g + 1]], axis=0)
            else:
                left, right = picked[0], tiles[g]
            product = jnp.dot(left, right, preferred_element_type=jnp.float32)
            for k in range(pair):
                own = product[2 * scen * k : 2 * scen * (k + 1)]
                results.append(own[:scen] + own[scen:])
        for where, value in zip(landing, results):
            acc[where] += value

    over_parts(tiles, live, part)


def half_products(live, reads, lands, tiles, depth, source, acc):
    spare = acc.shape[0] - 1
    dims = (((1,), (depth,)), ((), ()))

    def part(first, size):
        landing, results = [], []
        for g in range(first, first + size):
            landing.append(jnp.where(g < live, lands(g), spare))
        pair = 2 if size % 2 == 0 else 1
        for g in range(first, first + size, pair):
            left = jnp.concatenate([source[k, reads(g + k)] for k in range(pair)], axis=1)
            right = jnp.concatenate([tiles[g + k] for k in range(pair)], axis=depth)
            product = lax.dot_general(left, right, dims, preferred_element_type=jnp.float32)
            rows = product.shape[0] // 2
            results += [product[rows * k : rows * (k + 1)] for k in range(pair)]
        for where, value in zip(landing, results):
            acc[where] += value

    over_parts(tiles, live, part, HALF_PARTS)


def put_source(source, k, quad):
    q, rows = source.shape[1] // 4, quad.shape[0] // 2
    high = quad.astype(jnp.bfloat16).astype(jnp.float32)
    low = quad - high
    for h in range(2):
        a, b = high[rows * h : rows * (h + 1)], low[rows * h : rows * (h + 1)]
        for j, block in ((0, upper_half(a, b)), (1, lower_half(a, b))):
            blank = jnp.zeros_like(block)
            where = k + (2 * h + j) * q
            source[0, where] = jnp.concatenate([block, blank], axis=0).astype(jnp.bfloat16)
            source[1, where] = jnp.concatenate([blank, block], axis=0).astype(jnp.bfloat16)


def pack(acc, out, norm, slot):
    q = (acc.shape[0] - 1) // 4
    for k in range(q):
        sums = [acc[k + j * q] for j in range(4)]
        sums = [value + turn_rows(value) for value in sums]
        halves = [jnp.where(top(sums[0].shape), sums[2 * h], sums[2 * h + 1]) for h in range(2)]
        out[k] = jnp.concatenate(halves, axis=0).astype(jnp.bfloat16)
    lanes = lax.broadcasted_iota(jnp.int32, acc.shape[1:], 1)
    out[q] = split_rows(jnp.where(lanes == slot, norm, 0.0))


def total_norm(parts):
    both = add_up([p[p.shape[0] - 1].astype(jnp.float32) for p in parts])
    rows = both.shape[0] // 2
    return jnp.sum(both[:rows] + both[rows:], axis=1, keepdims=True)


def partial_norm(squares):
    rows = squares.shape[0] // 2
    both = squares[:rows] + squares[rows:]
    return jnp.sum(both + turn_rows(both), axis=1, keepdims=True)


def quad_of_rows(array, k):
    q = array.shape[0] // 4
    rows = [array[k + j * q : k + j * q + 1, :] for j in range(4)]
    shape = (8, array.shape[1])
    return jnp.concatenate([jnp.where(top(shape), rows[2 * h], rows[2 * h + 1]) for h in range(2)], axis=0)


def pair_of_blocks(array, k, gap, odd):
    tile = 128
    a, b = (mine_first(array[:, n * tile : (n + 1) * tile], odd) for n in (k, k + gap))
    return upper_half(a, b), lower_half(a, b)


def is_odd():
    return lax.rem(lax.axis_index("rowblk"), 2) == 1


def first_kernel(*refs):
    count, rows_far, cols_far, tiles_far, dual_far, keep, send, tiles, rows, cols, source, acc, dual, sems = refs
    tile = tiles.shape[1]
    get_dual = pltpu.make_async_copy(dual_far, dual, sems.at[2])
    get_dual.start()
    copies = [
        pltpu.make_async_copy(rows_far, rows, sems.at[0]),
        pltpu.make_async_copy(cols_far, cols, sems.at[1]),
    ]
    for copy in copies:
        copy.start()
    get_tiles = {}
    for n, first in enumerate(range(0, tiles.shape[0], PART)):
        span = pl.ds(first, min(PART, tiles.shape[0] - first))
        get_tiles[first] = pltpu.make_async_copy(tiles_far.at[span], tiles.at[span], sems.at[3 + n])
        pl.when(first < count[0])(get_tiles[first].start)
    get_dual.wait()
    for b in range(source.shape[0]):
        source[b] = split_rows(dual[:, b * tile : (b + 1) * tile])
    for copy in copies:
        copy.wait()
    first_products(count, rows, cols, tiles, source, acc, lambda first: get_tiles[first].wait())
    odd = is_odd()
    q = keep.shape[0]
    for k in range(q):
        halves = []
        for h in range(2):
            a, b = (mine_first(acc[k + (2 * h + j) * q], odd) for j in range(2))
            halves.append((upper_half(a, b), lower_half(a, b)))
        keep[k] = jnp.concatenate([halves[0][0], halves[1][0]], axis=0)
        send[k] = jnp.concatenate([halves[0][1], halves[1][1]], axis=0).astype(jnp.bfloat16)


def turn_tiles(live, tiles, turned):
    def part(first, size):
        for g in range(first, first + size):
            turned[g] = tiles[g].T

    over_parts(tiles, live, part)


def turn_kernel(count, rows, cols, tiles, dual, demand, flag, after, turned, extra):
    del after
    total, half = rows.shape[1], flag.shape[0] // 2
    odd = is_odd()
    for k in range(half):
        extra[k] = pair_of_blocks(dual, k, half, odd)[1]
        extra[half + k] = pair_of_blocks(demand, k, half, odd)[1]
    for n in range(flag.shape[0] // 8):
        extra[2 * half + n] = flag[8 * n : 8 * (n + 1), :].astype(jnp.float32)
    last = extra.shape[0] - 1
    extra[last] = jnp.zeros(extra.shape[1:], jnp.float32)
    extra[last, 0:1, 0:total] = rows[...].astype(jnp.float32)
    extra[last, 1:2, 0:total] = cols[...].astype(jnp.float32)
    extra[last, 2:3, :] = jnp.full((1, extra.shape[2]), count[0], jnp.int32).astype(jnp.float32)
    turn_tiles(count[0], tiles, turned)


def col_kernel(begin, cost, upper, flag, after, start, price, limit):
    del after
    odd = is_odd()
    q = start.shape[0]
    for k in range(q):
        start[k] = jnp.concatenate([pair_of_blocks(begin, k + 2 * h * q, q, odd)[0] for h in range(2)], axis=0)
        price[k] = quad_of_rows(cost, k)
        limit[k] = jnp.where(quad_of_rows(flag, k) > 0, quad_of_rows(upper, k), jnp.inf)


def row_kernel(extra, demand, flag, begin, after, start, right, floor):
    del after
    odd = is_odd()
    half, tile = start.shape[0], start.shape[2]
    for k in range(half):
        start[k] = jnp.concatenate([pair_of_blocks(begin, k, half, odd)[0], extra[k]], axis=0)
        right[k] = jnp.concatenate([pair_of_blocks(demand, k, half, odd)[0], extra[half + k]], axis=0)
        own = [flag[n : n + 1, :].astype(jnp.float32) for n in (k, k + half)]
        far = [extra[2 * half + n // 8, n % 8 : n % 8 + 1, :] for n in (k, k + half)]
        marks = [jnp.where(top((8, tile)), a, b) for a, b in (own, far)]
        floor[k] = jnp.where(jnp.concatenate(marks, axis=0) > 0.0, 0.0, -jnp.inf)


def turn_other_kernel(grid, tiles, after, turned):
    del after
    turn_tiles(grid[2, 0], tiles, turned)


def primal_kernel(mix, last, n_parts, *refs):
    count, rows, cols, tiles, other = refs[:5]
    parts = refs[5 : 5 + n_parts]
    price, limit, start, *refs = refs[5 + n_parts :]
    if last:
        grid, weight_in, primal_norm, point, point_out, weight_out, out, source, acc = refs
        dual_norm = total_norm(parts)
        weight = weight_in[:, :1]
        ratio = (dual_norm + EPS) / (primal_norm[:, :1] + EPS)
        weight = jnp.sqrt(weight * jnp.sqrt(ratio))
        weight_out[...] = jnp.broadcast_to(weight, weight_out.shape)
    else:
        extra, point_out, out, grid, source, acc, whole, sem = refs
        point = start
        whole[...] = extra[extra.shape[0] - 1].astype(jnp.int32)
        get_grid = pltpu.make_async_copy(whole, grid, sem)
        get_grid.start()
        weight = jnp.ones((8, 1), jnp.float32)
    q = point_out.shape[0]
    tile = point_out.shape[2]
    tau = jnp.broadcast_to(ETA / weight, (weight.shape[0], tile))
    tau = jnp.concatenate([tau, tau], axis=0)
    squares = jnp.zeros_like(tau)
    for k in range(q):
        value = add_up([p[k].astype(jnp.float32) for p in parts])
        old = point[k]
        moved = old - tau * (price[k] - value)
        x_hat = jnp.maximum(jnp.minimum(moved, limit[k]), 0.0)
        step = x_hat - old
        squares += step * step
        x_bar = 2.0 * x_hat - old
        point_out[k] = mix * x_bar + (1.0 - mix) * start[k]
        put_source(source, k, x_bar)
    acc[...] = jnp.zeros_like(acc)
    near = (acc.shape[0] - 1) // 2
    half_products(count[0], lambda g: cols[g], lambda g: rows[g], tiles, 0, source, acc)
    if not last:
        get_grid.wait()
    half_products(grid[2, 0], lambda g: grid[1, g], lambda g: near + grid[0, g], other, 0 if last else 1, source, acc)
    pack(acc, out, partial_norm(squares), lax.axis_index("colblk"))


def dual_kernel(mix, last, n_parts, *refs):
    if last:
        parts = refs[:n_parts]
        refs = refs[n_parts:]
        weight, start, right, floor, dual, keep, send, small = refs
    else:
        count, rows, cols, grid, tiles, other = refs[:6]
        parts = refs[6 : 6 + n_parts]
        refs = refs[6 + n_parts :]
        weight, start, right, floor, dual_out, primal_norm, out, source, acc = refs
        dual = start
    if n_parts == 4:
        parts = [parts[0], parts[2], parts[1], parts[3]]
    primal_total = total_norm(parts)
    sigma = jnp.concatenate([ETA * weight[...]] * 2, axis=0)
    squares = jnp.zeros_like(sigma)
    for k in range(start.shape[0]):
        value = add_up([p[k].astype(jnp.float32) for p in parts])
        old = dual[k]
        moved = old + sigma * (right[k] - value)
        y_hat = jnp.maximum(moved, floor[k])
        step = y_hat - old
        squares += step * step
        new = mix * (2.0 * y_hat - old) + (1.0 - mix) * start[k]
        if last:
            keep[k] = new[:8]
            send[k] = new[8:]
        else:
            dual_out[k] = new
            put_source(source, k, new)
    dual_norm = partial_norm(squares)
    if last:
        lanes = lax.broadcasted_iota(jnp.int32, small.shape, 1)
        first = jnp.where(is_odd(), 3, 0)
        values = jnp.where(lanes == first, dual_norm, 0.0)
        values = jnp.where(lanes == first + 1, primal_total, values)
        small[...] = jnp.where(lanes == first + 2, weight[...], values)
    else:
        primal_norm[...] = jnp.broadcast_to(primal_total, primal_norm.shape)
        acc[...] = jnp.zeros_like(acc)
        near = source.shape[1] // 2
        half_products(count[0], lambda g: rows[g], lambda g: cols[g], tiles, 0, source, acc)
        half_products(grid[2, 0], lambda g: near + grid[0, g], lambda g: grid[1, g], other, 0, source, acc)
        pack(acc, out, dual_norm, lax.axis_index("rowblk"))


def join(mine, others, out):
    tile = mine.shape[2]
    odd = is_odd()
    q, pairs = mine.shape[0], mine.shape[1] // 8
    for k in range(q):
        for h in range(pairs):
            a, b = mine[k, 8 * h : 8 * (h + 1), :], others[k, 8 * h : 8 * (h + 1), :]
            a, b = jnp.where(odd, b, a), jnp.where(odd, a, b)
            for j, value in ((0, upper_half(a, b)), (1, lower_half(a, b))):
                n = k + (2 * h + j) * q
                out[:, n * tile : (n + 1) * tile] = value


def end_kernel(share, *refs):
    mine_x, other_x, mine_y, other_y, *parts = refs[:-7]
    far_x, far_y, far_weight, x_out, y_out, weight_out, sems = refs[-7:]
    copies = []
    for n, (mine, others, out, target) in enumerate(((mine_x, other_x, x_out, far_x), (mine_y, other_y, y_out, far_y))):
        join(mine, others, out)
        copies.append(pltpu.make_async_copy(out, target, sems.at[n]))
        copies[-1].start()
    both = add_up([p[...] for p in parts])
    found = []
    for first in (0, 3):
        dual_norm, primal_norm, weight = (both[:, first + n : first + n + 1] for n in range(3))
        ratio = (dual_norm + EPS) / (primal_norm * share + EPS)
        found.append(jnp.sqrt(weight * share * jnp.sqrt(ratio)))
    weight = jnp.where(top(found[0].shape), found[0], found[1])
    lanes, rows = (lax.broadcasted_iota(jnp.int32, both.shape, n) for n in (1, 0))
    row = jnp.sum(jnp.where(lanes == rows, weight, 0.0), axis=0, keepdims=True)
    weight_out[...] = row[:, : weight_out.shape[1]]
    copies.append(pltpu.make_async_copy(weight_out, far_weight, sems.at[2]))
    copies[-1].start()
    for copy in copies:
        copy.wait()


def call(kernel, inputs, in_specs, outputs, out_specs, scratch, cost=None):
    return pl.pallas_call(
        kernel,
        out_shape=outputs,
        in_specs=in_specs,
        out_specs=out_specs,
        scratch_shapes=scratch,
        cost_estimate=cost,
        compiler_params=pltpu.CompilerParams(vmem_limit_bytes=VMEM_LIMIT),
    )(*inputs)


def far(value):
    return pltpu.with_memory_space_constraint(value, pltpu.HBM)


def swap(value, axis, mask):
    size = lax.axis_size(axis)
    return lax.ppermute(value, axis, [(i, i ^ mask) for i in range(size)])


def butterfly(value, axis, radix, mask=1):
    size = lax.axis_size(axis)
    parts = [value]
    while mask < size:
        total = add_up([p.astype(jnp.float32) for p in parts]).astype(value.dtype)
        span = min(radix, size // mask)
        parts = [total] + [swap(total, axis, mask * k) for k in range(1, span)]
        mask *= span
    return parts


def on_device(
    tiles,
    tile_row,
    tile_col,
    tile_count,
    cost,
    demand,
    upper,
    col_flag,
    row_flag,
    primal_start,
    dual_start,
):
    tile = tiles.shape[1]
    total = tile_row.shape[0]
    scen = primal_start.shape[0]
    col_blocks = primal_start.shape[1] // tile
    row_blocks = dual_start.shape[1] // tile
    bf16, f32, i32 = jnp.bfloat16, jnp.float32, jnp.int32
    cost, upper, col_flag = (v.reshape(col_blocks, tile) for v in (cost, upper, col_flag))
    row_flag = row_flag.reshape(row_blocks, tile)

    small = pltpu.VMEM((scen, tile), f32)
    col_quads, row_quads = col_blocks // 4, row_blocks // 2
    col_state = pltpu.VMEM((col_quads, 2 * scen, tile), f32)
    row_state = pltpu.VMEM((row_quads, 2 * scen, tile), f32)
    row_half = pltpu.VMEM((row_quads, scen, tile), f32)
    col_terms = pltpu.VMEM((col_quads + 1, 2 * scen, tile), bf16)
    row_terms = pltpu.VMEM((row_quads + 1, 2 * scen, tile), bf16)
    tiles_like = pltpu.VMEM(tiles.shape, tiles.dtype)
    index = pltpu.SMEM((total,), i32)
    to_cols = [
        pltpu.VMEM((2, 2 * row_blocks, 2 * scen, tile), bf16),
        pltpu.VMEM((col_blocks + 1, scen, tile), f32),
    ]
    to_rows = [
        pltpu.VMEM((2, col_blocks, 2 * scen, tile), bf16),
        pltpu.VMEM((2 * row_blocks + 1, scen, tile), f32),
    ]
    turning = pl.CostEstimate(flops=0, bytes_accessed=2 * tiles.size * 2, transcendentals=0)

    keep, send, tiles, rows, cols = call(
        first_kernel,
        [tile_count, far(tile_row), far(tile_col), far(tiles), far(dual_start)],
        [SMEM_SPEC] + [FAR_SPEC] * 4,
        [col_state, pltpu.VMEM((col_quads, 2 * scen, tile), bf16), tiles_like, index, index],
        [VMEM_SPEC] * 3 + [SMEM_SPEC] * 2,
        [
            pltpu.VMEM((row_blocks, 2 * scen, tile), bf16),
            pltpu.VMEM((col_blocks + 1, scen, tile), f32),
            pltpu.VMEM(dual_start.shape, f32),
            pltpu.SemaphoreType.DMA((3 + pl.cdiv(total, PART),)),
        ],
    )
    terms = (keep + swap(send, "rowblk", 1).astype(f32)).astype(bf16)
    held_tiles, terms = lax.optimization_barrier((tiles, terms))
    parts = butterfly(terms, "rowblk", 2, 2)
    other = swap(held_tiles, "rowblk", 1)
    turned, extra = call(
        turn_kernel,
        [tile_count, tile_row.reshape(1, total), tile_col.reshape(1, total), tiles, dual_start, demand, row_flag, terms],
        [SMEM_SPEC] + [VMEM_SPEC] * 7,
        [tiles_like, pltpu.VMEM((2 * row_quads + row_blocks // 8 + 1, scen, tile), f32)],
        [VMEM_SPEC] * 2,
        [],
        turning,
    )
    extra = swap(extra, "rowblk", 1)
    columns = call(
        col_kernel,
        [primal_start, cost, upper, col_flag, terms],
        [VMEM_SPEC] * 5,
        [col_state] * 3,
        [VMEM_SPEC] * 3,
        [],
    )
    start, price, limit = columns
    own = [tile_count, rows, cols]
    weight = jnp.ones((scen, tile), f32)
    for step in range(ITERS):
        mix = (step + 1.0) / (step + 2.0)
        last = step == ITERS - 1
        if step:
            parts = butterfly(terms, "rowblk", 2, 2)
            (other_turned,) = call(
                turn_other_kernel,
                [grid, other, terms],
                [SMEM_SPEC] + [VMEM_SPEC] * 2,
                [tiles_like],
                [VMEM_SPEC],
                [],
                turning,
            )
            vectors = [*parts, price, limit, start]
            point, weight, terms = call(
                functools.partial(primal_kernel, mix, True, len(parts)),
                [*own, turned, other_turned, *vectors, grid, weight, primal_norm, point],
                [SMEM_SPEC] * 3 + [VMEM_SPEC] * (2 + len(vectors)) + [SMEM_SPEC] + [VMEM_SPEC] * 3,
                [col_state, small, row_terms],
                [VMEM_SPEC] * 3,
                to_rows,
            )
        else:
            vectors = [*parts, price, limit, start, extra]
            point, terms, grid = call(
                functools.partial(primal_kernel, mix, False, len(parts)),
                [*own, turned, other, *vectors],
                [SMEM_SPEC] * 3 + [VMEM_SPEC] * (2 + len(vectors)),
                [col_state, row_terms, pltpu.SMEM((scen, tile), i32)],
                [VMEM_SPEC] * 2 + [SMEM_SPEC],
                [*to_rows, pltpu.VMEM((scen, tile), i32), pltpu.SemaphoreType.DMA],
            )
        parts = butterfly(terms, "colblk", 4)
        if len(parts) == 4:
            parts = [parts[n] for n in (0, 2, 1, 3)]
        if step == 0:
            lines = call(
                row_kernel,
                [extra, demand, row_flag, dual_start, terms],
                [VMEM_SPEC] * 5,
                [row_state] * 3,
                [VMEM_SPEC] * 3,
                [],
            )
        vectors = [*parts, weight, *lines]
        if last:
            keep, send, terms = call(
                functools.partial(dual_kernel, mix, True, len(parts)),
                [*vectors, dual],
                [VMEM_SPEC] * (1 + len(vectors)),
                [row_half, row_half, small],
                [VMEM_SPEC] * 3,
                [],
            )
        else:
            dual, primal_norm, terms = call(
                functools.partial(dual_kernel, mix, False, len(parts)),
                [*own, grid, tiles, other, *vectors],
                [SMEM_SPEC] * 4 + [VMEM_SPEC] * (2 + len(vectors)),
                [row_state, small, col_terms],
                [VMEM_SPEC] * 3,
                to_cols,
            )
    point, terms = lax.optimization_barrier((point, terms))
    parts = butterfly(terms, "rowblk", 4)
    halves = [point, swap(point, "rowblk", 1), keep, swap(send, "rowblk", 1)]
    shapes = [primal_start.shape, dual_start.shape, (1, scen)]
    point, dual, weight = call(
        functools.partial(end_kernel, 2.0 / lax.axis_size("rowblk")),
        [*halves, *parts],
        [VMEM_SPEC] * (4 + len(parts)),
        [jax.ShapeDtypeStruct(shape, f32) for shape in shapes],
        [FAR_SPEC] * 3,
        [pltpu.VMEM(shape, f32) for shape in shapes] + [pltpu.SemaphoreType.DMA((3,))],
    )
    return point, dual, weight.reshape(scen)


def solution(mesh):
    return jax.shard_map(
        on_device,
        mesh=mesh,
        in_specs=(
            P(("groups", "rowblk", "colblk"), None, None),
            P(("groups", "rowblk", "colblk")),
            P(("groups", "rowblk", "colblk")),
            P(("groups", "rowblk", "colblk")),
            P(("groups", "colblk")),
            P(None, ("groups", "rowblk")),
            P(("groups", "colblk")),
            P(("groups", "colblk")),
            P(("groups", "rowblk")),
            P(None, ("groups", "colblk")),
            P(None, ("groups", "rowblk")),
        ),
        out_specs=(P(None, ("groups", "colblk")), P(None, ("groups", "rowblk")), P("groups")),
        check_vma=False,
    )
```

time: 45.1 us -> 45.2 us (level)
  Pallas kernels: 4.06 us -> 8.3 us
  waiting for transfers between devices: 20 us -> 16.4 us
  starting transfers between devices: 17.5 us -> 19.5 us
  local copies, waits for them, and re-layouts: 1.51 us -> 0.04 us
  other arithmetic: 0.85 us -> 0.02 us
    pallas_call x6 -> x10, Pallas kernels: 4.06 us -> 8.3 us  [call(): pl.pallas_call(kernel, out_shape=outputs, in_specs=in_specs, out_specs=ou...]
    ppermute x13 -> x16, waiting for transfers between devices: 20 us -> 16.4 us  [swap(): return lax.ppermute(value, axis, [(i, i ^ mask) for i in range(size)])]
    ppermute x13 -> x16, starting transfers between devices: 17.5 us -> 19.5 us  [swap(): return lax.ppermute(value, axis, [(i, i ^ mask) for i in range(size)])]
    unnamed x16 -> x18, local copies, waits for them, and re-layouts: 1.39 us -> 0.04 us
    sqrt x1 -> x0, other arithmetic: 0.54 us -> none  [on_device(): weight = jnp.sqrt(weight[:, 0] * jnp.sqrt(ratio))]
  transfers between devices with their start and end apart: 13 -> 16, of which waited for: 12 -> 9; matrix products, arithmetic and copies ran while one was open for 4% -> 0% of each run, Pallas kernels for 1% -> 3%
where the time goes in v6:
time: 45.2 us; the launch traced here: 45.8 us
  starting transfers between devices  19.5 us (43%)
  waiting for transfers between devices  16.4 us (36%)
  Pallas kernels  8.3 us (18%)
  between operations  1.53 us (3%)
    ppermute x16, starting transfers between devices, swap(): return lax.ppermute(value, axis, [(i, i ^ mask) for i in range(size)])  19.5 us
    ppermute x16, waiting for transfers between devices, swap(): return lax.ppermute(value, axis, [(i, i ^ mask) for i in range(size)])  16.4 us
    pallas_call x10, Pallas kernels, call(): pl.pallas_call(kernel, out_shape=outputs, in_specs=in_specs, out_specs=ou...  8.3 us
  transfers between devices with their start and end apart: 16, of which 9 were waited for; matrix products, arithmetic and copies ran while one was open for 0% of the time, Pallas kernels for 3%

profile of v6, /device:TPU:0, one launch (start us, length us, event | category | flops | bytes accessed | tf_op | source)
XLA Modules:
  0.0 45.8 jit_solution(14586890981757295921)
XLA Ops:
  0.6 0.0 copy-start
  0.6 0.0 copy-start.8
  0.7 0.0 copy-start.7
  0.7 0.0 copy-start.1
  1.5 1.9 %shard_map.130 = (f32[16,16,128]{2,1,0:T(8,128)S(1)}, bf16[16,16,128]{2,1,0:T(8,128)(2,1)S(1)}, bf16[96,128,128]{2,1,0:T(8,128)(2,1)S(1)}, s32[96]{0:T(128)S(4)}, s32[96]{0:T(128)S(4)}) custom-call(s32[1]{0:T(128)S(6)} %copy.14.refs_0_.count, s32[96]{0:T(128)} %refs_1_.1, s32[96]{0:T(128)} %refs_2_.1, bf16[96,128,128]{2,1,0:T(8,128)(2,1)} %refs_3_.1, ...), custom_call_target="tpu_custom_call" | custom-call | tf_op jit(solution)/shard_map/pallas_call | solution.py:383
  3.4 0.5 %collective-permute-start = (bf16[16,16,128]{2,1,0:T(8,128)(2,1)S(1)}, bf16[16,16,128]{2,1,0:T(8,128)(2,1)S(1)}, u32[]{:S(2)}, u32[]{:S(2)}) collective-permute-start(bf16[16,16,128]{2,1,0:T(8,128)(2,1)S(1)} %get-tuple-element.39), channel_id=1, source_target_pairs={{0,4},{4,0},{8,12},{12,8},{1,5},{5,1},{9,13},{13,9},{2,6},{6,2},{1... | collective-permute-start | bytes 196616 | tf_op jit(solution)/shard_map/ppermute | solution.py:400
  3.9 0.9 %collective-permute-done = bf16[16,16,128]{2,1,0:T(8,128)(2,1)S(1)} collective-permute-done((bf16[16,16,128]{2,1,0:T(8,128)(2,1)S(1)}, bf16[16,16,128]{2,1,0:T(8,128)(2,1)S(1)}, u32[]{:S(2)}, u32[]{:S(2)}) %collective-permute-start) | collective-permute-done | bytes 65568 | tf_op jit(solution)/shard_map/ppermute | solution.py:400
  4.8 0.4 collective-permute-start.1
  5.2 0.0 copy-done
  5.2 0.0 copy-done.3
  5.2 0.6 %shard_map.131 = (bf16[96,128,128]{2,1,0:T(8,128)(2,1)S(1)}, f32[37,8,128]{2,1,0:T(8,128)S(1)}) custom-call(s32[1]{0:T(128)S(6)} %copy.14.refs_0_.count, s32[1,96]{1,0:T(1,128)S(1)} %bitcast.12, s32[1,96]{1,0:T(1,128)S(1)} %bitcast.13, bf16[96,128,128]{2,1,0:T(8,128)(2,1)S(1)} %get-tuple-element.42.tiles.refs_4_, f32[8,4096]{1,0:T(8,128)S(1)} %copy-done, ...), custom_call_target="tpu_custom_call" | custom-call | bytes 6291456 | tf_op jit(solution)/shard_map/pallas_call | solution.py:383
  5.8 0.2 collective-permute-start.3
  6.0 3.6 %collective-permute-start.2 = (bf16[16,16,128]{2,1,0:T(8,128)(2,1)S(1)}, bf16[16,16,128]{2,1,0:T(8,128)(2,1)S(1)}, u32[]{:S(2)}, u32[]{:S(2)}) collective-permute-start(bf16[16,16,128]{2,1,0:T(8,128)(2,1)S(1)} %add_convert_fusion.after.refs_5_), channel_id=1, source_target_pairs={{0,8},{4,12},{8,0},{12,4},{1,9},{5,13},{9,1},{13,5},{2,10},{6,14},... | collective-permute-start | bytes 196616 | tf_op jit(solution)/shard_map/ppermute | solution.py:400
  9.6 0.1 shard_map.132
  9.7 2.6 %collective-permute-done.2.refs_6_ = bf16[16,16,128]{2,1,0:T(8,128)(2,1)S(1)} collective-permute-done((bf16[16,16,128]{2,1,0:T(8,128)(2,1)S(1)}, bf16[16,16,128]{2,1,0:T(8,128)(2,1)S(1)}, u32[]{:S(2)}, u32[]{:S(2)}) %collective-permute-start.2) | collective-permute-done | bytes 65568 | tf_op jit(solution)/shard_map/ppermute | solution.py:400
  12.3 0.0 collective-permute-done.3.refs_10_.extra
  12.3 0.0 collective-permute-done.1.refs_4_.refs_5_.tiles
  12.3 1.4 %shard_map.133 = (f32[16,16,128]{2,1,0:T(8,128)S(1)}, bf16[17,16,128]{2,1,0:T(8,128)(2,1)S(1)}, s32[8,128]{1,0:T(8,128)S(4)}) custom-call(s32[1]{0:T(128)S(6)} %copy.14.refs_0_.count, s32[96]{0:T(128)S(4)} %get-tuple-element.35.refs_1_, s32[96]{0:T(128)S(4)} %get-tuple-element.36.refs_2_, bf16[96,128,128]{2,1,0:T(8,128)(2,1)S(1)} %get-tuple-element.41.refs_3_, ...), custom_call_target="tpu_custom_call" | custom-call | tf_op jit(solution)/shard_map/pallas_call | solution.py:383
  13.7 3.2 %collective-permute-start.6 = (bf16[17,16,128]{2,1,0:T(8,128)(2,1)S(1)}, bf16[17,16,128]{2,1,0:T(8,128)(2,1)S(1)}, u32[]{:S(2)}, u32[]{:S(2)}) collective-permute-start(bf16[17,16,128]{2,1,0:T(8,128)(2,1)S(1)} %get-tuple-element.48.after.refs_6_), channel_id=1, source_target_pairs={{0,3},{1,2},{2,1},{3,0},{4,7},{5,6},{6,5},{7,4},{8,11},{9,10},{10,... | collective-permute-start | bytes 208904 | tf_op jit(solution)/shard_map/ppermute | solution.py:400
  16.9 0.0 collective-permute-start.5
  16.9 1.2 %collective-permute-start.4 = (bf16[17,16,128]{2,1,0:T(8,128)(2,1)S(1)}, bf16[17,16,128]{2,1,0:T(8,128)(2,1)S(1)}, u32[]{:S(2)}, u32[]{:S(2)}) collective-permute-start(bf16[17,16,128]{2,1,0:T(8,128)(2,1)S(1)} %get-tuple-element.48.after.refs_6_), channel_id=1, source_target_pairs={{0,2},{1,3},{2,0},{3,1},{4,6},{5,7},{6,4},{7,5},{8,10},{9,11},{10,... | collective-permute-start | bytes 208904 | tf_op jit(solution)/shard_map/ppermute | solution.py:400
  18.2 0.1 shard_map.134
  18.2 2.1 %collective-permute-done.6.refs_9_ = bf16[17,16,128]{2,1,0:T(8,128)(2,1)S(1)} collective-permute-done((bf16[17,16,128]{2,1,0:T(8,128)(2,1)S(1)}, bf16[17,16,128]{2,1,0:T(8,128)(2,1)S(1)}, u32[]{:S(2)}, u32[]{:S(2)}) %collective-permute-start.6) | collective-permute-done | bytes 69664 | tf_op jit(solution)/shard_map/ppermute | solution.py:400
  20.3 2.6 %collective-permute-done.5.refs_8_ = bf16[17,16,128]{2,1,0:T(8,128)(2,1)S(1)} collective-permute-done((bf16[17,16,128]{2,1,0:T(8,128)(2,1)S(1)}, bf16[17,16,128]{2,1,0:T(8,128)(2,1)S(1)}, u32[]{:S(2)}, u32[]{:S(2)}) %collective-permute-start.5) | collective-permute-done | bytes 69664 | tf_op jit(solution)/shard_map/ppermute | solution.py:400
  23.0 0.0 collective-permute-done.4.refs_7_
  23.0 1.2 %shard_map.135 = (f32[16,16,128]{2,1,0:T(8,128)S(1)}, f32[8,128]{1,0:T(8,128)S(1)}, bf16[17,16,128]{2,1,0:T(8,128)(2,1)S(1)}) custom-call(s32[1]{0:T(128)S(6)} %copy.14.refs_0_.count, s32[96]{0:T(128)S(4)} %get-tuple-element.35.refs_1_, s32[96]{0:T(128)S(4)} %get-tuple-element.36.refs_2_, s32[8,128]{1,0:T(8,128)S(4)} %get-tuple-element.47.refs_3_.grid.refs_10_, ...), custom_call_target="tpu_custom_call" | custom-call | tf_op jit(solution)/shard_map/pallas_call | solution.py:383
  24.2 2.9 %collective-permute-start.7 = (bf16[17,16,128]{2,1,0:T(8,128)(2,1)S(1)}, bf16[17,16,128]{2,1,0:T(8,128)(2,1)S(1)}, u32[]{:S(2)}, u32[]{:S(2)}) collective-permute-start(bf16[17,16,128]{2,1,0:T(8,128)(2,1)S(1)} %get-tuple-element.52.after.refs_5_), channel_id=1, source_target_pairs={{0,8},{4,12},{8,0},{12,4},{1,9},{5,13},{9,1},{13,5},{2,10},{6,14},... | collective-permute-start | bytes 208904 | tf_op jit(solution)/shard_map/ppermute | solution.py:400
  27.1 0.5 %shard_map.136.refs_4_ = bf16[96,128,128]{2,1,0:T(8,128)(2,1)S(1)} custom-call(s32[8,128]{1,0:T(8,128)S(4)} %get-tuple-element.47.refs_3_.grid.refs_10_, bf16[96,128,128]{2,1,0:T(8,128)(2,1)S(1)} %collective-permute-done.1.refs_4_.refs_5_.tiles, bf16[17,16,128]{2,1,0:T(8,128)(2,1)S(1)} %get-tuple-element.52.after.refs_5_), custom_call_target="tpu_custom_call" | custom-call | bytes 6291456 | tf_op jit(solution)/shard_map/pallas_call | solution.py:383
  27.6 1.8 %collective-permute-done.7.refs_6_ = bf16[17,16,128]{2,1,0:T(8,128)(2,1)S(1)} collective-permute-done((bf16[17,16,128]{2,1,0:T(8,128)(2,1)S(1)}, bf16[17,16,128]{2,1,0:T(8,128)(2,1)S(1)}, u32[]{:S(2)}, u32[]{:S(2)}) %collective-permute-start.7) | collective-permute-done | bytes 69664 | tf_op jit(solution)/shard_map/ppermute | solution.py:400
  29.4 1.4 %shard_map.137 = (f32[16,16,128]{2,1,0:T(8,128)S(1)}, f32[8,128]{1,0:T(8,128)S(1)}, bf16[17,16,128]{2,1,0:T(8,128)(2,1)S(1)}) custom-call(s32[1]{0:T(128)S(6)} %copy.14.refs_0_.count, s32[96]{0:T(128)S(4)} %get-tuple-element.35.refs_1_, s32[96]{0:T(128)S(4)} %get-tuple-element.36.refs_2_, bf16[96,128,128]{2,1,0:T(8,128)(2,1)S(1)} %get-tuple-element.41.refs_3_, ...), custom_call_target="tpu_custom_call" | custom-call | tf_op jit(solution)/shard_map/pallas_call | solution.py:383
  30.8 1.5 %collective-permute-start.10 = (bf16[17,16,128]{2,1,0:T(8,128)(2,1)S(1)}, bf16[17,16,128]{2,1,0:T(8,128)(2,1)S(1)}, u32[]{:S(2)}, u32[]{:S(2)}) collective-permute-start(bf16[17,16,128]{2,1,0:T(8,128)(2,1)S(1)} %get-tuple-element.56.refs_0_), channel_id=1, source_target_pairs={{0,3},{1,2},{2,1},{3,0},{4,7},{5,6},{6,5},{7,4},{8,11},{9,10},{10,... | collective-permute-start | bytes 208904 | tf_op jit(solution)/shard_map/ppermute | solution.py:400
  32.3 0.0 collective-permute-start.9
  32.3 2.9 %collective-permute-start.8 = (bf16[17,16,128]{2,1,0:T(8,128)(2,1)S(1)}, bf16[17,16,128]{2,1,0:T(8,128)(2,1)S(1)}, u32[]{:S(2)}, u32[]{:S(2)}) collective-permute-start(bf16[17,16,128]{2,1,0:T(8,128)(2,1)S(1)} %get-tuple-element.56.refs_0_), channel_id=1, source_target_pairs={{0,2},{1,3},{2,0},{3,1},{4,6},{5,7},{6,4},{7,5},{8,10},{9,11},{10,... | collective-permute-start | bytes 208904 | tf_op jit(solution)/shard_map/ppermute | solution.py:400
  35.2 2.0 %collective-permute-done.10.refs_3_ = bf16[17,16,128]{2,1,0:T(8,128)(2,1)S(1)} collective-permute-done((bf16[17,16,128]{2,1,0:T(8,128)(2,1)S(1)}, bf16[17,16,128]{2,1,0:T(8,128)(2,1)S(1)}, u32[]{:S(2)}, u32[]{:S(2)}) %collective-permute-start.10) | collective-permute-done | bytes 69664 | tf_op jit(solution)/shard_map/ppermute | solution.py:400
  37.2 1.2 %collective-permute-done.9.refs_2_ = bf16[17,16,128]{2,1,0:T(8,128)(2,1)S(1)} collective-permute-done((bf16[17,16,128]{2,1,0:T(8,128)(2,1)S(1)}, bf16[17,16,128]{2,1,0:T(8,128)(2,1)S(1)}, u32[]{:S(2)}, u32[]{:S(2)}) %collective-permute-start.9) | collective-permute-done | bytes 69664 | tf_op jit(solution)/shard_map/ppermute | solution.py:400
  38.4 0.0 collective-permute-done.8.refs_1_
  38.4 0.2 shard_map.138
  38.5 0.0 collective-permute-start.11
  38.6 0.5 %collective-permute-start.12 = (f32[16,8,128]{2,1,0:T(8,128)S(1)}, f32[16,8,128]{2,1,0:T(8,128)S(1)}, u32[]{:S(2)}, u32[]{:S(2)}) collective-permute-start(f32[16,8,128]{2,1,0:T(8,128)S(1)} %get-tuple-element.62), channel_id=1, source_target_pairs={{0,4},{4,0},{8,12},{12,8},{1,5},{5,1},{9,13},{13,9},{2,6},{6,2},{1... | collective-permute-start | bytes 196616 | tf_op jit(solution)/shard_map/ppermute | solution.py:400
  39.1 2.1 %collective-permute-start.15 = (f32[8,128]{1,0:T(8,128)S(1)}, f32[8,128]{1,0:T(8,128)S(1)}, u32[]{:S(2)}, u32[]{:S(2)}) collective-permute-start(f32[8,128]{1,0:T(8,128)S(1)} %get-tuple-element.63.refs_4_), channel_id=1, source_target_pairs={{0,12},{4,8},{8,4},{12,0},{1,13},{5,9},{9,5},{13,1},{2,14},{6,10},... | collective-permute-start | bytes 12296 | tf_op jit(solution)/shard_map/ppermute | solution.py:400
  41.1 0.3 collective-permute-start.14
  41.5 0.1 collective-permute-start.13
  41.6 0.9 %collective-permute-done.15.refs_7_ = f32[8,128]{1,0:T(8,128)S(1)} collective-permute-done((f32[8,128]{1,0:T(8,128)S(1)}, f32[8,128]{1,0:T(8,128)S(1)}, u32[]{:S(2)}, u32[]{:S(2)}) %collective-permute-start.15) | collective-permute-done | bytes 4128 | tf_op jit(solution)/shard_map/ppermute | solution.py:400
  42.5 2.3 %collective-permute-done.14.refs_6_ = f32[8,128]{1,0:T(8,128)S(1)} collective-permute-done((f32[8,128]{1,0:T(8,128)S(1)}, f32[8,128]{1,0:T(8,128)S(1)}, u32[]{:S(2)}, u32[]{:S(2)}) %collective-permute-start.14) | collective-permute-done | bytes 4128 | tf_op jit(solution)/shard_map/ppermute | solution.py:400
  44.7 0.0 collective-permute-done.13.refs_5_
  44.7 0.0 collective-permute-done.12.refs_3_
  44.7 0.0 collective-permute-done.11.refs_1_
  44.7 1.0 %shard_map.139 = (f32[8,8192]{1,0:T(8,128)}, f32[8,4096]{1,0:T(8,128)}, f32[1,8]{1,0:T(1,128)}) custom-call(f32[16,16,128]{2,1,0:T(8,128)S(1)} %get-tuple-element.60.refs_0_, f32[16,16,128]{2,1,0:T(8,128)S(1)} %collective-permute-done.11.refs_1_, f32[16,8,128]{2,1,0:T(8,128)S(1)} %get-tuple-element.61.refs_2_, ...), custom_call_target="tpu_custom_call" | custom-call | tf_op jit(solution)/shard_map/pallas_call | solution.py:383
  (14 shorter events, 0.0 us)
Async XLA Ops:
  0.6 4.6 %copy-start = (f32[8,4096]{1,0:T(8,128)S(1)}, f32[8,4096]{1,0:T(8,128)}, u32[]{:S(2)}) copy-start(f32[8,4096]{1,0:T(8,128)} %begin.3) | copy-start | bytes 393220
  0.6 4.6 %copy-start.8 = (s32[96]{0:T(128)S(1)}, s32[96]{0:T(128)}, u32[]{:S(2)}) copy-start(s32[96]{0:T(128)} %refs_2_.1) | copy-start | bytes 1156
  0.7 4.5 %copy-start.7 = (s32[96]{0:T(128)S(1)}, s32[96]{0:T(128)}, u32[]{:S(2)}) copy-start(s32[96]{0:T(128)} %refs_1_.1) | copy-start | bytes 1156
  0.7 4.5 %copy-start.1 = (f32[8,4096]{1,0:T(8,128)S(1)}, f32[8,4096]{1,0:T(8,128)}, u32[]{:S(2)}) copy-start(f32[8,4096]{1,0:T(8,128)} %demand.3) | copy-start | bytes 393220
  0.7 4.5 %copy-start.3 = (s32[4096]{0:T(1024)S(1)}, s32[4096]{0:T(1024)}, u32[]{:S(2)}) copy-start(s32[4096]{0:T(1024)} %param.19) | copy-start | bytes 49156
  1.4 8.2 %copy-start.2 = (f32[8,8192]{1,0:T(8,128)S(1)}, f32[8,8192]{1,0:T(8,128)}, u32[]{:S(2)}) copy-start(f32[8,8192]{1,0:T(8,128)} %begin.2) | copy-start | bytes 786436
  1.4 8.2 %copy-start.4 = (f32[8192]{0:T(1024)S(1)}, f32[8192]{0:T(1024)}, u32[]{:S(2)}) copy-start(f32[8192]{0:T(1024)} %param.15) | copy-start | bytes 98308
  1.4 8.2 %copy-start.5 = (f32[8192]{0:T(1024)S(1)}, f32[8192]{0:T(1024)}, u32[]{:S(2)}) copy-start(f32[8192]{0:T(1024)} %param.17) | copy-start | bytes 98308
  1.4 8.2 %copy-start.6 = (s32[8192]{0:T(1024)S(1)}, s32[8192]{0:T(1024)}, u32[]{:S(2)}) copy-start(s32[8192]{0:T(1024)} %param.18) | copy-start | bytes 98308
  3.4 1.4 %collective-permute-start = (bf16[16,16,128]{2,1,0:T(8,128)(2,1)S(1)}, bf16[16,16,128]{2,1,0:T(8,128)(2,1)S(1)}, u32[]{:S(2)}, u32[]{:S(2)}) collective-permute-start(bf16[16,16,128]{2,1,0:T(8,128)(2,1)S(1)} %get-tuple-element.39), channel_id=1, source_target_pairs={{0,4},{4,0},{8,12},{12,8},{1,5},{5,1},{9,13},{13,9},{2,6},{6,2},{1... | collective-permute-start | bytes 196616 | tf_op jit(solution)/shard_map/ppermute | solution.py:400
  4.8 7.5 %collective-permute-start.1 = (bf16[96,128,128]{2,1,0:T(8,128)(2,1)S(1)}, bf16[96,128,128]{2,1,0:T(8,128)(2,1)S(1)}, u32[]{:S(2)}, u32[]{:S(2)}) collective-permute-start(bf16[96,128,128]{2,1,0:T(8,128)(2,1)S(1)} %get-tuple-element.42.tiles.refs_4_), channel_id=1, source_target_pairs={{0,4},{4,0},{8,12},{12,8},{1,5},{5,1},{9,13},{13,9},{2,6},{6,2},{1... | collective-permute-start | bytes 9437192 | tf_op jit(solution)/shard_map/ppermute | solution.py:400
  5.8 6.5 %collective-permute-start.3 = (f32[37,8,128]{2,1,0:T(8,128)S(1)}, f32[37,8,128]{2,1,0:T(8,128)S(1)}, u32[]{:S(2)}, u32[]{:S(2)}) collective-permute-start(f32[37,8,128]{2,1,0:T(8,128)S(1)} %get-tuple-element.46), channel_id=1, source_target_pairs={{0,4},{4,0},{8,12},{12,8},{1,5},{5,1},{9,13},{13,9},{2,6},{6,2},{1... | collective-permute-start | bytes 454664 | tf_op jit(solution)/shard_map/ppermute | solution.py:400
  6.0 6.3 %collective-permute-start.2 = (bf16[16,16,128]{2,1,0:T(8,128)(2,1)S(1)}, bf16[16,16,128]{2,1,0:T(8,128)(2,1)S(1)}, u32[]{:S(2)}, u32[]{:S(2)}) collective-permute-start(bf16[16,16,128]{2,1,0:T(8,128)(2,1)S(1)} %add_convert_fusion.after.refs_5_), channel_id=1, source_target_pairs={{0,8},{4,12},{8,0},{12,4},{1,9},{5,13},{9,1},{13,5},{2,10},{6,14},... | collective-permute-start | bytes 196616 | tf_op jit(solution)/shard_map/ppermute | solution.py:400
  13.7 6.6 %collective-permute-start.6 = (bf16[17,16,128]{2,1,0:T(8,128)(2,1)S(1)}, bf16[17,16,128]{2,1,0:T(8,128)(2,1)S(1)}, u32[]{:S(2)}, u32[]{:S(2)}) collective-permute-start(bf16[17,16,128]{2,1,0:T(8,128)(2,1)S(1)} %get-tuple-element.48.after.refs_6_), channel_id=1, source_target_pairs={{0,3},{1,2},{2,1},{3,0},{4,7},{5,6},{6,5},{7,4},{8,11},{9,10},{10,... | collective-permute-start | bytes 208904 | tf_op jit(solution)/shard_map/ppermute | solution.py:400
  16.9 6.1 %collective-permute-start.5 = (bf16[17,16,128]{2,1,0:T(8,128)(2,1)S(1)}, bf16[17,16,128]{2,1,0:T(8,128)(2,1)S(1)}, u32[]{:S(2)}, u32[]{:S(2)}) collective-permute-start(bf16[17,16,128]{2,1,0:T(8,128)(2,1)S(1)} %get-tuple-element.48.after.refs_6_), channel_id=1, source_target_pairs={{0,1},{1,0},{2,3},{3,2},{4,5},{5,4},{6,7},{7,6},{8,9},{9,8},{10,11... | collective-permute-start | bytes 208904 | tf_op jit(solution)/shard_map/ppermute | solution.py:400
  16.9 6.1 %collective-permute-start.4 = (bf16[17,16,128]{2,1,0:T(8,128)(2,1)S(1)}, bf16[17,16,128]{2,1,0:T(8,128)(2,1)S(1)}, u32[]{:S(2)}, u32[]{:S(2)}) collective-permute-start(bf16[17,16,128]{2,1,0:T(8,128)(2,1)S(1)} %get-tuple-element.48.after.refs_6_), channel_id=1, source_target_pairs={{0,2},{1,3},{2,0},{3,1},{4,6},{5,7},{6,4},{7,5},{8,10},{9,11},{10,... | collective-permute-start | bytes 208904 | tf_op jit(solution)/shard_map/ppermute | solution.py:400
  24.2 5.2 %collective-permute-start.7 = (bf16[17,16,128]{2,1,0:T(8,128)(2,1)S(1)}, bf16[17,16,128]{2,1,0:T(8,128)(2,1)S(1)}, u32[]{:S(2)}, u32[]{:S(2)}) collective-permute-start(bf16[17,16,128]{2,1,0:T(8,128)(2,1)S(1)} %get-tuple-element.52.after.refs_5_), channel_id=1, source_target_pairs={{0,8},{4,12},{8,0},{12,4},{1,9},{5,13},{9,1},{13,5},{2,10},{6,14},... | collective-permute-start | bytes 208904 | tf_op jit(solution)/shard_map/ppermute | solution.py:400
  30.8 6.4 %collective-permute-start.10 = (bf16[17,16,128]{2,1,0:T(8,128)(2,1)S(1)}, bf16[17,16,128]{2,1,0:T(8,128)(2,1)S(1)}, u32[]{:S(2)}, u32[]{:S(2)}) collective-permute-start(bf16[17,16,128]{2,1,0:T(8,128)(2,1)S(1)} %get-tuple-element.56.refs_0_), channel_id=1, source_target_pairs={{0,3},{1,2},{2,1},{3,0},{4,7},{5,6},{6,5},{7,4},{8,11},{9,10},{10,... | collective-permute-start | bytes 208904 | tf_op jit(solution)/shard_map/ppermute | solution.py:400
  32.3 6.1 %collective-permute-start.9 = (bf16[17,16,128]{2,1,0:T(8,128)(2,1)S(1)}, bf16[17,16,128]{2,1,0:T(8,128)(2,1)S(1)}, u32[]{:S(2)}, u32[]{:S(2)}) collective-permute-start(bf16[17,16,128]{2,1,0:T(8,128)(2,1)S(1)} %get-tuple-element.56.refs_0_), channel_id=1, source_target_pairs={{0,1},{1,0},{2,3},{3,2},{4,5},{5,4},{6,7},{7,6},{8,9},{9,8},{10,11... | collective-permute-start | bytes 208904 | tf_op jit(solution)/shard_map/ppermute | solution.py:400
  32.3 6.1 %collective-permute-start.8 = (bf16[17,16,128]{2,1,0:T(8,128)(2,1)S(1)}, bf16[17,16,128]{2,1,0:T(8,128)(2,1)S(1)}, u32[]{:S(2)}, u32[]{:S(2)}) collective-permute-start(bf16[17,16,128]{2,1,0:T(8,128)(2,1)S(1)} %get-tuple-element.56.refs_0_), channel_id=1, source_target_pairs={{0,2},{1,3},{2,0},{3,1},{4,6},{5,7},{6,4},{7,5},{8,10},{9,11},{10,... | collective-permute-start | bytes 208904 | tf_op jit(solution)/shard_map/ppermute | solution.py:400
  38.5 6.2 %collective-permute-start.11 = (f32[16,16,128]{2,1,0:T(8,128)S(1)}, f32[16,16,128]{2,1,0:T(8,128)S(1)}, u32[]{:S(2)}, u32[]{:S(2)}) collective-permute-start(f32[16,16,128]{2,1,0:T(8,128)S(1)} %get-tuple-element.60.refs_0_), channel_id=1, source_target_pairs={{0,4},{4,0},{8,12},{12,8},{1,5},{5,1},{9,13},{13,9},{2,6},{6,2},{1... | collective-permute-start | bytes 393224 | tf_op jit(solution)/shard_map/ppermute | solution.py:400
  38.6 6.2 %collective-permute-start.12 = (f32[16,8,128]{2,1,0:T(8,128)S(1)}, f32[16,8,128]{2,1,0:T(8,128)S(1)}, u32[]{:S(2)}, u32[]{:S(2)}) collective-permute-start(f32[16,8,128]{2,1,0:T(8,128)S(1)} %get-tuple-element.62), channel_id=1, source_target_pairs={{0,4},{4,0},{8,12},{12,8},{1,5},{5,1},{9,13},{13,9},{2,6},{6,2},{1... | collective-permute-start | bytes 196616 | tf_op jit(solution)/shard_map/ppermute | solution.py:400
  39.1 3.4 %collective-permute-start.15 = (f32[8,128]{1,0:T(8,128)S(1)}, f32[8,128]{1,0:T(8,128)S(1)}, u32[]{:S(2)}, u32[]{:S(2)}) collective-permute-start(f32[8,128]{1,0:T(8,128)S(1)} %get-tuple-element.63.refs_4_), channel_id=1, source_target_pairs={{0,12},{4,8},{8,4},{12,0},{1,13},{5,9},{9,5},{13,1},{2,14},{6,10},... | collective-permute-start | bytes 12296 | tf_op jit(solution)/shard_map/ppermute | solution.py:400
  41.1 3.6 %collective-permute-start.14 = (f32[8,128]{1,0:T(8,128)S(1)}, f32[8,128]{1,0:T(8,128)S(1)}, u32[]{:S(2)}, u32[]{:S(2)}) collective-permute-start(f32[8,128]{1,0:T(8,128)S(1)} %get-tuple-element.63.refs_4_), channel_id=1, source_target_pairs={{0,8},{4,12},{8,0},{12,4},{1,9},{5,13},{9,1},{13,5},{2,10},{6,14},... | collective-permute-start | bytes 12296 | tf_op jit(solution)/shard_map/ppermute | solution.py:400
  41.5 3.3 %collective-permute-start.13 = (f32[8,128]{1,0:T(8,128)S(1)}, f32[8,128]{1,0:T(8,128)S(1)}, u32[]{:S(2)}, u32[]{:S(2)}) collective-permute-start(f32[8,128]{1,0:T(8,128)S(1)} %get-tuple-element.63.refs_4_), channel_id=1, source_target_pairs={{0,4},{4,0},{8,12},{12,8},{1,5},{5,1},{9,13},{13,9},{2,6},{6,2},{1... | collective-permute-start | bytes 12296 | tf_op jit(solution)/shard_map/ppermute | solution.py:400

commit v7 on v6

--- a/solution.py
+++ b/solution.py
@@ -168,6 +168,20 @@
     return lax.rem(lax.axis_index("rowblk"), 2) == 1
 
 
+def grid_lines(count, rows, cols, shape):
+    lanes, lines = (lax.broadcasted_iota(jnp.int32, (shape[0] // 2, shape[1]), n) for n in (1, 0))
+    ways = 4
+    found = []
+    for index in (rows, cols):
+        terms = [jnp.zeros(lanes.shape, jnp.int32)] * ways
+        for g in range(index.shape[0]):
+            terms[g % ways] = jnp.where(lanes == g, index[g], terms[g % ways])
+        found.append(add_up(terms))
+    both = jnp.where(lines == 0, found[0], jnp.where(lines == 1, found[1], count[0]))
+    both = both.astype(jnp.float32)
+    return jnp.concatenate([both, jnp.zeros_like(both)], axis=0).astype(jnp.bfloat16)
+
+
 def first_kernel(*refs):
     count, rows_far, cols_far, tiles_far, dual_far, keep, send, tiles, rows, cols, source, acc, dual, sems = refs
     tile = tiles.shape[1]
@@ -189,6 +203,7 @@
         source[b] = split_rows(dual[:, b * tile : (b + 1) * tile])
     for copy in copies:
         copy.wait()
+    lines = grid_lines(count, rows, cols, send.shape[1:])
     first_products(count, rows, cols, tiles, source, acc, lambda first: get_tiles[first].wait())
     odd = is_odd()
     q = keep.shape[0]
@@ -199,6 +214,7 @@
             halves.append((upper_half(a, b), lower_half(a, b)))
         keep[k] = jnp.concatenate([halves[0][0], halves[1][0]], axis=0)
         send[k] = jnp.concatenate([halves[0][1], halves[1][1]], axis=0).astype(jnp.bfloat16)
+    send[q] = lines
 
 
 def turn_tiles(live, tiles, turned):
@@ -209,21 +225,29 @@
     over_parts(tiles, live, part)
 
 
-def turn_kernel(count, rows, cols, tiles, dual, demand, flag, after, turned, extra):
+def turn_kernel(count, tiles, after, turned):
     del after
-    total, half = rows.shape[1], flag.shape[0] // 2
+    turn_tiles(count[0], tiles, turned)
+
+
+def extra_kernel(dual, demand, flag, after, extra):
+    del after
+    half = flag.shape[0] // 2
     odd = is_odd()
     for k in range(half):
         extra[k] = pair_of_blocks(dual, k, half, odd)[1]
         extra[half + k] = pair_of_blocks(demand, k, half, odd)[1]
     for n in range(flag.shape[0] // 8):
         extra[2 * half + n] = flag[8 * n : 8 * (n + 1), :].astype(jnp.float32)
-    last = extra.shape[0] - 1
-    extra[last] = jnp.zeros(extra.shape[1:], jnp.float32)
-    extra[last, 0:1, 0:total] = rows[...].astype(jnp.float32)
-    extra[last, 1:2, 0:total] = cols[...].astype(jnp.float32)
-    extra[last, 2:3, :] = jnp.full((1, extra.shape[2]), count[0], jnp.int32).astype(jnp.float32)
-    turn_tiles(count[0], tiles, turned)
+
+
+def grid_kernel(received, after, grid, whole, sem):
+    del after
+    last = received[received.shape[0] - 1].astype(jnp.float32)
+    whole[...] = last[: whole.shape[0]].astype(jnp.int32)
+    copy = pltpu.make_async_copy(whole, grid, sem)
+    copy.start()
+    copy.wait()
 
 
 def col_kernel(begin, cost, upper, flag, after, start, price, limit):
@@ -266,11 +290,8 @@
         weight = jnp.sqrt(weight * jnp.sqrt(ratio))
         weight_out[...] = jnp.broadcast_to(weight, weight_out.shape)
     else:
-        extra, point_out, out, grid, source, acc, whole, sem = refs
+        grid, point_out, out, source, acc = refs
         point = start
-        whole[...] = extra[extra.shape[0] - 1].astype(jnp.int32)
-        get_grid = pltpu.make_async_copy(whole, grid, sem)
-        get_grid.start()
         weight = jnp.ones((8, 1), jnp.float32)
     q = point_out.shape[0]
     tile = point_out.shape[2]
@@ -290,8 +311,6 @@
     acc[...] = jnp.zeros_like(acc)
     near = (acc.shape[0] - 1) // 2
     half_products(count[0], lambda g: cols[g], lambda g: rows[g], tiles, 0, source, acc)
-    if not last:
-        get_grid.wait()
     half_products(grid[2, 0], lambda g: grid[1, g], lambda g: near + grid[0, g], other, 0 if last else 1, source, acc)
     pack(acc, out, partial_norm(squares), lax.axis_index("colblk"))
 
@@ -348,21 +367,36 @@
     q, pairs = mine.shape[0], mine.shape[1] // 8
     for k in range(q):
         for h in range(pairs):
-            a, b = mine[k, 8 * h : 8 * (h + 1), :], others[k, 8 * h : 8 * (h + 1), :]
+            a, b = mine[k, 8 * h : 8 * (h + 1), :], others(k, h)
             a, b = jnp.where(odd, b, a), jnp.where(odd, a, b)
             for j, value in ((0, upper_half(a, b)), (1, lower_half(a, b))):
                 n = k + (2 * h + j) * q
                 out[:, n * tile : (n + 1) * tile] = value
 
 
-def end_kernel(share, *refs):
-    mine_x, other_x, mine_y, other_y, *parts = refs[:-7]
-    far_x, far_y, far_weight, x_out, y_out, weight_out, sems = refs[-7:]
+def gather_kernel(point, send, both):
+    q = point.shape[0]
+    both[:q] = point[...]
+    for k in range(send.shape[0] // 2):
+        both[q + k] = jnp.concatenate([send[2 * k], send[2 * k + 1]], axis=0)
+
+
+def result_kernel(mine_x, mine_y, other, far_x, far_y, x_out, y_out, sems):
     copies = []
-    for n, (mine, others, out, target) in enumerate(((mine_x, other_x, x_out, far_x), (mine_y, other_y, y_out, far_y))):
+    q = mine_x.shape[0]
+    from_x = lambda k, h: other[k, 8 * h : 8 * (h + 1), :]
+    from_y = lambda k, h: other[q + k // 2, 8 * (k % 2) : 8 * (k % 2 + 1), :]
+    for n, (mine, others, out, target) in enumerate(((mine_x, from_x, x_out, far_x), (mine_y, from_y, y_out, far_y))):
         join(mine, others, out)
         copies.append(pltpu.make_async_copy(out, target, sems.at[n]))
         copies[-1].start()
+    for copy in copies:
+        copy.wait()
+
+
+def weight_kernel(share, *refs):
+    *parts, after, out = refs
+    del after
     both = add_up([p[...] for p in parts])
     found = []
     for first in (0, 3):
@@ -372,11 +406,7 @@
     weight = jnp.where(top(found[0].shape), found[0], found[1])
     lanes, rows = (lax.broadcasted_iota(jnp.int32, both.shape, n) for n in (1, 0))
     row = jnp.sum(jnp.where(lanes == rows, weight, 0.0), axis=0, keepdims=True)
-    weight_out[...] = row[:, : weight_out.shape[1]]
-    copies.append(pltpu.make_async_copy(weight_out, far_weight, sems.at[2]))
-    copies[-1].start()
-    for copy in copies:
-        copy.wait()
+    out[...] = row[:, : out.shape[1]]
 
 
 def call(kernel, inputs, in_specs, outputs, out_specs, scratch, cost=None):
@@ -456,7 +486,7 @@
         first_kernel,
         [tile_count, far(tile_row), far(tile_col), far(tiles), far(dual_start)],
         [SMEM_SPEC] + [FAR_SPEC] * 4,
-        [col_state, pltpu.VMEM((col_quads, 2 * scen, tile), bf16), tiles_like, index, index],
+        [col_state, col_terms, tiles_like, index, index],
         [VMEM_SPEC] * 3 + [SMEM_SPEC] * 2,
         [
             pltpu.VMEM((row_blocks, 2 * scen, tile), bf16),
@@ -465,18 +495,27 @@
             pltpu.SemaphoreType.DMA((3 + pl.cdiv(total, PART),)),
         ],
     )
-    terms = (keep + swap(send, "rowblk", 1).astype(f32)).astype(bf16)
+    received = swap(send, "rowblk", 1)
+    terms = (keep + received[:col_quads].astype(f32)).astype(bf16)
     held_tiles, terms = lax.optimization_barrier((tiles, terms))
     parts = butterfly(terms, "rowblk", 2, 2)
     other = swap(held_tiles, "rowblk", 1)
-    turned, extra = call(
+    (turned,) = call(
         turn_kernel,
-        [tile_count, tile_row.reshape(1, total), tile_col.reshape(1, total), tiles, dual_start, demand, row_flag, terms],
-        [SMEM_SPEC] + [VMEM_SPEC] * 7,
-        [tiles_like, pltpu.VMEM((2 * row_quads + row_blocks // 8 + 1, scen, tile), f32)],
-        [VMEM_SPEC] * 2,
+        [tile_count, tiles, terms],
+        [SMEM_SPEC] + [VMEM_SPEC] * 2,
+        [tiles_like],
+        [VMEM_SPEC],
         [],
         turning,
+    )
+    (extra,) = call(
+        extra_kernel,
+        [dual_start, demand, row_flag, terms],
+        [VMEM_SPEC] * 4,
+        [pltpu.VMEM((2 * row_quads + row_blocks // 8, scen, tile), f32)],
+        [VMEM_SPEC],
+        [],
     )
     extra = swap(extra, "rowblk", 1)
     columns = call(
@@ -488,6 +527,14 @@
         [],
     )
     start, price, limit = columns
+    (grid,) = call(
+        grid_kernel,
+        [received, terms],
+        [VMEM_SPEC] * 2,
+        [pltpu.SMEM((scen, tile), i32)],
+        [SMEM_SPEC],
+        [pltpu.VMEM((scen, tile), i32), pltpu.SemaphoreType.DMA],
+    )
     own = [tile_count, rows, cols]
     weight = jnp.ones((scen, tile), f32)
     for step in range(ITERS):
@@ -514,14 +561,14 @@
                 to_rows,
             )
         else:
-            vectors = [*parts, price, limit, start, extra]
-            point, terms, grid = call(
+            vectors = [*parts, price, limit, start]
+            point, terms = call(
                 functools.partial(primal_kernel, mix, False, len(parts)),
-                [*own, turned, other, *vectors],
-                [SMEM_SPEC] * 3 + [VMEM_SPEC] * (2 + len(vectors)),
-                [col_state, row_terms, pltpu.SMEM((scen, tile), i32)],
-                [VMEM_SPEC] * 2 + [SMEM_SPEC],
-                [*to_rows, pltpu.VMEM((scen, tile), i32), pltpu.SemaphoreType.DMA],
+                [*own, turned, other, *vectors, grid],
+                [SMEM_SPEC] * 3 + [VMEM_SPEC] * (2 + len(vectors)) + [SMEM_SPEC],
+                [col_state, row_terms],
+                [VMEM_SPEC] * 2,
+                to_rows,
             )
         parts = butterfly(terms, "colblk", 4)
         if len(parts) == 4:
@@ -554,17 +601,32 @@
                 [VMEM_SPEC] * 3,
                 to_cols,
             )
-    point, terms = lax.optimization_barrier((point, terms))
     parts = butterfly(terms, "rowblk", 4)
-    halves = [point, swap(point, "rowblk", 1), keep, swap(send, "rowblk", 1)]
-    shapes = [primal_start.shape, dual_start.shape, (1, scen)]
-    point, dual, weight = call(
-        functools.partial(end_kernel, 2.0 / lax.axis_size("rowblk")),
-        [*halves, *parts],
-        [VMEM_SPEC] * (4 + len(parts)),
+    (both,) = call(
+        gather_kernel,
+        [point, send],
+        [VMEM_SPEC] * 2,
+        [pltpu.VMEM((col_quads + row_quads // 2, 2 * scen, tile), f32)],
+        [VMEM_SPEC],
+        [],
+    )
+    halves = [point, keep, swap(both, "rowblk", 1)]
+    shapes = [primal_start.shape, dual_start.shape]
+    point, dual = call(
+        result_kernel,
+        halves,
+        [VMEM_SPEC] * 3,
         [jax.ShapeDtypeStruct(shape, f32) for shape in shapes],
-        [FAR_SPEC] * 3,
-        [pltpu.VMEM(shape, f32) for shape in shapes] + [pltpu.SemaphoreType.DMA((3,))],
+        [FAR_SPEC] * 2,
+        [pltpu.VMEM(shape, f32) for shape in shapes] + [pltpu.SemaphoreType.DMA((2,))],
+    )
+    (weight,) = call(
+        functools.partial(weight_kernel, 2.0 / lax.axis_size("rowblk")),
+        [*parts, far(dual)],
+        [VMEM_SPEC] * len(parts) + [FAR_SPEC],
+        [jax.ShapeDtypeStruct((1, scen), f32)],
+        [VMEM_SPEC],
+        [],
     )
     return point, dual, weight.reshape(scen)
 

time: 45.2 us -> 44.3 us (0.980); the launches traced: 45.8 us -> 43.6 us
  waiting for transfers between devices: 16.4 us -> 14.8 us
  starting transfers between devices: 19.5 us -> 18.5 us
  Pallas kernels: 8.3 us -> 8.77 us
    ppermute x16 -> x15, waiting for transfers between devices: 16.4 us -> 14.8 us  [swap(): return lax.ppermute(value, axis, [(i, i ^ mask) for i in range(size)])]
    ppermute x16 -> x15, starting transfers between devices: 19.5 us -> 18.5 us  [swap(): return lax.ppermute(value, axis, [(i, i ^ mask) for i in range(size)])]
    pallas_call x10 -> x14, Pallas kernels: 8.3 us -> 8.77 us  [call(): pl.pallas_call(kernel, out_shape=outputs, in_specs=in_specs, out_specs=ou...]
  transfers between devices with their start and end apart: 16 -> 15, of which waited for: 9 -> 10; matrix products, arithmetic and copies ran while one was open for 0% -> 0% of each run, Pallas kernels for 3% -> 9%
where the time goes in v7:
time: 44.3 us; the launch traced here: 43.6 us
  starting transfers between devices  18.5 us (42%)
  waiting for transfers between devices  14.8 us (33%)
  Pallas kernels  8.77 us (20%)
  between operations  1.5 us (3%)
    ppermute x15, starting transfers between devices, swap(): return lax.ppermute(value, axis, [(i, i ^ mask) for i in range(size)])  18.5 us
    ppermute x15, waiting for transfers between devices, swap(): return lax.ppermute(value, axis, [(i, i ^ mask) for i in range(size)])  14.8 us
    pallas_call x14, Pallas kernels, call(): pl.pallas_call(kernel, out_shape=outputs, in_specs=in_specs, out_specs=ou...  8.77 us
  transfers between devices with their start and end apart: 15, of which 10 were waited for; matrix products, arithmetic and copies ran while one was open for 0% of the time, Pallas kernels for 9%

profile of v7, /device:TPU:0, one launch (start us, length us, event | category | flops | bytes accessed | tf_op | source)
XLA Modules:
  0.0 43.6 jit_solution(16847381150898122478)
XLA Ops:
  0.6 0.0 copy-start
  1.3 1.9 %shard_map.130 = (f32[16,16,128]{2,1,0:T(8,128)S(1)}, bf16[17,16,128]{2,1,0:T(8,128)(2,1)S(1)}, bf16[96,128,128]{2,1,0:T(8,128)(2,1)S(1)}, s32[96]{0:T(128)S(4)}, s32[96]{0:T(128)S(4)}) custom-call(s32[1]{0:T(128)S(6)} %copy.14.refs_0_.count, s32[96]{0:T(128)} %refs_1_.1, s32[96]{0:T(128)} %refs_2_.1, bf16[96,128,128]{2,1,0:T(8,128)(2,1)} %refs_3_.1, ...), custom_call_target="tpu_custom_call" | custom-call | tf_op jit(solution)/shard_map/pallas_call | solution.py:413
  3.2 0.5 %collective-permute-start = (bf16[17,16,128]{2,1,0:T(8,128)(2,1)S(1)}, bf16[17,16,128]{2,1,0:T(8,128)(2,1)S(1)}, u32[]{:S(2)}, u32[]{:S(2)}) collective-permute-start(bf16[17,16,128]{2,1,0:T(8,128)(2,1)S(1)} %get-tuple-element.33), channel_id=1, source_target_pairs={{0,4},{4,0},{8,12},{12,8},{1,5},{5,1},{9,13},{13,9},{2,6},{6,2},{1... | collective-permute-start | bytes 208904 | tf_op jit(solution)/shard_map/ppermute | solution.py:430
  3.8 0.9 %collective-permute-done.received = bf16[17,16,128]{2,1,0:T(8,128)(2,1)S(1)} collective-permute-done((bf16[17,16,128]{2,1,0:T(8,128)(2,1)S(1)}, bf16[17,16,128]{2,1,0:T(8,128)(2,1)S(1)}, u32[]{:S(2)}, u32[]{:S(2)}) %collective-permute-start) | collective-permute-done | bytes 69664 | tf_op jit(solution)/shard_map/ppermute | solution.py:430
  4.7 0.4 collective-permute-start.1
  5.1 0.0 copy-done.1
  5.2 0.0 copy-start.2
  5.2 0.0 copy-start.4
  5.2 0.0 copy-start.5
  5.2 0.0 copy-start.6
  5.2 0.2 collective-permute-start.6
  5.4 2.6 %collective-permute-start.2 = (bf16[16,16,128]{2,1,0:T(8,128)(2,1)S(1)}, bf16[16,16,128]{2,1,0:T(8,128)(2,1)S(1)}, u32[]{:S(2)}, u32[]{:S(2)}) collective-permute-start(bf16[16,16,128]{2,1,0:T(8,128)(2,1)S(1)} %add_convert_fusion.after.refs_5_), channel_id=1, source_target_pairs={{0,8},{4,12},{8,0},{12,4},{1,9},{5,13},{9,1},{13,5},{2,10},{6,14},... | collective-permute-start | bytes 196616 | tf_op jit(solution)/shard_map/ppermute | solution.py:430
  8.0 0.5 %shard_map.131.refs_3_ = bf16[96,128,128]{2,1,0:T(8,128)(2,1)S(1)} custom-call(s32[1]{0:T(128)S(6)} %copy.14.refs_0_.count, bf16[96,128,128]{2,1,0:T(8,128)(2,1)S(1)} %get-tuple-element.35.tiles.refs_4_, bf16[16,16,128]{2,1,0:T(8,128)(2,1)S(1)} %add_convert_fusion.after.refs_5_), custom_call_target="tpu_custom_call" | custom-call | bytes 6291456 | tf_op jit(solution)/shard_map/pallas_call | solution.py:413
  8.6 0.1 shard_map.133
  8.6 0.6 %shard_map.132.refs_10_.refs_3_.grid = s32[8,128]{1,0:T(8,128)S(4)} custom-call(bf16[17,16,128]{2,1,0:T(8,128)(2,1)S(1)} %collective-permute-done.received, bf16[16,16,128]{2,1,0:T(8,128)(2,1)S(1)} %add_convert_fusion.after.refs_5_), custom_call_target="tpu_custom_call" | custom-call | tf_op jit(solution)/shard_map/pallas_call | solution.py:413
  9.3 1.1 %collective-permute-done.2.refs_6_ = bf16[16,16,128]{2,1,0:T(8,128)(2,1)S(1)} collective-permute-done((bf16[16,16,128]{2,1,0:T(8,128)(2,1)S(1)}, bf16[16,16,128]{2,1,0:T(8,128)(2,1)S(1)}, u32[]{:S(2)}, u32[]{:S(2)}) %collective-permute-start.2) | collective-permute-done | bytes 65568 | tf_op jit(solution)/shard_map/ppermute | solution.py:430
  10.4 0.0 collective-permute-done.1.refs_4_.refs_5_.tiles
  10.4 1.1 %shard_map.134 = (f32[16,16,128]{2,1,0:T(8,128)S(1)}, bf16[17,16,128]{2,1,0:T(8,128)(2,1)S(1)}) custom-call(s32[1]{0:T(128)S(6)} %copy.14.refs_0_.count, s32[96]{0:T(128)S(4)} %get-tuple-element.29.refs_1_, s32[96]{0:T(128)S(4)} %get-tuple-element.30.refs_2_, bf16[96,128,128]{2,1,0:T(8,128)(2,1)S(1)} %shard_map.131.refs_3_, ...), custom_call_target="tpu_custom_call" | custom-call | tf_op jit(solution)/shard_map/pallas_call | solution.py:413
  11.5 4.8 %collective-permute-start.5 = (bf16[17,16,128]{2,1,0:T(8,128)(2,1)S(1)}, bf16[17,16,128]{2,1,0:T(8,128)(2,1)S(1)}, u32[]{:S(2)}, u32[]{:S(2)}) collective-permute-start(bf16[17,16,128]{2,1,0:T(8,128)(2,1)S(1)} %get-tuple-element.39.after.refs_6_), channel_id=1, source_target_pairs={{0,3},{1,2},{2,1},{3,0},{4,7},{5,6},{6,5},{7,4},{8,11},{9,10},{10,... | collective-permute-start | bytes 208904 | tf_op jit(solution)/shard_map/ppermute | solution.py:430
  16.3 0.0 collective-permute-start.4
  16.3 0.6 %collective-permute-start.3 = (bf16[17,16,128]{2,1,0:T(8,128)(2,1)S(1)}, bf16[17,16,128]{2,1,0:T(8,128)(2,1)S(1)}, u32[]{:S(2)}, u32[]{:S(2)}) collective-permute-start(bf16[17,16,128]{2,1,0:T(8,128)(2,1)S(1)} %get-tuple-element.39.after.refs_6_), channel_id=1, source_target_pairs={{0,2},{1,3},{2,0},{3,1},{4,6},{5,7},{6,4},{7,5},{8,10},{9,11},{10,... | collective-permute-start | bytes 208904 | tf_op jit(solution)/shard_map/ppermute | solution.py:430
  16.9 0.0 collective-permute-done.6.extra
  16.9 0.1 shard_map.136
  17.0 2.3 %collective-permute-done.5.refs_9_ = bf16[17,16,128]{2,1,0:T(8,128)(2,1)S(1)} collective-permute-done((bf16[17,16,128]{2,1,0:T(8,128)(2,1)S(1)}, bf16[17,16,128]{2,1,0:T(8,128)(2,1)S(1)}, u32[]{:S(2)}, u32[]{:S(2)}) %collective-permute-start.5) | collective-permute-done | bytes 69664 | tf_op jit(solution)/shard_map/ppermute | solution.py:430
  19.3 2.1 %collective-permute-done.4.refs_8_ = bf16[17,16,128]{2,1,0:T(8,128)(2,1)S(1)} collective-permute-done((bf16[17,16,128]{2,1,0:T(8,128)(2,1)S(1)}, bf16[17,16,128]{2,1,0:T(8,128)(2,1)S(1)}, u32[]{:S(2)}, u32[]{:S(2)}) %collective-permute-start.4) | collective-permute-done | bytes 69664 | tf_op jit(solution)/shard_map/ppermute | solution.py:430
  21.4 0.9 %collective-permute-done.3.refs_7_ = bf16[17,16,128]{2,1,0:T(8,128)(2,1)S(1)} collective-permute-done((bf16[17,16,128]{2,1,0:T(8,128)(2,1)S(1)}, bf16[17,16,128]{2,1,0:T(8,128)(2,1)S(1)}, u32[]{:S(2)}, u32[]{:S(2)}) %collective-permute-start.3) | collective-permute-done | bytes 69664 | tf_op jit(solution)/shard_map/ppermute | solution.py:430
  22.3 1.0 %shard_map.137 = (f32[16,16,128]{2,1,0:T(8,128)S(1)}, f32[8,128]{1,0:T(8,128)S(1)}, bf16[17,16,128]{2,1,0:T(8,128)(2,1)S(1)}) custom-call(s32[1]{0:T(128)S(6)} %copy.14.refs_0_.count, s32[96]{0:T(128)S(4)} %get-tuple-element.29.refs_1_, s32[96]{0:T(128)S(4)} %get-tuple-element.30.refs_2_, s32[8,128]{1,0:T(8,128)S(4)} %shard_map.132.refs_10_.refs_3_.grid, ...), custom_call_target="tpu_custom_call" | custom-call | tf_op jit(solution)/shard_map/pallas_call | solution.py:413
  23.3 2.7 %collective-permute-start.7 = (bf16[17,16,128]{2,1,0:T(8,128)(2,1)S(1)}, bf16[17,16,128]{2,1,0:T(8,128)(2,1)S(1)}, u32[]{:S(2)}, u32[]{:S(2)}) collective-permute-start(bf16[17,16,128]{2,1,0:T(8,128)(2,1)S(1)} %get-tuple-element.43.after.refs_5_), channel_id=1, source_target_pairs={{0,8},{4,12},{8,0},{12,4},{1,9},{5,13},{9,1},{13,5},{2,10},{6,14},... | collective-permute-start | bytes 208904 | tf_op jit(solution)/shard_map/ppermute | solution.py:430
  26.0 0.5 %shard_map.138.refs_4_ = bf16[96,128,128]{2,1,0:T(8,128)(2,1)S(1)} custom-call(s32[8,128]{1,0:T(8,128)S(4)} %shard_map.132.refs_10_.refs_3_.grid, bf16[96,128,128]{2,1,0:T(8,128)(2,1)S(1)} %collective-permute-done.1.refs_4_.refs_5_.tiles, bf16[17,16,128]{2,1,0:T(8,128)(2,1)S(1)} %get-tuple-element.43.after.refs_5_), custom_call_target="tpu_custom_call" | custom-call | bytes 6291456 | tf_op jit(solution)/shard_map/pallas_call | solution.py:413
  26.5 1.8 %collective-permute-done.7.refs_6_ = bf16[17,16,128]{2,1,0:T(8,128)(2,1)S(1)} collective-permute-done((bf16[17,16,128]{2,1,0:T(8,128)(2,1)S(1)}, bf16[17,16,128]{2,1,0:T(8,128)(2,1)S(1)}, u32[]{:S(2)}, u32[]{:S(2)}) %collective-permute-start.7) | collective-permute-done | bytes 69664 | tf_op jit(solution)/shard_map/ppermute | solution.py:430
  28.2 1.2 %shard_map.139 = (f32[16,16,128]{2,1,0:T(8,128)S(1)}, f32[8,128]{1,0:T(8,128)S(1)}, bf16[17,16,128]{2,1,0:T(8,128)(2,1)S(1)}) custom-call(s32[1]{0:T(128)S(6)} %copy.14.refs_0_.count, s32[96]{0:T(128)S(4)} %get-tuple-element.29.refs_1_, s32[96]{0:T(128)S(4)} %get-tuple-element.30.refs_2_, bf16[96,128,128]{2,1,0:T(8,128)(2,1)S(1)} %shard_map.131.refs_3_, ...), custom_call_target="tpu_custom_call" | custom-call | tf_op jit(solution)/shard_map/pallas_call | solution.py:413
  29.4 2.6 %collective-permute-start.10 = (bf16[17,16,128]{2,1,0:T(8,128)(2,1)S(1)}, bf16[17,16,128]{2,1,0:T(8,128)(2,1)S(1)}, u32[]{:S(2)}, u32[]{:S(2)}) collective-permute-start(bf16[17,16,128]{2,1,0:T(8,128)(2,1)S(1)} %get-tuple-element.47.refs_0_), channel_id=1, source_target_pairs={{0,3},{1,2},{2,1},{3,0},{4,7},{5,6},{6,5},{7,4},{8,11},{9,10},{10,... | collective-permute-start | bytes 208904 | tf_op jit(solution)/shard_map/ppermute | solution.py:430
  32.0 0.0 collective-permute-start.9
  32.0 1.8 %collective-permute-start.8 = (bf16[17,16,128]{2,1,0:T(8,128)(2,1)S(1)}, bf16[17,16,128]{2,1,0:T(8,128)(2,1)S(1)}, u32[]{:S(2)}, u32[]{:S(2)}) collective-permute-start(bf16[17,16,128]{2,1,0:T(8,128)(2,1)S(1)} %get-tuple-element.47.refs_0_), channel_id=1, source_target_pairs={{0,2},{1,3},{2,0},{3,1},{4,6},{5,7},{6,4},{7,5},{8,10},{9,11},{10,... | collective-permute-start | bytes 208904 | tf_op jit(solution)/shard_map/ppermute | solution.py:430
  33.8 2.2 %collective-permute-done.10.refs_3_ = bf16[17,16,128]{2,1,0:T(8,128)(2,1)S(1)} collective-permute-done((bf16[17,16,128]{2,1,0:T(8,128)(2,1)S(1)}, bf16[17,16,128]{2,1,0:T(8,128)(2,1)S(1)}, u32[]{:S(2)}, u32[]{:S(2)}) %collective-permute-start.10) | collective-permute-done | bytes 69664 | tf_op jit(solution)/shard_map/ppermute | solution.py:430
  36.0 1.4 %collective-permute-done.9.refs_2_ = bf16[17,16,128]{2,1,0:T(8,128)(2,1)S(1)} collective-permute-done((bf16[17,16,128]{2,1,0:T(8,128)(2,1)S(1)}, bf16[17,16,128]{2,1,0:T(8,128)(2,1)S(1)}, u32[]{:S(2)}, u32[]{:S(2)}) %collective-permute-start.9) | collective-permute-done | bytes 69664 | tf_op jit(solution)/shard_map/ppermute | solution.py:430
  37.4 0.0 collective-permute-done.8.refs_1_
  37.4 0.2 shard_map.140
  37.6 0.1 collective-permute-start.11
  37.7 1.5 %collective-permute-start.14 = (f32[8,128]{1,0:T(8,128)S(1)}, f32[8,128]{1,0:T(8,128)S(1)}, u32[]{:S(2)}, u32[]{:S(2)}) collective-permute-start(f32[8,128]{1,0:T(8,128)S(1)} %get-tuple-element.54.refs_0_), channel_id=1, source_target_pairs={{0,12},{4,8},{8,4},{12,0},{1,13},{5,9},{9,5},{13,1},{2,14},{6,10},... | collective-permute-start | bytes 12296 | tf_op jit(solution)/shard_map/ppermute | solution.py:430
  39.1 0.7 %collective-permute-start.13 = (f32[8,128]{1,0:T(8,128)S(1)}, f32[8,128]{1,0:T(8,128)S(1)}, u32[]{:S(2)}, u32[]{:S(2)}) collective-permute-start(f32[8,128]{1,0:T(8,128)S(1)} %get-tuple-element.54.refs_0_), channel_id=1, source_target_pairs={{0,8},{4,12},{8,0},{12,4},{1,9},{5,13},{9,1},{13,5},{2,10},{6,14},... | collective-permute-start | bytes 12296 | tf_op jit(solution)/shard_map/ppermute | solution.py:430
  39.8 0.0 collective-permute-start.12
  39.8 0.0 collective-permute-done.11.other
  39.8 0.8 %shard_map.142 = (f32[8,8192]{1,0:T(8,128)}, f32[8,4096]{1,0:T(8,128)}) custom-call(f32[16,16,128]{2,1,0:T(8,128)S(1)} %get-tuple-element.46.point.mine_x, f32[16,8,128]{2,1,0:T(8,128)S(1)} %get-tuple-element.50.mine_y, f32[24,16,128]{2,1,0:T(8,128)S(1)} %collective-permute-done.11.other), custom_call_target="tpu_custom_call" | custom-call | tf_op jit(solution)/shard_map/pallas_call | solution.py:413
  40.6 0.1 collective-permute-done.14.refs_3_
  40.8 2.0 %collective-permute-done.13.refs_2_ = f32[8,128]{1,0:T(8,128)S(1)} collective-permute-done((f32[8,128]{1,0:T(8,128)S(1)}, f32[8,128]{1,0:T(8,128)S(1)}, u32[]{:S(2)}, u32[]{:S(2)}) %collective-permute-start.13) | collective-permute-done | bytes 4128 | tf_op jit(solution)/shard_map/ppermute | solution.py:430
  42.8 0.0 collective-permute-done.12.refs_1_
  42.8 0.8 %shard_map.143 = f32[1,8]{1,0:T(1,128)} custom-call(f32[8,128]{1,0:T(8,128)S(1)} %get-tuple-element.54.refs_0_, f32[8,128]{1,0:T(8,128)S(1)} %collective-permute-done.12.refs_1_, f32[8,128]{1,0:T(8,128)S(1)} %collective-permute-done.13.refs_2_, f32[8,128]{1,0:T(8,128)S(1)} %collective-permute-done.14.refs_3_, f32[8,4096]{1,0:T(8,128)} %get-tuple-element.27.refs_4_), custom_call_target="tpu_custom_call" | custom-call | tf_op jit(solution)/shard_map/pallas_call | solution.py:413
  (12 shorter events, 0.1 us)
Async XLA Ops:
  0.6 4.5 %copy-start = (f32[8,4096]{1,0:T(8,128)S(1)}, f32[8,4096]{1,0:T(8,128)}, u32[]{:S(2)}) copy-start(f32[8,4096]{1,0:T(8,128)} %begin.3) | copy-start | bytes 393220
  0.6 4.5 %copy-start.1 = (f32[8,4096]{1,0:T(8,128)S(1)}, f32[8,4096]{1,0:T(8,128)}, u32[]{:S(2)}) copy-start(f32[8,4096]{1,0:T(8,128)} %demand.3) | copy-start | bytes 393220
  0.7 4.5 %copy-start.3 = (s32[4096]{0:T(1024)S(1)}, s32[4096]{0:T(1024)}, u32[]{:S(2)}) copy-start(s32[4096]{0:T(1024)} %param.19) | copy-start | bytes 49156
  3.2 1.4 %collective-permute-start = (bf16[17,16,128]{2,1,0:T(8,128)(2,1)S(1)}, bf16[17,16,128]{2,1,0:T(8,128)(2,1)S(1)}, u32[]{:S(2)}, u32[]{:S(2)}) collective-permute-start(bf16[17,16,128]{2,1,0:T(8,128)(2,1)S(1)} %get-tuple-element.33), channel_id=1, source_target_pairs={{0,4},{4,0},{8,12},{12,8},{1,5},{5,1},{9,13},{13,9},{2,6},{6,2},{1... | collective-permute-start | bytes 208904 | tf_op jit(solution)/shard_map/ppermute | solution.py:430
  4.7 5.7 %collective-permute-start.1 = (bf16[96,128,128]{2,1,0:T(8,128)(2,1)S(1)}, bf16[96,128,128]{2,1,0:T(8,128)(2,1)S(1)}, u32[]{:S(2)}, u32[]{:S(2)}) collective-permute-start(bf16[96,128,128]{2,1,0:T(8,128)(2,1)S(1)} %get-tuple-element.35.tiles.refs_4_), channel_id=1, source_target_pairs={{0,4},{4,0},{8,12},{12,8},{1,5},{5,1},{9,13},{13,9},{2,6},{6,2},{1... | collective-permute-start | bytes 9437192 | tf_op jit(solution)/shard_map/ppermute | solution.py:430
  5.2 3.4 %copy-start.2 = (f32[8,8192]{1,0:T(8,128)S(1)}, f32[8,8192]{1,0:T(8,128)}, u32[]{:S(2)}) copy-start(f32[8,8192]{1,0:T(8,128)} %begin.2) | copy-start | bytes 786436
  5.2 3.4 %copy-start.4 = (f32[8192]{0:T(1024)S(1)}, f32[8192]{0:T(1024)}, u32[]{:S(2)}) copy-start(f32[8192]{0:T(1024)} %param.15) | copy-start | bytes 98308
  5.2 3.4 %copy-start.5 = (f32[8192]{0:T(1024)S(1)}, f32[8192]{0:T(1024)}, u32[]{:S(2)}) copy-start(f32[8192]{0:T(1024)} %param.17) | copy-start | bytes 98308
  5.2 3.4 %copy-start.6 = (s32[8192]{0:T(1024)S(1)}, s32[8192]{0:T(1024)}, u32[]{:S(2)}) copy-start(s32[8192]{0:T(1024)} %param.18) | copy-start | bytes 98308
  5.2 11.7 %collective-permute-start.6 = (f32[36,8,128]{2,1,0:T(8,128)S(1)}, f32[36,8,128]{2,1,0:T(8,128)S(1)}, u32[]{:S(2)}, u32[]{:S(2)}) collective-permute-start(f32[36,8,128]{2,1,0:T(8,128)S(1)} %shard_map.135), channel_id=1, source_target_pairs={{0,4},{4,0},{8,12},{12,8},{1,5},{5,1},{9,13},{13,9},{2,6},{6,2},{1... | collective-permute-start | bytes 442376 | tf_op jit(solution)/shard_map/ppermute | solution.py:430
  5.4 5.0 %collective-permute-start.2 = (bf16[16,16,128]{2,1,0:T(8,128)(2,1)S(1)}, bf16[16,16,128]{2,1,0:T(8,128)(2,1)S(1)}, u32[]{:S(2)}, u32[]{:S(2)}) collective-permute-start(bf16[16,16,128]{2,1,0:T(8,128)(2,1)S(1)} %add_convert_fusion.after.refs_5_), channel_id=1, source_target_pairs={{0,8},{4,12},{8,0},{12,4},{1,9},{5,13},{9,1},{13,5},{2,10},{6,14},... | collective-permute-start | bytes 196616 | tf_op jit(solution)/shard_map/ppermute | solution.py:430
  11.5 7.8 %collective-permute-start.5 = (bf16[17,16,128]{2,1,0:T(8,128)(2,1)S(1)}, bf16[17,16,128]{2,1,0:T(8,128)(2,1)S(1)}, u32[]{:S(2)}, u32[]{:S(2)}) collective-permute-start(bf16[17,16,128]{2,1,0:T(8,128)(2,1)S(1)} %get-tuple-element.39.after.refs_6_), channel_id=1, source_target_pairs={{0,3},{1,2},{2,1},{3,0},{4,7},{5,6},{6,5},{7,4},{8,11},{9,10},{10,... | collective-permute-start | bytes 208904 | tf_op jit(solution)/shard_map/ppermute | solution.py:430
  16.3 5.1 %collective-permute-start.4 = (bf16[17,16,128]{2,1,0:T(8,128)(2,1)S(1)}, bf16[17,16,128]{2,1,0:T(8,128)(2,1)S(1)}, u32[]{:S(2)}, u32[]{:S(2)}) collective-permute-start(bf16[17,16,128]{2,1,0:T(8,128)(2,1)S(1)} %get-tuple-element.39.after.refs_6_), channel_id=1, source_target_pairs={{0,1},{1,0},{2,3},{3,2},{4,5},{5,4},{6,7},{7,6},{8,9},{9,8},{10,11... | collective-permute-start | bytes 208904 | tf_op jit(solution)/shard_map/ppermute | solution.py:430
  16.3 6.0 %collective-permute-start.3 = (bf16[17,16,128]{2,1,0:T(8,128)(2,1)S(1)}, bf16[17,16,128]{2,1,0:T(8,128)(2,1)S(1)}, u32[]{:S(2)}, u32[]{:S(2)}) collective-permute-start(bf16[17,16,128]{2,1,0:T(8,128)(2,1)S(1)} %get-tuple-element.39.after.refs_6_), channel_id=1, source_target_pairs={{0,2},{1,3},{2,0},{3,1},{4,6},{5,7},{6,4},{7,5},{8,10},{9,11},{10,... | collective-permute-start | bytes 208904 | tf_op jit(solution)/shard_map/ppermute | solution.py:430
  23.3 5.0 %collective-permute-start.7 = (bf16[17,16,128]{2,1,0:T(8,128)(2,1)S(1)}, bf16[17,16,128]{2,1,0:T(8,128)(2,1)S(1)}, u32[]{:S(2)}, u32[]{:S(2)}) collective-permute-start(bf16[17,16,128]{2,1,0:T(8,128)(2,1)S(1)} %get-tuple-element.43.after.refs_5_), channel_id=1, source_target_pairs={{0,8},{4,12},{8,0},{12,4},{1,9},{5,13},{9,1},{13,5},{2,10},{6,14},... | collective-permute-start | bytes 208904 | tf_op jit(solution)/shard_map/ppermute | solution.py:430
  29.4 6.6 %collective-permute-start.10 = (bf16[17,16,128]{2,1,0:T(8,128)(2,1)S(1)}, bf16[17,16,128]{2,1,0:T(8,128)(2,1)S(1)}, u32[]{:S(2)}, u32[]{:S(2)}) collective-permute-start(bf16[17,16,128]{2,1,0:T(8,128)(2,1)S(1)} %get-tuple-element.47.refs_0_), channel_id=1, source_target_pairs={{0,3},{1,2},{2,1},{3,0},{4,7},{5,6},{6,5},{7,4},{8,11},{9,10},{10,... | collective-permute-start | bytes 208904 | tf_op jit(solution)/shard_map/ppermute | solution.py:430
  32.0 5.4 %collective-permute-start.9 = (bf16[17,16,128]{2,1,0:T(8,128)(2,1)S(1)}, bf16[17,16,128]{2,1,0:T(8,128)(2,1)S(1)}, u32[]{:S(2)}, u32[]{:S(2)}) collective-permute-start(bf16[17,16,128]{2,1,0:T(8,128)(2,1)S(1)} %get-tuple-element.47.refs_0_), channel_id=1, source_target_pairs={{0,1},{1,0},{2,3},{3,2},{4,5},{5,4},{6,7},{7,6},{8,9},{9,8},{10,11... | collective-permute-start | bytes 208904 | tf_op jit(solution)/shard_map/ppermute | solution.py:430
  32.0 5.4 %collective-permute-start.8 = (bf16[17,16,128]{2,1,0:T(8,128)(2,1)S(1)}, bf16[17,16,128]{2,1,0:T(8,128)(2,1)S(1)}, u32[]{:S(2)}, u32[]{:S(2)}) collective-permute-start(bf16[17,16,128]{2,1,0:T(8,128)(2,1)S(1)} %get-tuple-element.47.refs_0_), channel_id=1, source_target_pairs={{0,2},{1,3},{2,0},{3,1},{4,6},{5,7},{6,4},{7,5},{8,10},{9,11},{10,... | collective-permute-start | bytes 208904 | tf_op jit(solution)/shard_map/ppermute | solution.py:430
  37.6 2.2 %collective-permute-start.11 = (f32[24,16,128]{2,1,0:T(8,128)S(1)}, f32[24,16,128]{2,1,0:T(8,128)S(1)}, u32[]{:S(2)}, u32[]{:S(2)}) collective-permute-start(f32[24,16,128]{2,1,0:T(8,128)S(1)} %shard_map.141), channel_id=1, source_target_pairs={{0,4},{4,0},{8,12},{12,8},{1,5},{5,1},{9,13},{13,9},{2,6},{6,2},{1... | collective-permute-start | bytes 589832 | tf_op jit(solution)/shard_map/ppermute | solution.py:430
  37.7 3.1 %collective-permute-start.14 = (f32[8,128]{1,0:T(8,128)S(1)}, f32[8,128]{1,0:T(8,128)S(1)}, u32[]{:S(2)}, u32[]{:S(2)}) collective-permute-start(f32[8,128]{1,0:T(8,128)S(1)} %get-tuple-element.54.refs_0_), channel_id=1, source_target_pairs={{0,12},{4,8},{8,4},{12,0},{1,13},{5,9},{9,5},{13,1},{2,14},{6,10},... | collective-permute-start | bytes 12296 | tf_op jit(solution)/shard_map/ppermute | solution.py:430
  39.1 3.6 %collective-permute-start.13 = (f32[8,128]{1,0:T(8,128)S(1)}, f32[8,128]{1,0:T(8,128)S(1)}, u32[]{:S(2)}, u32[]{:S(2)}) collective-permute-start(f32[8,128]{1,0:T(8,128)S(1)} %get-tuple-element.54.refs_0_), channel_id=1, source_target_pairs={{0,8},{4,12},{8,0},{12,4},{1,9},{5,13},{9,1},{13,5},{2,10},{6,14},... | collective-permute-start | bytes 12296 | tf_op jit(solution)/shard_map/ppermute | solution.py:430
  39.8 2.9 %collective-permute-start.12 = (f32[8,128]{1,0:T(8,128)S(1)}, f32[8,128]{1,0:T(8,128)S(1)}, u32[]{:S(2)}, u32[]{:S(2)}) collective-permute-start(f32[8,128]{1,0:T(8,128)S(1)} %get-tuple-element.54.refs_0_), channel_id=1, source_target_pairs={{0,4},{4,0},{8,12},{12,8},{1,5},{5,1},{9,13},{13,9},{2,6},{6,2},{1... | collective-permute-start | bytes 12296 | tf_op jit(solution)/shard_map/ppermute | solution.py:430

commit v8 on v7

--- a/solution.py
+++ b/solution.py
@@ -279,18 +279,18 @@
 
 
 def primal_kernel(mix, last, n_parts, *refs):
-    count, rows, cols, tiles, other = refs[:5]
-    parts = refs[5 : 5 + n_parts]
-    price, limit, start, *refs = refs[5 + n_parts :]
+    count, rows, cols, tiles = refs[:4]
+    parts = refs[4 : 4 + n_parts]
+    price, limit, start, *refs = refs[4 + n_parts :]
     if last:
-        grid, weight_in, primal_norm, point, point_out, weight_out, out, source, acc = refs
+        other, grid, weight_in, primal_norm, point, point_out, weight_out, out, source, acc = refs
         dual_norm = total_norm(parts)
         weight = weight_in[:, :1]
         ratio = (dual_norm + EPS) / (primal_norm[:, :1] + EPS)
         weight = jnp.sqrt(weight * jnp.sqrt(ratio))
         weight_out[...] = jnp.broadcast_to(weight, weight_out.shape)
     else:
-        grid, point_out, out, source, acc = refs
+        point_out, source, acc, norm_out = refs
         point = start
         weight = jnp.ones((8, 1), jnp.float32)
     q = point_out.shape[0]
@@ -311,8 +311,19 @@
     acc[...] = jnp.zeros_like(acc)
     near = (acc.shape[0] - 1) // 2
     half_products(count[0], lambda g: cols[g], lambda g: rows[g], tiles, 0, source, acc)
-    half_products(grid[2, 0], lambda g: grid[1, g], lambda g: near + grid[0, g], other, 0 if last else 1, source, acc)
-    pack(acc, out, partial_norm(squares), lax.axis_index("colblk"))
+    norm = partial_norm(squares)
+    if last:
+        half_products(grid[2, 0], lambda g: grid[1, g], lambda g: near + grid[0, g], other, 0, source, acc)
+        pack(acc, out, norm, lax.axis_index("colblk"))
+    else:
+        norm_out[...] = jnp.broadcast_to(norm, norm_out.shape)
+
+
+def other_kernel(grid, other, source, own, norm, out, acc):
+    acc[...] = own[...]
+    near = (acc.shape[0] - 1) // 2
+    half_products(grid[2, 0], lambda g: grid[1, g], lambda g: near + grid[0, g], other, 1, source, acc)
+    pack(acc, out, norm[:, :1], lax.axis_index("colblk"))
 
 
 def dual_kernel(mix, last, n_parts, *refs):
@@ -554,7 +565,7 @@
             vectors = [*parts, price, limit, start]
             point, weight, terms = call(
                 functools.partial(primal_kernel, mix, True, len(parts)),
-                [*own, turned, other_turned, *vectors, grid, weight, primal_norm, point],
+                [*own, turned, *vectors, other_turned, grid, weight, primal_norm, point],
                 [SMEM_SPEC] * 3 + [VMEM_SPEC] * (2 + len(vectors)) + [SMEM_SPEC] + [VMEM_SPEC] * 3,
                 [col_state, small, row_terms],
                 [VMEM_SPEC] * 3,
@@ -562,13 +573,21 @@
             )
         else:
             vectors = [*parts, price, limit, start]
-            point, terms = call(
+            point, *half_way = call(
                 functools.partial(primal_kernel, mix, False, len(parts)),
-                [*own, turned, other, *vectors, grid],
-                [SMEM_SPEC] * 3 + [VMEM_SPEC] * (2 + len(vectors)) + [SMEM_SPEC],
-                [col_state, row_terms],
-                [VMEM_SPEC] * 2,
-                to_rows,
+                [*own, turned, *vectors],
+                [SMEM_SPEC] * 3 + [VMEM_SPEC] * (1 + len(vectors)),
+                [col_state, *to_rows, small],
+                [VMEM_SPEC] * 4,
+                [],
+            )
+            (terms,) = call(
+                other_kernel,
+                [grid, other, *half_way],
+                [SMEM_SPEC] + [VMEM_SPEC] * 4,
+                [row_terms],
+                [VMEM_SPEC],
+                [to_rows[1]],
             )
         parts = butterfly(terms, "colblk", 4)
         if len(parts) == 4:

time: 44.3 us -> 43.9 us (level); the launches traced: 43.6 us -> 43.9 us
  waiting for transfers between devices: 14.8 us -> 16.1 us
  starting transfers between devices: 18.5 us -> 17.5 us
    ppermute x15, waiting for transfers between devices: 14.8 us -> 16.1 us  [swap(): return lax.ppermute(value, axis, [(i, i ^ mask) for i in range(size)])]
    ppermute x15, starting transfers between devices: 18.5 us -> 17.5 us  [swap(): return lax.ppermute(value, axis, [(i, i ^ mask) for i in range(size)])]
    pallas_call x14 -> x15, Pallas kernels: 8.77 us -> 8.62 us  [call(): pl.pallas_call(kernel, out_shape=outputs, in_specs=in_specs, out_specs=ou...]
  transfers between devices with their start and end apart: 15 -> 15, of which waited for: 10 -> 10; matrix products, arithmetic and copies ran while one was open for 0% -> 0% of each run, Pallas kernels for 9% -> 8%
where the time goes in v8:
time: 43.9 us
  starting transfers between devices  17.5 us (40%)
  waiting for transfers between devices  16.1 us (37%)
  Pallas kernels  8.62 us (20%)
  between operations  1.52 us (3%)
    ppermute x15, starting transfers between devices, swap(): return lax.ppermute(value, axis, [(i, i ^ mask) for i in range(size)])  17.5 us
    ppermute x15, waiting for transfers between devices, swap(): return lax.ppermute(value, axis, [(i, i ^ mask) for i in range(size)])  16.1 us
    pallas_call x15, Pallas kernels, call(): pl.pallas_call(kernel, out_shape=outputs, in_specs=in_specs, out_specs=ou...  8.62 us
  transfers between devices with their start and end apart: 15, of which 10 were waited for; matrix products, arithmetic and copies ran while one was open for 0% of the time, Pallas kernels for 8%

profile of v8, /device:TPU:0, one launch (start us, length us, event | category | flops | bytes accessed | tf_op | source)
XLA Modules:
  0.0 43.9 jit_solution(16423108020793364674)
XLA Ops:
  0.6 0.0 copy-start
  1.3 1.9 %shard_map.130 = (f32[16,16,128]{2,1,0:T(8,128)S(1)}, bf16[17,16,128]{2,1,0:T(8,128)(2,1)S(1)}, bf16[96,128,128]{2,1,0:T(8,128)(2,1)S(1)}, s32[96]{0:T(128)S(4)}, s32[96]{0:T(128)S(4)}) custom-call(s32[1]{0:T(128)S(6)} %copy.14.refs_0_.count, s32[96]{0:T(128)} %refs_1_.1, s32[96]{0:T(128)} %refs_2_.1, bf16[96,128,128]{2,1,0:T(8,128)(2,1)} %refs_3_.1, ...), custom_call_target="tpu_custom_call" | custom-call | tf_op jit(solution)/shard_map/pallas_call | solution.py:424
  3.2 0.3 collective-permute-start
  3.5 1.1 %collective-permute-done.received = bf16[17,16,128]{2,1,0:T(8,128)(2,1)S(1)} collective-permute-done((bf16[17,16,128]{2,1,0:T(8,128)(2,1)S(1)}, bf16[17,16,128]{2,1,0:T(8,128)(2,1)S(1)}, u32[]{:S(2)}, u32[]{:S(2)}) %collective-permute-start) | collective-permute-done | bytes 69664 | tf_op jit(solution)/shard_map/ppermute | solution.py:441
  4.6 0.3 collective-permute-start.1
  4.9 0.0 copy-start.2
  4.9 0.0 copy-start.4
  4.9 0.0 copy-start.5
  4.9 0.0 copy-start.6
  4.9 0.4 collective-permute-start.6
  5.3 2.9 %collective-permute-start.2 = (bf16[16,16,128]{2,1,0:T(8,128)(2,1)S(1)}, bf16[16,16,128]{2,1,0:T(8,128)(2,1)S(1)}, u32[]{:S(2)}, u32[]{:S(2)}) collective-permute-start(bf16[16,16,128]{2,1,0:T(8,128)(2,1)S(1)} %add_convert_fusion.after.refs_4_), channel_id=1, source_target_pairs={{0,8},{4,12},{8,0},{12,4},{1,9},{5,13},{9,1},{13,5},{2,10},{6,14},... | collective-permute-start | bytes 196616 | tf_op jit(solution)/shard_map/ppermute | solution.py:441
  8.3 0.5 %shard_map.131.refs_3_ = bf16[96,128,128]{2,1,0:T(8,128)(2,1)S(1)} custom-call(s32[1]{0:T(128)S(6)} %copy.14.refs_0_.count, bf16[96,128,128]{2,1,0:T(8,128)(2,1)S(1)} %get-tuple-element.37.tiles.refs_4_, bf16[16,16,128]{2,1,0:T(8,128)(2,1)S(1)} %add_convert_fusion.after.refs_4_), custom_call_target="tpu_custom_call" | custom-call | bytes 6291456 | tf_op jit(solution)/shard_map/pallas_call | solution.py:424
  8.8 0.1 shard_map.133
  8.9 0.6 %shard_map.132.grid.refs_3_.refs_10_ = s32[8,128]{1,0:T(8,128)S(4)} custom-call(bf16[17,16,128]{2,1,0:T(8,128)(2,1)S(1)} %collective-permute-done.received, bf16[16,16,128]{2,1,0:T(8,128)(2,1)S(1)} %add_convert_fusion.after.refs_4_), custom_call_target="tpu_custom_call" | custom-call | tf_op jit(solution)/shard_map/pallas_call | solution.py:424
  9.5 1.1 %collective-permute-done.2.refs_5_ = bf16[16,16,128]{2,1,0:T(8,128)(2,1)S(1)} collective-permute-done((bf16[16,16,128]{2,1,0:T(8,128)(2,1)S(1)}, bf16[16,16,128]{2,1,0:T(8,128)(2,1)S(1)}, u32[]{:S(2)}, u32[]{:S(2)}) %collective-permute-start.2) | collective-permute-done | bytes 65568 | tf_op jit(solution)/shard_map/ppermute | solution.py:441
  10.7 0.7 %shard_map.134 = (f32[16,16,128]{2,1,0:T(8,128)S(1)}, bf16[2,64,16,128]{3,2,1,0:T(8,128)(2,1)S(1)}, f32[65,8,128]{2,1,0:T(8,128)S(1)}, f32[8,128]{1,0:T(8,128)S(1)}) custom-call(s32[1]{0:T(128)S(6)} %copy.14.refs_0_.count, s32[96]{0:T(128)S(4)} %get-tuple-element.31.refs_1_, s32[96]{0:T(128)S(4)} %get-tuple-element.32.refs_2_, ...), custom_call_target="tpu_custom_call" | custom-call | tf_op jit(solution)/shard_map/pallas_call | solution.py:424
  11.4 0.0 collective-permute-done.1.other.refs_5_.tiles
  11.4 0.5 %shard_map.135.after.refs_6_ = bf16[17,16,128]{2,1,0:T(8,128)(2,1)S(1)} custom-call(s32[8,128]{1,0:T(8,128)S(4)} %shard_map.132.grid.refs_3_.refs_10_, bf16[96,128,128]{2,1,0:T(8,128)(2,1)S(1)} %collective-permute-done.1.other.refs_5_.tiles, bf16[2,64,16,128]{3,2,1,0:T(8,128)(2,1)S(1)} %get-tuple-element.41.source, f32[65,8,128]{2,1,0:T(8,128)S(1)} %get-tuple-element.42.own, ...), custom_call_target="tpu_custom_call" | custom-call | tf_op jit(solution)/shard_map/pallas_call | solution.py:424
  11.9 3.3 %collective-permute-start.3 = (bf16[17,16,128]{2,1,0:T(8,128)(2,1)S(1)}, bf16[17,16,128]{2,1,0:T(8,128)(2,1)S(1)}, u32[]{:S(2)}, u32[]{:S(2)}) collective-permute-start(bf16[17,16,128]{2,1,0:T(8,128)(2,1)S(1)} %shard_map.135.after.refs_6_), channel_id=1, source_target_pairs={{0,2},{1,3},{2,0},{3,1},{4,6},{5,7},{6,4},{7,5},{8,10},{9,11},{10,... | collective-permute-start | bytes 208904 | tf_op jit(solution)/shard_map/ppermute | solution.py:441
  15.2 1.3 %collective-permute-start.4 = (bf16[17,16,128]{2,1,0:T(8,128)(2,1)S(1)}, bf16[17,16,128]{2,1,0:T(8,128)(2,1)S(1)}, u32[]{:S(2)}, u32[]{:S(2)}) collective-permute-start(bf16[17,16,128]{2,1,0:T(8,128)(2,1)S(1)} %shard_map.135.after.refs_6_), channel_id=1, source_target_pairs={{0,1},{1,0},{2,3},{3,2},{4,5},{5,4},{6,7},{7,6},{8,9},{9,8},{10,11... | collective-permute-start | bytes 208904 | tf_op jit(solution)/shard_map/ppermute | solution.py:441
  16.5 0.2 collective-permute-start.5
  16.7 0.0 collective-permute-done.6.extra
  16.7 0.1 shard_map.137
  16.8 2.4 %collective-permute-done.3.refs_7_ = bf16[17,16,128]{2,1,0:T(8,128)(2,1)S(1)} collective-permute-done((bf16[17,16,128]{2,1,0:T(8,128)(2,1)S(1)}, bf16[17,16,128]{2,1,0:T(8,128)(2,1)S(1)}, u32[]{:S(2)}, u32[]{:S(2)}) %collective-permute-start.3) | collective-permute-done | bytes 69664 | tf_op jit(solution)/shard_map/ppermute | solution.py:441
  19.2 0.5 %collective-permute-done.4.refs_8_ = bf16[17,16,128]{2,1,0:T(8,128)(2,1)S(1)} collective-permute-done((bf16[17,16,128]{2,1,0:T(8,128)(2,1)S(1)}, bf16[17,16,128]{2,1,0:T(8,128)(2,1)S(1)}, u32[]{:S(2)}, u32[]{:S(2)}) %collective-permute-start.4) | collective-permute-done | bytes 69664 | tf_op jit(solution)/shard_map/ppermute | solution.py:441
  19.6 2.9 %collective-permute-done.5.refs_9_ = bf16[17,16,128]{2,1,0:T(8,128)(2,1)S(1)} collective-permute-done((bf16[17,16,128]{2,1,0:T(8,128)(2,1)S(1)}, bf16[17,16,128]{2,1,0:T(8,128)(2,1)S(1)}, u32[]{:S(2)}, u32[]{:S(2)}) %collective-permute-start.5) | collective-permute-done | bytes 69664 | tf_op jit(solution)/shard_map/ppermute | solution.py:441
  22.6 1.0 %shard_map.138 = (f32[16,16,128]{2,1,0:T(8,128)S(1)}, f32[8,128]{1,0:T(8,128)S(1)}, bf16[17,16,128]{2,1,0:T(8,128)(2,1)S(1)}) custom-call(s32[1]{0:T(128)S(6)} %copy.14.refs_0_.count, s32[96]{0:T(128)S(4)} %get-tuple-element.31.refs_1_, s32[96]{0:T(128)S(4)} %get-tuple-element.32.refs_2_, s32[8,128]{1,0:T(8,128)S(4)} %shard_map.132.grid.refs_3_.refs_10_, ...), custom_call_target="tpu_custom_call" | custom-call | tf_op jit(solution)/shard_map/pallas_call | solution.py:424
  23.6 1.8 %collective-permute-start.7 = (bf16[17,16,128]{2,1,0:T(8,128)(2,1)S(1)}, bf16[17,16,128]{2,1,0:T(8,128)(2,1)S(1)}, u32[]{:S(2)}, u32[]{:S(2)}) collective-permute-start(bf16[17,16,128]{2,1,0:T(8,128)(2,1)S(1)} %get-tuple-element.47.after.refs_4_), channel_id=1, source_target_pairs={{0,8},{4,12},{8,0},{12,4},{1,9},{5,13},{9,1},{13,5},{2,10},{6,14},... | collective-permute-start | bytes 208904 | tf_op jit(solution)/shard_map/ppermute | solution.py:441
  25.4 0.3 shard_map.139.refs_9_
  25.7 2.3 %collective-permute-done.7.refs_5_ = bf16[17,16,128]{2,1,0:T(8,128)(2,1)S(1)} collective-permute-done((bf16[17,16,128]{2,1,0:T(8,128)(2,1)S(1)}, bf16[17,16,128]{2,1,0:T(8,128)(2,1)S(1)}, u32[]{:S(2)}, u32[]{:S(2)}) %collective-permute-start.7) | collective-permute-done | bytes 69664 | tf_op jit(solution)/shard_map/ppermute | solution.py:441
  28.0 1.2 %shard_map.140 = (f32[16,16,128]{2,1,0:T(8,128)S(1)}, f32[8,128]{1,0:T(8,128)S(1)}, bf16[17,16,128]{2,1,0:T(8,128)(2,1)S(1)}) custom-call(s32[1]{0:T(128)S(6)} %copy.14.refs_0_.count, s32[96]{0:T(128)S(4)} %get-tuple-element.31.refs_1_, s32[96]{0:T(128)S(4)} %get-tuple-element.32.refs_2_, bf16[96,128,128]{2,1,0:T(8,128)(2,1)S(1)} %shard_map.131.refs_3_, ...), custom_call_target="tpu_custom_call" | custom-call | tf_op jit(solution)/shard_map/pallas_call | solution.py:424
  29.1 1.8 %collective-permute-start.10 = (bf16[17,16,128]{2,1,0:T(8,128)(2,1)S(1)}, bf16[17,16,128]{2,1,0:T(8,128)(2,1)S(1)}, u32[]{:S(2)}, u32[]{:S(2)}) collective-permute-start(bf16[17,16,128]{2,1,0:T(8,128)(2,1)S(1)} %get-tuple-element.51.refs_0_), channel_id=1, source_target_pairs={{0,3},{1,2},{2,1},{3,0},{4,7},{5,6},{6,5},{7,4},{8,11},{9,10},{10,... | collective-permute-start | bytes 208904 | tf_op jit(solution)/shard_map/ppermute | solution.py:441
  31.0 0.9 %collective-permute-start.8 = (bf16[17,16,128]{2,1,0:T(8,128)(2,1)S(1)}, bf16[17,16,128]{2,1,0:T(8,128)(2,1)S(1)}, u32[]{:S(2)}, u32[]{:S(2)}) collective-permute-start(bf16[17,16,128]{2,1,0:T(8,128)(2,1)S(1)} %get-tuple-element.51.refs_0_), channel_id=1, source_target_pairs={{0,2},{1,3},{2,0},{3,1},{4,6},{5,7},{6,4},{7,5},{8,10},{9,11},{10,... | collective-permute-start | bytes 208904 | tf_op jit(solution)/shard_map/ppermute | solution.py:441
  31.8 1.7 %collective-permute-start.9 = (bf16[17,16,128]{2,1,0:T(8,128)(2,1)S(1)}, bf16[17,16,128]{2,1,0:T(8,128)(2,1)S(1)}, u32[]{:S(2)}, u32[]{:S(2)}) collective-permute-start(bf16[17,16,128]{2,1,0:T(8,128)(2,1)S(1)} %get-tuple-element.51.refs_0_), channel_id=1, source_target_pairs={{0,1},{1,0},{2,3},{3,2},{4,5},{5,4},{6,7},{7,6},{8,9},{9,8},{10,11... | collective-permute-start | bytes 208904 | tf_op jit(solution)/shard_map/ppermute | solution.py:441
  33.6 2.5 %collective-permute-done.10.refs_3_ = bf16[17,16,128]{2,1,0:T(8,128)(2,1)S(1)} collective-permute-done((bf16[17,16,128]{2,1,0:T(8,128)(2,1)S(1)}, bf16[17,16,128]{2,1,0:T(8,128)(2,1)S(1)}, u32[]{:S(2)}, u32[]{:S(2)}) %collective-permute-start.10) | collective-permute-done | bytes 69664 | tf_op jit(solution)/shard_map/ppermute | solution.py:441
  36.1 1.1 %collective-permute-done.8.refs_1_ = bf16[17,16,128]{2,1,0:T(8,128)(2,1)S(1)} collective-permute-done((bf16[17,16,128]{2,1,0:T(8,128)(2,1)S(1)}, bf16[17,16,128]{2,1,0:T(8,128)(2,1)S(1)}, u32[]{:S(2)}, u32[]{:S(2)}) %collective-permute-start.8) | collective-permute-done | bytes 69664 | tf_op jit(solution)/shard_map/ppermute | solution.py:441
  37.2 0.0 collective-permute-done.9.refs_2_
  37.2 0.2 shard_map.141
  37.4 0.1 collective-permute-start.11
  37.5 0.5 %collective-permute-start.12 = (f32[8,128]{1,0:T(8,128)S(1)}, f32[8,128]{1,0:T(8,128)S(1)}, u32[]{:S(2)}, u32[]{:S(2)}) collective-permute-start(f32[8,128]{1,0:T(8,128)S(1)} %get-tuple-element.58.refs_0_), channel_id=1, source_target_pairs={{0,4},{4,0},{8,12},{12,8},{1,5},{5,1},{9,13},{13,9},{2,6},{6,2},{1... | collective-permute-start | bytes 12296 | tf_op jit(solution)/shard_map/ppermute | solution.py:441
  38.0 2.0 %collective-permute-start.13 = (f32[8,128]{1,0:T(8,128)S(1)}, f32[8,128]{1,0:T(8,128)S(1)}, u32[]{:S(2)}, u32[]{:S(2)}) collective-permute-start(f32[8,128]{1,0:T(8,128)S(1)} %get-tuple-element.58.refs_0_), channel_id=1, source_target_pairs={{0,8},{4,12},{8,0},{12,4},{1,9},{5,13},{9,1},{13,5},{2,10},{6,14},... | collective-permute-start | bytes 12296 | tf_op jit(solution)/shard_map/ppermute | solution.py:441
  40.0 0.0 collective-permute-start.14
  40.0 0.0 collective-permute-done.11.other
  40.0 0.8 %shard_map.143 = (f32[8,8192]{1,0:T(8,128)}, f32[8,4096]{1,0:T(8,128)}) custom-call(f32[16,16,128]{2,1,0:T(8,128)S(1)} %get-tuple-element.50.point.mine_x, f32[16,8,128]{2,1,0:T(8,128)S(1)} %get-tuple-element.54.mine_y, f32[24,16,128]{2,1,0:T(8,128)S(1)} %collective-permute-done.11.other), custom_call_target="tpu_custom_call" | custom-call | tf_op jit(solution)/shard_map/pallas_call | solution.py:424
  40.8 0.0 collective-permute-done.12.refs_1_
  40.8 0.8 %collective-permute-done.13.refs_2_ = f32[8,128]{1,0:T(8,128)S(1)} collective-permute-done((f32[8,128]{1,0:T(8,128)S(1)}, f32[8,128]{1,0:T(8,128)S(1)}, u32[]{:S(2)}, u32[]{:S(2)}) %collective-permute-start.13) | collective-permute-done | bytes 4128 | tf_op jit(solution)/shard_map/ppermute | solution.py:441
  41.6 1.5 %collective-permute-done.14.refs_3_ = f32[8,128]{1,0:T(8,128)S(1)} collective-permute-done((f32[8,128]{1,0:T(8,128)S(1)}, f32[8,128]{1,0:T(8,128)S(1)}, u32[]{:S(2)}, u32[]{:S(2)}) %collective-permute-start.14) | collective-permute-done | bytes 4128 | tf_op jit(solution)/shard_map/ppermute | solution.py:441
  43.1 0.8 %shard_map.144 = f32[1,8]{1,0:T(1,128)} custom-call(f32[8,128]{1,0:T(8,128)S(1)} %get-tuple-element.58.refs_0_, f32[8,128]{1,0:T(8,128)S(1)} %collective-permute-done.12.refs_1_, f32[8,128]{1,0:T(8,128)S(1)} %collective-permute-done.13.refs_2_, f32[8,128]{1,0:T(8,128)S(1)} %collective-permute-done.14.refs_3_, f32[8,4096]{1,0:T(8,128)} %get-tuple-element.29.refs_4_), custom_call_target="tpu_custom_call" | custom-call | tf_op jit(solution)/shard_map/pallas_call | solution.py:424
  (13 shorter events, 0.1 us)
Async XLA Ops:
  0.6 4.2 %copy-start = (f32[8,4096]{1,0:T(8,128)S(1)}, f32[8,4096]{1,0:T(8,128)}, u32[]{:S(2)}) copy-start(f32[8,4096]{1,0:T(8,128)} %begin.3) | copy-start | bytes 393220
  0.6 4.2 %copy-start.3 = (s32[4096]{0:T(1024)S(1)}, s32[4096]{0:T(1024)}, u32[]{:S(2)}) copy-start(s32[4096]{0:T(1024)} %param.19) | copy-start | bytes 49156
  0.7 4.2 %copy-start.1 = (f32[8,4096]{1,0:T(8,128)S(1)}, f32[8,4096]{1,0:T(8,128)}, u32[]{:S(2)}) copy-start(f32[8,4096]{1,0:T(8,128)} %demand.3) | copy-start | bytes 393220
  3.2 1.3 %collective-permute-start = (bf16[17,16,128]{2,1,0:T(8,128)(2,1)S(1)}, bf16[17,16,128]{2,1,0:T(8,128)(2,1)S(1)}, u32[]{:S(2)}, u32[]{:S(2)}) collective-permute-start(bf16[17,16,128]{2,1,0:T(8,128)(2,1)S(1)} %get-tuple-element.35), channel_id=1, source_target_pairs={{0,4},{4,0},{8,12},{12,8},{1,5},{5,1},{9,13},{13,9},{2,6},{6,2},{1... | collective-permute-start | bytes 208904 | tf_op jit(solution)/shard_map/ppermute | solution.py:441
  4.6 6.8 %collective-permute-start.1 = (bf16[96,128,128]{2,1,0:T(8,128)(2,1)S(1)}, bf16[96,128,128]{2,1,0:T(8,128)(2,1)S(1)}, u32[]{:S(2)}, u32[]{:S(2)}) collective-permute-start(bf16[96,128,128]{2,1,0:T(8,128)(2,1)S(1)} %get-tuple-element.37.tiles.refs_4_), channel_id=1, source_target_pairs={{0,4},{4,0},{8,12},{12,8},{1,5},{5,1},{9,13},{13,9},{2,6},{6,2},{1... | collective-permute-start | bytes 9437192 | tf_op jit(solution)/shard_map/ppermute | solution.py:441
  4.9 3.9 %copy-start.2 = (f32[8,8192]{1,0:T(8,128)S(1)}, f32[8,8192]{1,0:T(8,128)}, u32[]{:S(2)}) copy-start(f32[8,8192]{1,0:T(8,128)} %begin.2) | copy-start | bytes 786436
  4.9 3.9 %copy-start.4 = (f32[8192]{0:T(1024)S(1)}, f32[8192]{0:T(1024)}, u32[]{:S(2)}) copy-start(f32[8192]{0:T(1024)} %param.15) | copy-start | bytes 98308
  4.9 3.9 %copy-start.5 = (f32[8192]{0:T(1024)S(1)}, f32[8192]{0:T(1024)}, u32[]{:S(2)}) copy-start(f32[8192]{0:T(1024)} %param.17) | copy-start | bytes 98308
  4.9 3.9 %copy-start.6 = (s32[8192]{0:T(1024)S(1)}, s32[8192]{0:T(1024)}, u32[]{:S(2)}) copy-start(s32[8192]{0:T(1024)} %param.18) | copy-start | bytes 98308
  4.9 11.8 %collective-permute-start.6 = (f32[36,8,128]{2,1,0:T(8,128)S(1)}, f32[36,8,128]{2,1,0:T(8,128)S(1)}, u32[]{:S(2)}, u32[]{:S(2)}) collective-permute-start(f32[36,8,128]{2,1,0:T(8,128)S(1)} %shard_map.136), channel_id=1, source_target_pairs={{0,4},{4,0},{8,12},{12,8},{1,5},{5,1},{9,13},{13,9},{2,6},{6,2},{1... | collective-permute-start | bytes 442376 | tf_op jit(solution)/shard_map/ppermute | solution.py:441
  5.3 5.4 %collective-permute-start.2 = (bf16[16,16,128]{2,1,0:T(8,128)(2,1)S(1)}, bf16[16,16,128]{2,1,0:T(8,128)(2,1)S(1)}, u32[]{:S(2)}, u32[]{:S(2)}) collective-permute-start(bf16[16,16,128]{2,1,0:T(8,128)(2,1)S(1)} %add_convert_fusion.after.refs_4_), channel_id=1, source_target_pairs={{0,8},{4,12},{8,0},{12,4},{1,9},{5,13},{9,1},{13,5},{2,10},{6,14},... | collective-permute-start | bytes 196616 | tf_op jit(solution)/shard_map/ppermute | solution.py:441
  11.9 7.3 %collective-permute-start.3 = (bf16[17,16,128]{2,1,0:T(8,128)(2,1)S(1)}, bf16[17,16,128]{2,1,0:T(8,128)(2,1)S(1)}, u32[]{:S(2)}, u32[]{:S(2)}) collective-permute-start(bf16[17,16,128]{2,1,0:T(8,128)(2,1)S(1)} %shard_map.135.after.refs_6_), channel_id=1, source_target_pairs={{0,2},{1,3},{2,0},{3,1},{4,6},{5,7},{6,4},{7,5},{8,10},{9,11},{10,... | collective-permute-start | bytes 208904 | tf_op jit(solution)/shard_map/ppermute | solution.py:441
  15.2 4.5 %collective-permute-start.4 = (bf16[17,16,128]{2,1,0:T(8,128)(2,1)S(1)}, bf16[17,16,128]{2,1,0:T(8,128)(2,1)S(1)}, u32[]{:S(2)}, u32[]{:S(2)}) collective-permute-start(bf16[17,16,128]{2,1,0:T(8,128)(2,1)S(1)} %shard_map.135.after.refs_6_), channel_id=1, source_target_pairs={{0,1},{1,0},{2,3},{3,2},{4,5},{5,4},{6,7},{7,6},{8,9},{9,8},{10,11... | collective-permute-start | bytes 208904 | tf_op jit(solution)/shard_map/ppermute | solution.py:441
  16.5 6.1 %collective-permute-start.5 = (bf16[17,16,128]{2,1,0:T(8,128)(2,1)S(1)}, bf16[17,16,128]{2,1,0:T(8,128)(2,1)S(1)}, u32[]{:S(2)}, u32[]{:S(2)}) collective-permute-start(bf16[17,16,128]{2,1,0:T(8,128)(2,1)S(1)} %shard_map.135.after.refs_6_), channel_id=1, source_target_pairs={{0,3},{1,2},{2,1},{3,0},{4,7},{5,6},{6,5},{7,4},{8,11},{9,10},{10,... | collective-permute-start | bytes 208904 | tf_op jit(solution)/shard_map/ppermute | solution.py:441
  23.6 4.4 %collective-permute-start.7 = (bf16[17,16,128]{2,1,0:T(8,128)(2,1)S(1)}, bf16[17,16,128]{2,1,0:T(8,128)(2,1)S(1)}, u32[]{:S(2)}, u32[]{:S(2)}) collective-permute-start(bf16[17,16,128]{2,1,0:T(8,128)(2,1)S(1)} %get-tuple-element.47.after.refs_4_), channel_id=1, source_target_pairs={{0,8},{4,12},{8,0},{12,4},{1,9},{5,13},{9,1},{13,5},{2,10},{6,14},... | collective-permute-start | bytes 208904 | tf_op jit(solution)/shard_map/ppermute | solution.py:441
  29.1 7.0 %collective-permute-start.10 = (bf16[17,16,128]{2,1,0:T(8,128)(2,1)S(1)}, bf16[17,16,128]{2,1,0:T(8,128)(2,1)S(1)}, u32[]{:S(2)}, u32[]{:S(2)}) collective-permute-start(bf16[17,16,128]{2,1,0:T(8,128)(2,1)S(1)} %get-tuple-element.51.refs_0_), channel_id=1, source_target_pairs={{0,3},{1,2},{2,1},{3,0},{4,7},{5,6},{6,5},{7,4},{8,11},{9,10},{10,... | collective-permute-start | bytes 208904 | tf_op jit(solution)/shard_map/ppermute | solution.py:441
  31.0 6.2 %collective-permute-start.8 = (bf16[17,16,128]{2,1,0:T(8,128)(2,1)S(1)}, bf16[17,16,128]{2,1,0:T(8,128)(2,1)S(1)}, u32[]{:S(2)}, u32[]{:S(2)}) collective-permute-start(bf16[17,16,128]{2,1,0:T(8,128)(2,1)S(1)} %get-tuple-element.51.refs_0_), channel_id=1, source_target_pairs={{0,2},{1,3},{2,0},{3,1},{4,6},{5,7},{6,4},{7,5},{8,10},{9,11},{10,... | collective-permute-start | bytes 208904 | tf_op jit(solution)/shard_map/ppermute | solution.py:441
  31.8 5.4 %collective-permute-start.9 = (bf16[17,16,128]{2,1,0:T(8,128)(2,1)S(1)}, bf16[17,16,128]{2,1,0:T(8,128)(2,1)S(1)}, u32[]{:S(2)}, u32[]{:S(2)}) collective-permute-start(bf16[17,16,128]{2,1,0:T(8,128)(2,1)S(1)} %get-tuple-element.51.refs_0_), channel_id=1, source_target_pairs={{0,1},{1,0},{2,3},{3,2},{4,5},{5,4},{6,7},{7,6},{8,9},{9,8},{10,11... | collective-permute-start | bytes 208904 | tf_op jit(solution)/shard_map/ppermute | solution.py:441
  37.4 2.6 %collective-permute-start.11 = (f32[24,16,128]{2,1,0:T(8,128)S(1)}, f32[24,16,128]{2,1,0:T(8,128)S(1)}, u32[]{:S(2)}, u32[]{:S(2)}) collective-permute-start(f32[24,16,128]{2,1,0:T(8,128)S(1)} %shard_map.142), channel_id=1, source_target_pairs={{0,4},{4,0},{8,12},{12,8},{1,5},{5,1},{9,13},{13,9},{2,6},{6,2},{1... | collective-permute-start | bytes 589832 | tf_op jit(solution)/shard_map/ppermute | solution.py:441
  37.5 3.3 %collective-permute-start.12 = (f32[8,128]{1,0:T(8,128)S(1)}, f32[8,128]{1,0:T(8,128)S(1)}, u32[]{:S(2)}, u32[]{:S(2)}) collective-permute-start(f32[8,128]{1,0:T(8,128)S(1)} %get-tuple-element.58.refs_0_), channel_id=1, source_target_pairs={{0,4},{4,0},{8,12},{12,8},{1,5},{5,1},{9,13},{13,9},{2,6},{6,2},{1... | collective-permute-start | bytes 12296 | tf_op jit(solution)/shard_map/ppermute | solution.py:441
  38.0 3.6 %collective-permute-start.13 = (f32[8,128]{1,0:T(8,128)S(1)}, f32[8,128]{1,0:T(8,128)S(1)}, u32[]{:S(2)}, u32[]{:S(2)}) collective-permute-start(f32[8,128]{1,0:T(8,128)S(1)} %get-tuple-element.58.refs_0_), channel_id=1, source_target_pairs={{0,8},{4,12},{8,0},{12,4},{1,9},{5,13},{9,1},{13,5},{2,10},{6,14},... | collective-permute-start | bytes 12296 | tf_op jit(solution)/shard_map/ppermute | solution.py:441
  40.0 3.1 %collective-permute-start.14 = (f32[8,128]{1,0:T(8,128)S(1)}, f32[8,128]{1,0:T(8,128)S(1)}, u32[]{:S(2)}, u32[]{:S(2)}) collective-permute-start(f32[8,128]{1,0:T(8,128)S(1)} %get-tuple-element.58.refs_0_), channel_id=1, source_target_pairs={{0,12},{4,8},{8,4},{12,0},{1,13},{5,9},{9,5},{13,1},{2,14},{6,10},... | collective-permute-start | bytes 12296 | tf_op jit(solution)/shard_map/ppermute | solution.py:441

commit v9 on v8

--- a/solution.py
+++ b/solution.py
@@ -11,7 +11,7 @@
 ETA = 0.3
 EPS = 1e-06
 PART = 24
-HALF_PARTS = (32, 16, 24)
+HALF_PARTS = (48, 24)
 VMEM_LIMIT = 8 * 1024 * 1024
 
 SMEM_SPEC = pl.BlockSpec(memory_space=pltpu.SMEM)

time: 43.9 us -> 43.8 us (level)
  waiting for transfers between devices: 16.1 us -> 15.1 us
  starting transfers between devices: 17.5 us -> 18.1 us
    ppermute x15, waiting for transfers between devices: 16.1 us -> 15.1 us  [swap(): return lax.ppermute(value, axis, [(i, i ^ mask) for i in range(size)])]
    ppermute x15, starting transfers between devices: 17.5 us -> 18.1 us  [swap(): return lax.ppermute(value, axis, [(i, i ^ mask) for i in range(size)])]
  transfers between devices with their start and end apart: 15 -> 15, of which waited for: 10 -> 10; matrix products, arithmetic and copies ran while one was open for 0% -> 0% of each run, Pallas kernels for 8% -> 9%
where the time goes in v9:
time: 43.8 us; the launch traced here: 43.7 us
  starting transfers between devices  18.1 us (41%)
  waiting for transfers between devices  15.1 us (34%)
  Pallas kernels  8.94 us (20%)
  between operations  1.52 us (3%)
    ppermute x15, starting transfers between devices, swap(): return lax.ppermute(value, axis, [(i, i ^ mask) for i in range(size)])  18.1 us
    ppermute x15, waiting for transfers between devices, swap(): return lax.ppermute(value, axis, [(i, i ^ mask) for i in range(size)])  15.1 us
    pallas_call x15, Pallas kernels, call(): pl.pallas_call(kernel, out_shape=outputs, in_specs=in_specs, out_specs=ou...  8.94 us
  transfers between devices with their start and end apart: 15, of which 10 were waited for; matrix products, arithmetic and copies ran while one was open for 0% of the time, Pallas kernels for 9%

profile of v9, /device:TPU:0, one launch (start us, length us, event | category | flops | bytes accessed | tf_op | source)
XLA Modules:
  0.0 43.7 jit_solution(1914852384078732936)
XLA Ops:
  0.6 0.0 copy-start
  1.3 1.9 %shard_map.130 = (f32[16,16,128]{2,1,0:T(8,128)S(1)}, bf16[17,16,128]{2,1,0:T(8,128)(2,1)S(1)}, bf16[96,128,128]{2,1,0:T(8,128)(2,1)S(1)}, s32[96]{0:T(128)S(4)}, s32[96]{0:T(128)S(4)}) custom-call(s32[1]{0:T(128)S(6)} %copy.14.refs_0_.count, s32[96]{0:T(128)} %refs_1_.1, s32[96]{0:T(128)} %refs_2_.1, bf16[96,128,128]{2,1,0:T(8,128)(2,1)} %refs_3_.1, ...), custom_call_target="tpu_custom_call" | custom-call | tf_op jit(solution)/shard_map/pallas_call | solution.py:424
  3.2 0.5 %collective-permute-start = (bf16[17,16,128]{2,1,0:T(8,128)(2,1)S(1)}, bf16[17,16,128]{2,1,0:T(8,128)(2,1)S(1)}, u32[]{:S(2)}, u32[]{:S(2)}) collective-permute-start(bf16[17,16,128]{2,1,0:T(8,128)(2,1)S(1)} %get-tuple-element.35), channel_id=1, source_target_pairs={{0,4},{4,0},{8,12},{12,8},{1,5},{5,1},{9,13},{13,9},{2,6},{6,2},{1... | collective-permute-start | bytes 208904 | tf_op jit(solution)/shard_map/ppermute | solution.py:441
  3.8 0.9 %collective-permute-done.received = bf16[17,16,128]{2,1,0:T(8,128)(2,1)S(1)} collective-permute-done((bf16[17,16,128]{2,1,0:T(8,128)(2,1)S(1)}, bf16[17,16,128]{2,1,0:T(8,128)(2,1)S(1)}, u32[]{:S(2)}, u32[]{:S(2)}) %collective-permute-start) | collective-permute-done | bytes 69664 | tf_op jit(solution)/shard_map/ppermute | solution.py:441
  4.7 0.4 collective-permute-start.1
  5.2 0.0 copy-start.2
  5.2 0.0 copy-start.4
  5.2 0.0 copy-start.5
  5.2 0.0 copy-start.6
  5.2 0.2 collective-permute-start.6
  5.4 2.6 %collective-permute-start.2 = (bf16[16,16,128]{2,1,0:T(8,128)(2,1)S(1)}, bf16[16,16,128]{2,1,0:T(8,128)(2,1)S(1)}, u32[]{:S(2)}, u32[]{:S(2)}) collective-permute-start(bf16[16,16,128]{2,1,0:T(8,128)(2,1)S(1)} %add_convert_fusion.after.refs_4_), channel_id=1, source_target_pairs={{0,8},{4,12},{8,0},{12,4},{1,9},{5,13},{9,1},{13,5},{2,10},{6,14},... | collective-permute-start | bytes 196616 | tf_op jit(solution)/shard_map/ppermute | solution.py:441
  8.0 0.5 %shard_map.131.refs_3_ = bf16[96,128,128]{2,1,0:T(8,128)(2,1)S(1)} custom-call(s32[1]{0:T(128)S(6)} %copy.14.refs_0_.count, bf16[96,128,128]{2,1,0:T(8,128)(2,1)S(1)} %get-tuple-element.37.tiles.refs_4_, bf16[16,16,128]{2,1,0:T(8,128)(2,1)S(1)} %add_convert_fusion.after.refs_4_), custom_call_target="tpu_custom_call" | custom-call | bytes 6291456 | tf_op jit(solution)/shard_map/pallas_call | solution.py:424
  8.6 0.1 shard_map.133
  8.6 0.6 %shard_map.132.grid.refs_3_.refs_10_ = s32[8,128]{1,0:T(8,128)S(4)} custom-call(bf16[17,16,128]{2,1,0:T(8,128)(2,1)S(1)} %collective-permute-done.received, bf16[16,16,128]{2,1,0:T(8,128)(2,1)S(1)} %add_convert_fusion.after.refs_4_), custom_call_target="tpu_custom_call" | custom-call | tf_op jit(solution)/shard_map/pallas_call | solution.py:424
  9.3 1.1 %collective-permute-done.2.refs_5_ = bf16[16,16,128]{2,1,0:T(8,128)(2,1)S(1)} collective-permute-done((bf16[16,16,128]{2,1,0:T(8,128)(2,1)S(1)}, bf16[16,16,128]{2,1,0:T(8,128)(2,1)S(1)}, u32[]{:S(2)}, u32[]{:S(2)}) %collective-permute-start.2) | collective-permute-done | bytes 65568 | tf_op jit(solution)/shard_map/ppermute | solution.py:441
  10.4 0.6 %shard_map.134 = (f32[16,16,128]{2,1,0:T(8,128)S(1)}, bf16[2,64,16,128]{3,2,1,0:T(8,128)(2,1)S(1)}, f32[65,8,128]{2,1,0:T(8,128)S(1)}, f32[8,128]{1,0:T(8,128)S(1)}) custom-call(s32[1]{0:T(128)S(6)} %copy.14.refs_0_.count, s32[96]{0:T(128)S(4)} %get-tuple-element.31.refs_1_, s32[96]{0:T(128)S(4)} %get-tuple-element.32.refs_2_, ...), custom_call_target="tpu_custom_call" | custom-call | tf_op jit(solution)/shard_map/pallas_call | solution.py:424
  11.0 0.0 collective-permute-done.1.other.refs_5_.tiles
  11.0 0.6 %shard_map.135.after.refs_6_ = bf16[17,16,128]{2,1,0:T(8,128)(2,1)S(1)} custom-call(s32[8,128]{1,0:T(8,128)S(4)} %shard_map.132.grid.refs_3_.refs_10_, bf16[96,128,128]{2,1,0:T(8,128)(2,1)S(1)} %collective-permute-done.1.other.refs_5_.tiles, bf16[2,64,16,128]{3,2,1,0:T(8,128)(2,1)S(1)} %get-tuple-element.41.source, f32[65,8,128]{2,1,0:T(8,128)S(1)} %get-tuple-element.42.own, ...), custom_call_target="tpu_custom_call" | custom-call | tf_op jit(solution)/shard_map/pallas_call | solution.py:424
  11.7 3.3 %collective-permute-start.3 = (bf16[17,16,128]{2,1,0:T(8,128)(2,1)S(1)}, bf16[17,16,128]{2,1,0:T(8,128)(2,1)S(1)}, u32[]{:S(2)}, u32[]{:S(2)}) collective-permute-start(bf16[17,16,128]{2,1,0:T(8,128)(2,1)S(1)} %shard_map.135.after.refs_6_), channel_id=1, source_target_pairs={{0,2},{1,3},{2,0},{3,1},{4,6},{5,7},{6,4},{7,5},{8,10},{9,11},{10,... | collective-permute-start | bytes 208904 | tf_op jit(solution)/shard_map/ppermute | solution.py:441
  15.0 1.3 %collective-permute-start.4 = (bf16[17,16,128]{2,1,0:T(8,128)(2,1)S(1)}, bf16[17,16,128]{2,1,0:T(8,128)(2,1)S(1)}, u32[]{:S(2)}, u32[]{:S(2)}) collective-permute-start(bf16[17,16,128]{2,1,0:T(8,128)(2,1)S(1)} %shard_map.135.after.refs_6_), channel_id=1, source_target_pairs={{0,1},{1,0},{2,3},{3,2},{4,5},{5,4},{6,7},{7,6},{8,9},{9,8},{10,11... | collective-permute-start | bytes 208904 | tf_op jit(solution)/shard_map/ppermute | solution.py:441
  16.4 0.2 collective-permute-start.5
  16.6 0.0 collective-permute-done.6.extra
  16.6 0.1 shard_map.137
  16.6 2.1 %collective-permute-done.3.refs_7_ = bf16[17,16,128]{2,1,0:T(8,128)(2,1)S(1)} collective-permute-done((bf16[17,16,128]{2,1,0:T(8,128)(2,1)S(1)}, bf16[17,16,128]{2,1,0:T(8,128)(2,1)S(1)}, u32[]{:S(2)}, u32[]{:S(2)}) %collective-permute-start.3) | collective-permute-done | bytes 69664 | tf_op jit(solution)/shard_map/ppermute | solution.py:441
  18.7 0.7 %collective-permute-done.4.refs_8_ = bf16[17,16,128]{2,1,0:T(8,128)(2,1)S(1)} collective-permute-done((bf16[17,16,128]{2,1,0:T(8,128)(2,1)S(1)}, bf16[17,16,128]{2,1,0:T(8,128)(2,1)S(1)}, u32[]{:S(2)}, u32[]{:S(2)}) %collective-permute-start.4) | collective-permute-done | bytes 69664 | tf_op jit(solution)/shard_map/ppermute | solution.py:441
  19.4 3.1 %collective-permute-done.5.refs_9_ = bf16[17,16,128]{2,1,0:T(8,128)(2,1)S(1)} collective-permute-done((bf16[17,16,128]{2,1,0:T(8,128)(2,1)S(1)}, bf16[17,16,128]{2,1,0:T(8,128)(2,1)S(1)}, u32[]{:S(2)}, u32[]{:S(2)}) %collective-permute-start.5) | collective-permute-done | bytes 69664 | tf_op jit(solution)/shard_map/ppermute | solution.py:441
  22.5 1.0 %shard_map.138 = (f32[16,16,128]{2,1,0:T(8,128)S(1)}, f32[8,128]{1,0:T(8,128)S(1)}, bf16[17,16,128]{2,1,0:T(8,128)(2,1)S(1)}) custom-call(s32[1]{0:T(128)S(6)} %copy.14.refs_0_.count, s32[96]{0:T(128)S(4)} %get-tuple-element.31.refs_1_, s32[96]{0:T(128)S(4)} %get-tuple-element.32.refs_2_, s32[8,128]{1,0:T(8,128)S(4)} %shard_map.132.grid.refs_3_.refs_10_, ...), custom_call_target="tpu_custom_call" | custom-call | tf_op jit(solution)/shard_map/pallas_call | solution.py:424
  23.5 2.5 %collective-permute-start.7 = (bf16[17,16,128]{2,1,0:T(8,128)(2,1)S(1)}, bf16[17,16,128]{2,1,0:T(8,128)(2,1)S(1)}, u32[]{:S(2)}, u32[]{:S(2)}) collective-permute-start(bf16[17,16,128]{2,1,0:T(8,128)(2,1)S(1)} %get-tuple-element.47.after.refs_4_), channel_id=1, source_target_pairs={{0,8},{4,12},{8,0},{12,4},{1,9},{5,13},{9,1},{13,5},{2,10},{6,14},... | collective-permute-start | bytes 208904 | tf_op jit(solution)/shard_map/ppermute | solution.py:441
  25.9 0.5 %shard_map.139.refs_9_ = bf16[96,128,128]{2,1,0:T(8,128)(2,1)S(1)} custom-call(s32[8,128]{1,0:T(8,128)S(4)} %shard_map.132.grid.refs_3_.refs_10_, bf16[96,128,128]{2,1,0:T(8,128)(2,1)S(1)} %collective-permute-done.1.other.refs_5_.tiles, bf16[17,16,128]{2,1,0:T(8,128)(2,1)S(1)} %get-tuple-element.47.after.refs_4_), custom_call_target="tpu_custom_call" | custom-call | bytes 6291456 | tf_op jit(solution)/shard_map/pallas_call | solution.py:424
  26.5 1.8 %collective-permute-done.7.refs_5_ = bf16[17,16,128]{2,1,0:T(8,128)(2,1)S(1)} collective-permute-done((bf16[17,16,128]{2,1,0:T(8,128)(2,1)S(1)}, bf16[17,16,128]{2,1,0:T(8,128)(2,1)S(1)}, u32[]{:S(2)}, u32[]{:S(2)}) %collective-permute-start.7) | collective-permute-done | bytes 69664 | tf_op jit(solution)/shard_map/ppermute | solution.py:441
  28.2 1.2 %shard_map.140 = (f32[16,16,128]{2,1,0:T(8,128)S(1)}, f32[8,128]{1,0:T(8,128)S(1)}, bf16[17,16,128]{2,1,0:T(8,128)(2,1)S(1)}) custom-call(s32[1]{0:T(128)S(6)} %copy.14.refs_0_.count, s32[96]{0:T(128)S(4)} %get-tuple-element.31.refs_1_, s32[96]{0:T(128)S(4)} %get-tuple-element.32.refs_2_, bf16[96,128,128]{2,1,0:T(8,128)(2,1)S(1)} %shard_map.131.refs_3_, ...), custom_call_target="tpu_custom_call" | custom-call | tf_op jit(solution)/shard_map/pallas_call | solution.py:424
  29.4 1.5 %collective-permute-start.10 = (bf16[17,16,128]{2,1,0:T(8,128)(2,1)S(1)}, bf16[17,16,128]{2,1,0:T(8,128)(2,1)S(1)}, u32[]{:S(2)}, u32[]{:S(2)}) collective-permute-start(bf16[17,16,128]{2,1,0:T(8,128)(2,1)S(1)} %get-tuple-element.51.refs_0_), channel_id=1, source_target_pairs={{0,3},{1,2},{2,1},{3,0},{4,7},{5,6},{6,5},{7,4},{8,11},{9,10},{10,... | collective-permute-start | bytes 208904 | tf_op jit(solution)/shard_map/ppermute | solution.py:441
  30.9 0.3 collective-permute-start.8
  31.1 2.7 %collective-permute-start.9 = (bf16[17,16,128]{2,1,0:T(8,128)(2,1)S(1)}, bf16[17,16,128]{2,1,0:T(8,128)(2,1)S(1)}, u32[]{:S(2)}, u32[]{:S(2)}) collective-permute-start(bf16[17,16,128]{2,1,0:T(8,128)(2,1)S(1)} %get-tuple-element.51.refs_0_), channel_id=1, source_target_pairs={{0,1},{1,0},{2,3},{3,2},{4,5},{5,4},{6,7},{7,6},{8,9},{9,8},{10,11... | collective-permute-start | bytes 208904 | tf_op jit(solution)/shard_map/ppermute | solution.py:441
  33.8 1.8 %collective-permute-done.10.refs_3_ = bf16[17,16,128]{2,1,0:T(8,128)(2,1)S(1)} collective-permute-done((bf16[17,16,128]{2,1,0:T(8,128)(2,1)S(1)}, bf16[17,16,128]{2,1,0:T(8,128)(2,1)S(1)}, u32[]{:S(2)}, u32[]{:S(2)}) %collective-permute-start.10) | collective-permute-done | bytes 69664 | tf_op jit(solution)/shard_map/ppermute | solution.py:441
  35.6 1.5 %collective-permute-done.8.refs_1_ = bf16[17,16,128]{2,1,0:T(8,128)(2,1)S(1)} collective-permute-done((bf16[17,16,128]{2,1,0:T(8,128)(2,1)S(1)}, bf16[17,16,128]{2,1,0:T(8,128)(2,1)S(1)}, u32[]{:S(2)}, u32[]{:S(2)}) %collective-permute-start.8) | collective-permute-done | bytes 69664 | tf_op jit(solution)/shard_map/ppermute | solution.py:441
  37.1 0.0 collective-permute-done.9.refs_2_
  37.1 0.2 shard_map.141
  37.2 0.1 collective-permute-start.11
  37.3 0.5 %collective-permute-start.12 = (f32[8,128]{1,0:T(8,128)S(1)}, f32[8,128]{1,0:T(8,128)S(1)}, u32[]{:S(2)}, u32[]{:S(2)}) collective-permute-start(f32[8,128]{1,0:T(8,128)S(1)} %get-tuple-element.58.refs_0_), channel_id=1, source_target_pairs={{0,4},{4,0},{8,12},{12,8},{1,5},{5,1},{9,13},{13,9},{2,6},{6,2},{1... | collective-permute-start | bytes 12296 | tf_op jit(solution)/shard_map/ppermute | solution.py:441
  37.8 2.0 %collective-permute-start.13 = (f32[8,128]{1,0:T(8,128)S(1)}, f32[8,128]{1,0:T(8,128)S(1)}, u32[]{:S(2)}, u32[]{:S(2)}) collective-permute-start(f32[8,128]{1,0:T(8,128)S(1)} %get-tuple-element.58.refs_0_), channel_id=1, source_target_pairs={{0,8},{4,12},{8,0},{12,4},{1,9},{5,13},{9,1},{13,5},{2,10},{6,14},... | collective-permute-start | bytes 12296 | tf_op jit(solution)/shard_map/ppermute | solution.py:441
  39.9 0.0 collective-permute-start.14
  39.9 0.0 collective-permute-done.11.other
  39.9 0.8 %shard_map.143 = (f32[8,8192]{1,0:T(8,128)}, f32[8,4096]{1,0:T(8,128)}) custom-call(f32[16,16,128]{2,1,0:T(8,128)S(1)} %get-tuple-element.50.point.mine_x, f32[16,8,128]{2,1,0:T(8,128)S(1)} %get-tuple-element.54.mine_y, f32[24,16,128]{2,1,0:T(8,128)S(1)} %collective-permute-done.11.other), custom_call_target="tpu_custom_call" | custom-call | tf_op jit(solution)/shard_map/pallas_call | solution.py:424
  40.7 0.0 collective-permute-done.12.refs_1_
  40.7 0.8 %collective-permute-done.13.refs_2_ = f32[8,128]{1,0:T(8,128)S(1)} collective-permute-done((f32[8,128]{1,0:T(8,128)S(1)}, f32[8,128]{1,0:T(8,128)S(1)}, u32[]{:S(2)}, u32[]{:S(2)}) %collective-permute-start.13) | collective-permute-done | bytes 4128 | tf_op jit(solution)/shard_map/ppermute | solution.py:441
  41.4 1.5 %collective-permute-done.14.refs_3_ = f32[8,128]{1,0:T(8,128)S(1)} collective-permute-done((f32[8,128]{1,0:T(8,128)S(1)}, f32[8,128]{1,0:T(8,128)S(1)}, u32[]{:S(2)}, u32[]{:S(2)}) %collective-permute-start.14) | collective-permute-done | bytes 4128 | tf_op jit(solution)/shard_map/ppermute | solution.py:441
  42.9 0.8 %shard_map.144 = f32[1,8]{1,0:T(1,128)} custom-call(f32[8,128]{1,0:T(8,128)S(1)} %get-tuple-element.58.refs_0_, f32[8,128]{1,0:T(8,128)S(1)} %collective-permute-done.12.refs_1_, f32[8,128]{1,0:T(8,128)S(1)} %collective-permute-done.13.refs_2_, f32[8,128]{1,0:T(8,128)S(1)} %collective-permute-done.14.refs_3_, f32[8,4096]{1,0:T(8,128)} %get-tuple-element.29.refs_4_), custom_call_target="tpu_custom_call" | custom-call | tf_op jit(solution)/shard_map/pallas_call | solution.py:424
  (13 shorter events, 0.1 us)
Async XLA Ops:
  0.6 4.5 %copy-start = (f32[8,4096]{1,0:T(8,128)S(1)}, f32[8,4096]{1,0:T(8,128)}, u32[]{:S(2)}) copy-start(f32[8,4096]{1,0:T(8,128)} %begin.3) | copy-start | bytes 393220
  0.6 4.5 %copy-start.3 = (s32[4096]{0:T(1024)S(1)}, s32[4096]{0:T(1024)}, u32[]{:S(2)}) copy-start(s32[4096]{0:T(1024)} %param.19) | copy-start | bytes 49156
  0.7 4.5 %copy-start.1 = (f32[8,4096]{1,0:T(8,128)S(1)}, f32[8,4096]{1,0:T(8,128)}, u32[]{:S(2)}) copy-start(f32[8,4096]{1,0:T(8,128)} %demand.3) | copy-start | bytes 393220
  3.2 1.4 %collective-permute-start = (bf16[17,16,128]{2,1,0:T(8,128)(2,1)S(1)}, bf16[17,16,128]{2,1,0:T(8,128)(2,1)S(1)}, u32[]{:S(2)}, u32[]{:S(2)}) collective-permute-start(bf16[17,16,128]{2,1,0:T(8,128)(2,1)S(1)} %get-tuple-element.35), channel_id=1, source_target_pairs={{0,4},{4,0},{8,12},{12,8},{1,5},{5,1},{9,13},{13,9},{2,6},{6,2},{1... | collective-permute-start | bytes 208904 | tf_op jit(solution)/shard_map/ppermute | solution.py:441
  4.7 6.3 %collective-permute-start.1 = (bf16[96,128,128]{2,1,0:T(8,128)(2,1)S(1)}, bf16[96,128,128]{2,1,0:T(8,128)(2,1)S(1)}, u32[]{:S(2)}, u32[]{:S(2)}) collective-permute-start(bf16[96,128,128]{2,1,0:T(8,128)(2,1)S(1)} %get-tuple-element.37.tiles.refs_4_), channel_id=1, source_target_pairs={{0,4},{4,0},{8,12},{12,8},{1,5},{5,1},{9,13},{13,9},{2,6},{6,2},{1... | collective-permute-start | bytes 9437192 | tf_op jit(solution)/shard_map/ppermute | solution.py:441
  5.2 3.4 %copy-start.2 = (f32[8,8192]{1,0:T(8,128)S(1)}, f32[8,8192]{1,0:T(8,128)}, u32[]{:S(2)}) copy-start(f32[8,8192]{1,0:T(8,128)} %begin.2) | copy-start | bytes 786436
  5.2 3.4 %copy-start.4 = (f32[8192]{0:T(1024)S(1)}, f32[8192]{0:T(1024)}, u32[]{:S(2)}) copy-start(f32[8192]{0:T(1024)} %param.15) | copy-start | bytes 98308
  5.2 3.3 %copy-start.5 = (f32[8192]{0:T(1024)S(1)}, f32[8192]{0:T(1024)}, u32[]{:S(2)}) copy-start(f32[8192]{0:T(1024)} %param.17) | copy-start | bytes 98308
  5.2 3.3 %copy-start.6 = (s32[8192]{0:T(1024)S(1)}, s32[8192]{0:T(1024)}, u32[]{:S(2)}) copy-start(s32[8192]{0:T(1024)} %param.18) | copy-start | bytes 98308
  5.2 11.3 %collective-permute-start.6 = (f32[36,8,128]{2,1,0:T(8,128)S(1)}, f32[36,8,128]{2,1,0:T(8,128)S(1)}, u32[]{:S(2)}, u32[]{:S(2)}) collective-permute-start(f32[36,8,128]{2,1,0:T(8,128)S(1)} %shard_map.136), channel_id=1, source_target_pairs={{0,4},{4,0},{8,12},{12,8},{1,5},{5,1},{9,13},{13,9},{2,6},{6,2},{1... | collective-permute-start | bytes 442376 | tf_op jit(solution)/shard_map/ppermute | solution.py:441
  5.4 5.0 %collective-permute-start.2 = (bf16[16,16,128]{2,1,0:T(8,128)(2,1)S(1)}, bf16[16,16,128]{2,1,0:T(8,128)(2,1)S(1)}, u32[]{:S(2)}, u32[]{:S(2)}) collective-permute-start(bf16[16,16,128]{2,1,0:T(8,128)(2,1)S(1)} %add_convert_fusion.after.refs_4_), channel_id=1, source_target_pairs={{0,8},{4,12},{8,0},{12,4},{1,9},{5,13},{9,1},{13,5},{2,10},{6,14},... | collective-permute-start | bytes 196616 | tf_op jit(solution)/shard_map/ppermute | solution.py:441
  11.7 7.0 %collective-permute-start.3 = (bf16[17,16,128]{2,1,0:T(8,128)(2,1)S(1)}, bf16[17,16,128]{2,1,0:T(8,128)(2,1)S(1)}, u32[]{:S(2)}, u32[]{:S(2)}) collective-permute-start(bf16[17,16,128]{2,1,0:T(8,128)(2,1)S(1)} %shard_map.135.after.refs_6_), channel_id=1, source_target_pairs={{0,2},{1,3},{2,0},{3,1},{4,6},{5,7},{6,4},{7,5},{8,10},{9,11},{10,... | collective-permute-start | bytes 208904 | tf_op jit(solution)/shard_map/ppermute | solution.py:441
  15.0 4.4 %collective-permute-start.4 = (bf16[17,16,128]{2,1,0:T(8,128)(2,1)S(1)}, bf16[17,16,128]{2,1,0:T(8,128)(2,1)S(1)}, u32[]{:S(2)}, u32[]{:S(2)}) collective-permute-start(bf16[17,16,128]{2,1,0:T(8,128)(2,1)S(1)} %shard_map.135.after.refs_6_), channel_id=1, source_target_pairs={{0,1},{1,0},{2,3},{3,2},{4,5},{5,4},{6,7},{7,6},{8,9},{9,8},{10,11... | collective-permute-start | bytes 208904 | tf_op jit(solution)/shard_map/ppermute | solution.py:441
  16.4 6.1 %collective-permute-start.5 = (bf16[17,16,128]{2,1,0:T(8,128)(2,1)S(1)}, bf16[17,16,128]{2,1,0:T(8,128)(2,1)S(1)}, u32[]{:S(2)}, u32[]{:S(2)}) collective-permute-start(bf16[17,16,128]{2,1,0:T(8,128)(2,1)S(1)} %shard_map.135.after.refs_6_), channel_id=1, source_target_pairs={{0,3},{1,2},{2,1},{3,0},{4,7},{5,6},{6,5},{7,4},{8,11},{9,10},{10,... | collective-permute-start | bytes 208904 | tf_op jit(solution)/shard_map/ppermute | solution.py:441
  23.5 4.7 %collective-permute-start.7 = (bf16[17,16,128]{2,1,0:T(8,128)(2,1)S(1)}, bf16[17,16,128]{2,1,0:T(8,128)(2,1)S(1)}, u32[]{:S(2)}, u32[]{:S(2)}) collective-permute-start(bf16[17,16,128]{2,1,0:T(8,128)(2,1)S(1)} %get-tuple-element.47.after.refs_4_), channel_id=1, source_target_pairs={{0,8},{4,12},{8,0},{12,4},{1,9},{5,13},{9,1},{13,5},{2,10},{6,14},... | collective-permute-start | bytes 208904 | tf_op jit(solution)/shard_map/ppermute | solution.py:441
  29.4 6.2 %collective-permute-start.10 = (bf16[17,16,128]{2,1,0:T(8,128)(2,1)S(1)}, bf16[17,16,128]{2,1,0:T(8,128)(2,1)S(1)}, u32[]{:S(2)}, u32[]{:S(2)}) collective-permute-start(bf16[17,16,128]{2,1,0:T(8,128)(2,1)S(1)} %get-tuple-element.51.refs_0_), channel_id=1, source_target_pairs={{0,3},{1,2},{2,1},{3,0},{4,7},{5,6},{6,5},{7,4},{8,11},{9,10},{10,... | collective-permute-start | bytes 208904 | tf_op jit(solution)/shard_map/ppermute | solution.py:441
  30.9 6.2 %collective-permute-start.8 = (bf16[17,16,128]{2,1,0:T(8,128)(2,1)S(1)}, bf16[17,16,128]{2,1,0:T(8,128)(2,1)S(1)}, u32[]{:S(2)}, u32[]{:S(2)}) collective-permute-start(bf16[17,16,128]{2,1,0:T(8,128)(2,1)S(1)} %get-tuple-element.51.refs_0_), channel_id=1, source_target_pairs={{0,2},{1,3},{2,0},{3,1},{4,6},{5,7},{6,4},{7,5},{8,10},{9,11},{10,... | collective-permute-start | bytes 208904 | tf_op jit(solution)/shard_map/ppermute | solution.py:441
  31.1 5.9 %collective-permute-start.9 = (bf16[17,16,128]{2,1,0:T(8,128)(2,1)S(1)}, bf16[17,16,128]{2,1,0:T(8,128)(2,1)S(1)}, u32[]{:S(2)}, u32[]{:S(2)}) collective-permute-start(bf16[17,16,128]{2,1,0:T(8,128)(2,1)S(1)} %get-tuple-element.51.refs_0_), channel_id=1, source_target_pairs={{0,1},{1,0},{2,3},{3,2},{4,5},{5,4},{6,7},{7,6},{8,9},{9,8},{10,11... | collective-permute-start | bytes 208904 | tf_op jit(solution)/shard_map/ppermute | solution.py:441
  37.2 2.6 %collective-permute-start.11 = (f32[24,16,128]{2,1,0:T(8,128)S(1)}, f32[24,16,128]{2,1,0:T(8,128)S(1)}, u32[]{:S(2)}, u32[]{:S(2)}) collective-permute-start(f32[24,16,128]{2,1,0:T(8,128)S(1)} %shard_map.142), channel_id=1, source_target_pairs={{0,4},{4,0},{8,12},{12,8},{1,5},{5,1},{9,13},{13,9},{2,6},{6,2},{1... | collective-permute-start | bytes 589832 | tf_op jit(solution)/shard_map/ppermute | solution.py:441
  37.3 3.4 %collective-permute-start.12 = (f32[8,128]{1,0:T(8,128)S(1)}, f32[8,128]{1,0:T(8,128)S(1)}, u32[]{:S(2)}, u32[]{:S(2)}) collective-permute-start(f32[8,128]{1,0:T(8,128)S(1)} %get-tuple-element.58.refs_0_), channel_id=1, source_target_pairs={{0,4},{4,0},{8,12},{12,8},{1,5},{5,1},{9,13},{13,9},{2,6},{6,2},{1... | collective-permute-start | bytes 12296 | tf_op jit(solution)/shard_map/ppermute | solution.py:441
  37.8 3.6 %collective-permute-start.13 = (f32[8,128]{1,0:T(8,128)S(1)}, f32[8,128]{1,0:T(8,128)S(1)}, u32[]{:S(2)}, u32[]{:S(2)}) collective-permute-start(f32[8,128]{1,0:T(8,128)S(1)} %get-tuple-element.58.refs_0_), channel_id=1, source_target_pairs={{0,8},{4,12},{8,0},{12,4},{1,9},{5,13},{9,1},{13,5},{2,10},{6,14},... | collective-permute-start | bytes 12296 | tf_op jit(solution)/shard_map/ppermute | solution.py:441
  39.9 3.1 %collective-permute-start.14 = (f32[8,128]{1,0:T(8,128)S(1)}, f32[8,128]{1,0:T(8,128)S(1)}, u32[]{:S(2)}, u32[]{:S(2)}) collective-permute-start(f32[8,128]{1,0:T(8,128)S(1)} %get-tuple-element.58.refs_0_), channel_id=1, source_target_pairs={{0,12},{4,8},{8,4},{12,0},{1,13},{5,9},{9,5},{13,1},{2,14},{6,10},... | collective-permute-start | bytes 12296 | tf_op jit(solution)/shard_map/ppermute | solution.py:441
